TPU v7x, 128 devices: a whole 4x4x4 slice. The times are simulated.
128 devices in a mesh: replica: 8 (over y_lo, x), tensor: 16 (over y_hi, z, core).
Axes of the slice: x: 4, y: 4 (y_hi: 2, y_lo: 2; y = y_hi * 2 + y_lo), z: 4, core: 2. Of those that a mesh axis runs over, the one named last changes fastest.
Arguments:
- tokens: bfloat16 [2048, 4096], P(('replica', 'tensor')), may hold values from -6 to 6
- cotangent: bfloat16 [2048, 4096], P(('replica', 'tensor')), may hold values from -6 to 6
- w_gate: bfloat16 [4096, 14336], P(None, 'tensor'), may hold values from -0.09375 to 0.09375
- w_up: bfloat16 [4096, 14336], P(None, 'tensor'), may hold values from -0.09375 to 0.09375
- w_down: bfloat16 [14336, 4096], P('tensor'), may hold values from -0.046875 to 0.046875
- outer_frag: float32 [512, 4096], P('tensor'), may hold values from -6 to 6
- local_frag: bfloat16 [8, 512, 4096], P('replica', 'tensor'), may hold values from -6 to 6
- momentum: float32 [512, 4096], P('tensor'), may hold values from -4 to 4
Outputs:
- layer_output: float32 [2048, 4096], P(('replica', 'tensor'))
- input_grad: float32 [2048, 4096], P(('replica', 'tensor'))
- new_outer: float32 [512, 4096], P('tensor')
- new_momentum: float32 [512, 4096], P('tensor')
All inputs are finite; a program needn't handle non-finite values.
Results may differ from a plain program's by a relative error of at most 0.0029.
Values may be sent and summed in bfloat16 or wider, within the bound.
No kernel may reach another device: no remote copies, remote signals or barrier semaphores. Data moves between devices by JAX's collectives and lax.ppermute only.
A program may use at most 128 MiB of HBM per device.

v0:
```python
import jax
import jax.numpy as jnp
from jax import lax
from jax.sharding import PartitionSpec as P

outer_rate = 0.7
outer_beta = 0.9


def times_transpose(left_rows, weight):
    return lax.dot_general(
        left_rows, weight, (((1,), (1,)), ((), ())), preferred_element_type=jnp.float32
    )


def nesterov_step(outer_rows, moment_rows, mean_delta):
    moment_next = outer_beta * moment_rows + mean_delta
    outer_next = outer_rows - outer_rate * (mean_delta + outer_beta * moment_next)
    return (outer_next, moment_next)


def on_device(tokens, cotangent, w_gate, w_up, w_down, outer_frag, local_frag, momentum):
    hidden_width = w_gate.shape[1]
    token_rows = lax.all_gather(tokens, "tensor", axis=0, tiled=True)
    projected = jnp.concatenate(
        [
            jnp.dot(token_rows, w_gate, preferred_element_type=jnp.float32),
            jnp.dot(token_rows, w_up, preferred_element_type=jnp.float32),
        ],
        1,
    )
    pre_gate = projected[:, :hidden_width]
    pre_up = projected[:, hidden_width:]
    sigmoid_gate = jax.nn.sigmoid(pre_gate)
    hidden = (pre_gate * sigmoid_gate * pre_up).astype(jnp.bfloat16)
    d_hidden = times_transpose(lax.all_gather(cotangent, "tensor", axis=0, tiled=True), w_down)
    d_gate = (d_hidden * pre_up * sigmoid_gate * (1.0 + pre_gate * (1.0 - sigmoid_gate))).astype(
        jnp.bfloat16
    )
    d_up = (d_hidden * pre_gate * sigmoid_gate).astype(jnp.bfloat16)
    output_part = lax.psum_scatter(
        jnp.dot(hidden, w_down, preferred_element_type=jnp.float32),
        "tensor",
        scatter_dimension=0,
        tiled=True,
    )
    grad_part = lax.psum_scatter(
        times_transpose(d_gate, w_gate) + times_transpose(d_up, w_up),
        "tensor",
        scatter_dimension=0,
        tiled=True,
    )
    pseudo_grad = outer_frag - local_frag[0].astype(jnp.float32)
    pseudo_total = lax.psum(pseudo_grad, "replica")
    new_outer, new_momentum = nesterov_step(
        outer_frag, momentum, pseudo_total / lax.axis_size("replica")
    )
    return (output_part, grad_part, new_outer, new_momentum)


def solution(mesh):
    in_specs = (
        P(("replica", "tensor"), None),
        P(("replica", "tensor"), None),
        P(None, "tensor"),
        P(None, "tensor"),
        P("tensor", None),
        P("tensor", None),
        P("replica", "tensor", None),
        P("tensor", None),
    )
    out_specs = (
        P(("replica", "tensor"), None),
        P(("replica", "tensor"), None),
        P("tensor", None),
        P("tensor", None),
    )
    return jax.shard_map(
        on_device, mesh=mesh, in_specs=in_specs, out_specs=out_specs, check_vma=False
    )
```

profile of v0, /device:TPU:0, one launch (start us, length us, event | category | flops | bytes accessed | tf_op | source)
XLA Modules:
  0.0 298.4 jit_solution(10259360874611188616)
XLA Ops:
  8.0 0.0 all-gather.3.cloned.1.call-start
  8.0 0.7 all-gather.3.cloned.1.call-update
  8.7 0.0 all-gather.5.cloned.1.call-start
  8.8 0.7 all-gather.5.cloned.1.call-update
  9.5 0.0 all-reduce.2.cloned.1.call-start
  9.5 1.9 convert_subtract_fusion
  11.5 0.0 all-reduce.2.cloned.1.call-update
  11.5 0.0 reduce-scatter.5.cloned.1.call-start
  11.6 50.6 %all-gather.3.cloned.1.call-done = bf16[256,4096]{1,0:T(8,128)(2,1)} async-done(((bf16[16,4096]{1,0:T(8,128)(2,1)}), bf16[256,4096]{1,0:T(8,128)(2,1)}) %all-gather.3.cloned.1.call-update) | async-done | bytes 2097168 | tf_op jit(solution)/shard_map/all_gather | solution.py:24
  62.1 0.0 copy-start.2
  62.1 6.2 %fusion.8 = f32[256,896]{1,0:T(8,128)S(1)} fusion(bf16[256,4096]{1,0:T(8,128)(2,1)} %all-gather.3.cloned.1.call-done, bf16[4096,896]{1,0:T(8,128)(2,1)} %param.10), kind=kOutput, calls=%fused_computation.16 | convolution fusion | flops 1879048192 | bytes 10354688 | tf_op jit(solution)/shard_map/dot_general | solution.py:27
  68.4 0.0 copy-done.2
  68.4 5.5 %fusion.9 = f32[256,896]{1,0:T(8,128)S(1)} fusion(bf16[256,4096]{1,0:T(8,128)(2,1)S(1)} %copy-done.2, bf16[4096,896]{1,0:T(8,128)(2,1)} %param.11), kind=kOutput, calls=%fused_computation.17 | convolution fusion | flops 1879048192 | bytes 10354688 | tf_op jit(solution)/shard_map/dot_general | solution.py:28
  73.9 36.9 %all-gather.5.cloned.1.call-done = bf16[256,4096]{1,0:T(8,128)(2,1)} async-done(((bf16[16,4096]{1,0:T(8,128)(2,1)}), bf16[256,4096]{1,0:T(8,128)(2,1)}) %all-gather.5.cloned.1.call-update) | async-done | bytes 2097168 | tf_op jit(solution)/shard_map/all_gather | solution.py:36
  110.8 6.2 %fusion.10 = f32[256,896]{1,0:T(8,128)S(1)} fusion(bf16[256,4096]{1,0:T(8,128)(2,1)} %all-gather.5.cloned.1.call-done, bf16[896,4096]{1,0:T(8,128)(2,1)} %param.12), kind=kOutput, calls=%fused_computation.18 | convolution fusion | flops 1879048192 | bytes 10354688 | tf_op jit(solution)/shard_map/dot_general | solution.py:11
  117.0 0.0 slice-start.1
  117.0 5.7 %fusion.1 = f32[256,4096]{1,0:T(8,128)S(1)} fusion(bf16[4096,896]{1,0:T(8,128)(2,1)} %param.10, f32[256,896]{1,0:T(8,128)S(1)} %fusion.8, f32[256,896]{1,0:T(8,128)S(1)} %fusion.10, f32[256,896]{1,0:T(8,128)S(1)} %fusion.9), kind=kOutput, calls=%fused_computation.9 | convolution fusion | flops 1881341952 | bytes 14286848 | tf_op jit(solution)/shard_map/dot_general | solution.py:11
  122.8 0.0 slice-done
  122.8 0.0 slice-done.1
  122.8 4.4 %convolution_add_fusion = f32[256,4096]{1,0:T(8,128)} fusion(f32[256,4096]{1,0:T(8,128)S(1)} %fusion.1, bf16[4096,896]{1,0:T(8,128)(2,1)S(1)} %bitcast.13, f32[256,896]{1,0:T(8,128)S(1)} %fusion.10, f32[256,896]{1,0:T(8,128)S(1)} %fusion.8), kind=kOutput, calls=%fused_computation | convolution fusion | flops 1881473024 | bytes 17563648 | tf_op jit(solution)/shard_map/dot_general | solution.py:11
  127.2 0.0 reduce-scatter.5.cloned.1.call-update
  127.2 0.0 copy-start
  127.2 0.0 copy-start.1
  127.3 0.0 reduce-scatter.3.cloned.1.call-start
  127.3 7.5 %fusion = f32[256,4096]{1,0:T(8,128)} fusion(bf16[896,4096]{1,0:T(8,128)(2,1)} %param.12, f32[256,896]{1,0:T(8,128)S(1)} %fusion.9, f32[256,896]{1,0:T(8,128)S(1)} %fusion.8), kind=kOutput, calls=%fused_computation.8 | convolution fusion | flops 1880424448 | bytes 13369344 | tf_op jit(solution)/shard_map/dot_general | solution.py:42
  134.8 0.0 reduce-scatter.3.cloned.1.call-update
  134.8 0.0 all-reduce.2.cloned.1.call-done
  134.8 0.0 copy-done
  134.8 0.0 copy-done.1
  134.9 2.2 multiply_subtract_fusion
  137.0 69.8 %reduce-scatter.5.cloned.1.call-done = f32[16,4096]{1,0:T(8,128)} async-done(((f32[256,4096]{1,0:T(8,128)}), f32[16,4096]{1,0:T(8,128)}) %reduce-scatter.5.cloned.1.call-update) | async-done | bytes 262160 | tf_op jit(solution)/shard_map/reduce_scatter | solution.py:47
  206.8 84.4 %reduce-scatter.3.cloned.1.call-done = f32[16,4096]{1,0:T(8,128)} async-done(((f32[256,4096]{1,0:T(8,128)}), f32[16,4096]{1,0:T(8,128)}) %reduce-scatter.3.cloned.1.call-update) | async-done | bytes 262160 | tf_op jit(solution)/shard_map/reduce_scatter | solution.py:41
  (2 shorter events, 0.0 us)
Async XLA Ops:
  8.0 54.1 %all-gather.3.cloned.1.call-start = ((), (), s32[]{:S(2)}) async-start(), calls=%async_computation.2 | async-start | bytes 2228224 | tf_op jit(solution)/shard_map/all_gather | solution.py:24
  8.7 102.1 %all-gather.5.cloned.1.call-start = ((), (), s32[]{:S(2)}) async-start(), calls=%async_computation.4 | async-start | bytes 2228224 | tf_op jit(solution)/shard_map/all_gather | solution.py:36
  9.5 125.3 %all-reduce.2.cloned.1.call-start = ((), (), s32[]{:S(2)}) async-start(), calls=%async_computation.6 | async-start | bytes 1048576 | tf_op jit(solution)/shard_map/psum | solution.py:54
  11.5 195.3 %reduce-scatter.5.cloned.1.call-start = ((), (), s32[]{:S(2)}) async-start(), calls=%async_computation.5 | async-start | bytes 4456448 | tf_op jit(solution)/shard_map/reduce_scatter | solution.py:47
  62.1 6.2 %copy-start.2 = (bf16[256,4096]{1,0:T(8,128)(2,1)S(1)}, bf16[256,4096]{1,0:T(8,128)(2,1)}, u32[]{:S(2)}) copy-start(bf16[256,4096]{1,0:T(8,128)(2,1)} %all-gather.3.cloned.1.call-done) | copy-start | bytes 6291460
  110.8 12.0 %slice-start = ((s8[7340032]{0:T(1024)(128)(4,1)}), s8[4194304]{0:T(1024)(128)(4,1)S(1)}, s32[]{:S(2)}) async-start(s8[7340032]{0:T(1024)(128)(4,1)} %bitcast.12), calls=%async_computation.7 | async-start | bytes 8388608
  117.0 5.7 %slice-start.1 = ((s8[7340032]{0:T(1024)(128)(4,1)}), s8[3145728]{0:T(1024)(128)(4,1)S(1)}, s32[]{:S(2)}) async-start(s8[7340032]{0:T(1024)(128)(4,1)} %bitcast.12), calls=%async_computation.8 | async-start | bytes 6291456
  127.2 7.6 %copy-start = (f32[32,4096]{1,0:T(8,128)S(1)}, f32[32,4096]{1,0:T(8,128)}, u32[]{:S(2)}) copy-start(f32[32,4096]{1,0:T(8,128)} %param.13) | copy-start | bytes 1572868
  127.2 7.6 %copy-start.1 = (f32[32,4096]{1,0:T(8,128)S(1)}, f32[32,4096]{1,0:T(8,128)}, u32[]{:S(2)}) copy-start(f32[32,4096]{1,0:T(8,128)} %param.15) | copy-start | bytes 1572868
  127.3 164.0 %reduce-scatter.3.cloned.1.call-start = ((), (), s32[]{:S(2)}) async-start(), calls=%async_computation.3 | async-start | bytes 4456448 | tf_op jit(solution)/shard_map/reduce_scatter | solution.py:41
Sparse Core Ops, SparseCore 0:
  11.3 50.8 all-gather.2
  64.6 46.1 all-gather.4
  127.4 79.4 reduce-scatter.4
  211.8 79.3 reduce-scatter.2
Sparse Core Ops, SparseCore 1:
  13.0 77.3 all-reduce.1
where the time goes:
time: 299 us; the launch traced here: 298 us
  waiting for transfers between devices  243 us (81%)
  matrix products  35.5 us (12%)
  between operations  15.3 us (5%)
  other arithmetic  4.14 us (1%)
    reduce_scatter x1, waiting for transfers between devices, on_device(): lax.psum_scatter(jnp.dot(hidden, w_down, preferred_element_type=jnp.float...  84.4 us
    reduce_scatter x1, waiting for transfers between devices, on_device(): lax.psum_scatter(times_transpose(d_gate, w_gate) + times_transpose(d_up,...  69.8 us
    all_gather x1, waiting for transfers between devices, on_device(): token_rows = lax.all_gather(tokens, 'tensor', axis=0, tiled=True)  50.6 us
    all_gather x1, waiting for transfers between devices, on_device(): lax.all_gather(cotangent, 'tensor', axis=0, tiled=True)  36.9 us
    dot_general x3, matrix products, times_transpose(): lax.dot_general(left_rows, weight, (((1,), (1,)), ((), ())), preferred_el...  16.3 us
    dot_general x1, matrix products, on_device(): jnp.dot(hidden, w_down, preferred_element_type=jnp.float32)  7.47 us
    dot_general x1, matrix products, on_device(): jnp.dot(token_rows, w_gate, preferred_element_type=jnp.float32)  6.21 us
  transfers between devices with their start and end apart: 5, of which 4 were waited for; matrix products, arithmetic and copies ran while one was open for 13% of the time, Pallas kernels for 0%

commit v1 on v0

v1 whole, which is shorter than its diff:
```python
import jax
import jax.numpy as jnp
from jax import lax
from jax.sharding import PartitionSpec as P

outer_rate = 0.7
outer_beta = 0.9
AXES = ("replica", "tensor")
EXTENT_X, EXTENT_Y, EXTENT_Z = 4, 4, 4


def position(x, y, z, core):
    return ((y % 2) * EXTENT_X + x) * 16 + (y // 2) * 8 + z * 2 + core


def pairs(move):
    return [
        (position(x, y, z, core), position(*move(x, y, z, core)))
        for x in range(EXTENT_X)
        for y in range(EXTENT_Y)
        for z in range(EXTENT_Z)
        for core in range(2)
    ]


def send_z(rows, distance):
    return lax.ppermute(
        rows, AXES, pairs(lambda x, y, z, core: (x, y, (z + distance) % EXTENT_Z, core))
    )


def swap_y(rows):
    return lax.ppermute(rows, AXES, pairs(lambda x, y, z, core: (x, 3 - y, z, core)))


def swap_core(rows):
    return lax.ppermute(rows, AXES, pairs(lambda x, y, z, core: (x, y, z, 1 - core)))


def times_transpose(left_rows, weight):
    return lax.dot_general(
        left_rows, weight, (((1,), (1,)), ((), ())), preferred_element_type=jnp.float32
    )


def gather_y_first(rows):
    both = jnp.concatenate([rows, swap_y(rows)], 0)
    near = jnp.concatenate([both] + order_z(both), 0)
    return jnp.concatenate([near, swap_core(near)], 0)


def order_z(block):
    one, three, two = send_z(block, -1), send_z(block, -3), send_z(block, -2)
    return [one, two, three]


def gather_z_first(rows):
    line = jnp.concatenate([rows] + order_z(rows), 0)
    across = swap_y(line)
    width = rows.shape[1]
    near = jnp.stack([line.reshape(4, 16, width), across.reshape(4, 16, width)], 1)
    near = near.reshape(128, width)
    return jnp.concatenate([near, swap_core(near)], 0)


def half(rows):
    return rows.astype(jnp.bfloat16)


def full(rows):
    return rows.astype(jnp.float32)


def sum_cores(partial):
    return partial[:128] + full(swap_core(half(partial[128:])))


def scatter_z_first(partial):
    blocks = sum_cores(partial).reshape(4, 32, -1)
    sent = half(blocks[1:])
    arrived = [send_z(sent[d - 1], d) for d in (1, 3, 2)]
    both = blocks[0] + full(arrived[0]) + full(arrived[1]) + full(arrived[2])
    return both[:16] + full(swap_y(half(both[16:])))


def scatter_y_first(partial):
    blocks = sum_cores(partial).reshape(4, 2, 16, -1)
    line = blocks[:, 0] + full(swap_y(half(blocks[:, 1])))
    sent = half(line[1:])
    arrived = [send_z(sent[d - 1], d) for d in (1, 3, 2)]
    return line[0] + full(arrived[0]) + full(arrived[1]) + full(arrived[2])


def on_device(tokens, cotangent, w_gate, w_up, w_down, outer_frag, local_frag, momentum):
    every_local = lax.all_gather(local_frag[0], "replica", axis=0, tiled=False)
    token_rows = gather_y_first(tokens)
    cotangent_rows = gather_z_first(cotangent)
    pre_gate = jnp.dot(token_rows, w_gate, preferred_element_type=jnp.float32)
    pre_up = jnp.dot(token_rows, w_up, preferred_element_type=jnp.float32)
    sigmoid_gate = jax.nn.sigmoid(pre_gate)
    hidden = (pre_gate * sigmoid_gate * pre_up).astype(jnp.bfloat16)
    layer_output = scatter_z_first(jnp.dot(hidden, w_down, preferred_element_type=jnp.float32))
    d_hidden = times_transpose(cotangent_rows, w_down)
    d_gate = (d_hidden * pre_up * sigmoid_gate * (1.0 + pre_gate * (1.0 - sigmoid_gate))).astype(
        jnp.bfloat16
    )
    d_up = (d_hidden * pre_gate * sigmoid_gate).astype(jnp.bfloat16)
    input_grad = scatter_y_first(times_transpose(d_gate, w_gate) + times_transpose(d_up, w_up))
    pseudo = jnp.sum(outer_frag[None] - every_local.astype(jnp.float32), axis=0)
    mean_delta = pseudo / every_local.shape[0]
    new_momentum = outer_beta * momentum + mean_delta
    new_outer = outer_frag - outer_rate * (mean_delta + outer_beta * new_momentum)
    return (layer_output, input_grad, new_outer, new_momentum)


def solution(mesh):
    in_specs = (
        P(AXES, None),
        P(AXES, None),
        P(None, "tensor"),
        P(None, "tensor"),
        P("tensor", None),
        P("tensor", None),
        P("replica", "tensor", None),
        P("tensor", None),
    )
    out_specs = (P(AXES, None), P(AXES, None), P("tensor", None), P("tensor", None))
    return jax.shard_map(
        on_device, mesh=mesh, in_specs=in_specs, out_specs=out_specs, check_vma=False
    )
```

time: 299 us -> 116 us (0.39)
  waiting for transfers between devices: 243 us -> 35.6 us
  starting transfers between devices: 0.2 us -> 33.2 us
  matrix products: 35.5 us -> 22.5 us
  local copies, waits for them, and re-layouts: 0.03 us -> 4.7 us
    reduce_scatter x2 -> x0, waiting for transfers between devices: 154 us -> none  [the longest x1 84.4 us: on_device(): lax.psum_scatter(jnp.dot(hidden, w_down, preferred_element_type=jnp.float...]
    all_gather x2 -> x1, waiting for transfers between devices: 87.5 us -> 0.01 us  [on_device(): every_local = lax.all_gather(local_frag[0], 'replica', axis=0, tiled=False)]
    ppermute x0 -> x20, waiting for transfers between devices: none -> 35.6 us  [the longest x12 22 us: send_z(): lax.ppermute(rows, AXES, pairs(lambda x, y, z, core: (x, y, (z + distance...]
    ppermute x0 -> x20, starting transfers between devices: none -> 33.2 us  [the longest x12 20.2 us: send_z(): lax.ppermute(rows, AXES, pairs(lambda x, y, z, core: (x, y, (z + distance...]
    dot_general x1, matrix products: 7.47 us -> 2.45 us  [on_device(): jnp.dot(hidden, w_down, preferred_element_type=jnp.float32)]
    dot_general x3, matrix products: 16.3 us -> 11.9 us  [times_transpose(): lax.dot_general(left_rows, weight, (((1,), (1,)), ((), ())), preferred_el...]
    unnamed x10 -> x25, local copies, waits for them, and re-layouts: 0.03 us -> 4.17 us
    dot_general x2, matrix products: 11.7 us -> 8.08 us  [the longest x1 5.69 us: on_device(): pre_gate = jnp.dot(token_rows, w_gate, preferred_element_type=jnp.float32)]
  transfers between devices with their start and end apart: 5 -> 21, of which waited for: 4 -> 9; matrix products, arithmetic and copies ran while one was open for 13% -> 24% of each run, Pallas kernels for 0% -> 0%
where the time goes in v1:
time: 116 us
  waiting for transfers between devices  35.6 us (31%)
  starting transfers between devices  33.2 us (29%)
  matrix products  22.5 us (19%)
  between operations  14.4 us (12%)
  other arithmetic  5.6 us (5%)
  local copies, waits for them, and re-layouts  4.7 us (4%)
    ppermute x12, waiting for transfers between devices, send_z(): lax.ppermute(rows, AXES, pairs(lambda x, y, z, core: (x, y, (z + distance...  22 us
    ppermute x12, starting transfers between devices, send_z(): lax.ppermute(rows, AXES, pairs(lambda x, y, z, core: (x, y, (z + distance...  20.2 us
    ppermute x4, waiting for transfers between devices, swap_y(): lax.ppermute(rows, AXES, pairs(lambda x, y, z, core: (x, 3 - y, z, core)))  13.5 us
    ppermute x4, starting transfers between devices, swap_y(): lax.ppermute(rows, AXES, pairs(lambda x, y, z, core: (x, 3 - y, z, core)))  12 us
    dot_general x3, matrix products, times_transpose(): lax.dot_general(left_rows, weight, (((1,), (1,)), ((), ())), preferred_el...  11.9 us
    dot_general x1, matrix products, on_device(): pre_gate = jnp.dot(token_rows, w_gate, preferred_element_type=jnp.float32)  5.69 us
    unnamed x25, local copies, waits for them, and re-layouts  4.17 us
    dot_general x1, matrix products, on_device(): jnp.dot(hidden, w_down, preferred_element_type=jnp.float32)  2.45 us
  transfers between devices with their start and end apart: 21, of which 9 were waited for; matrix products, arithmetic and copies ran while one was open for 24% of the time, Pallas kernels for 0%

profile of v1, /device:TPU:0, one launch (start us, length us, event | category | flops | bytes accessed | tf_op | source)
XLA Modules:
  0.0 115.9 jit_solution(749890190200390562)
XLA Ops:
  7.2 4.2 %collective-permute-start.10 = (bf16[16,4096]{1,0:T(8,128)(2,1)}, bf16[16,4096]{1,0:T(8,128)(2,1)S(1)}, u32[]{:S(2)}, u32[]{:S(2)}) collective-permute-start(bf16[16,4096]{1,0:T(8,128)(2,1)} %param.9), channel_id=1, source_target_pairs={{0,6},{1,7},{2,0},{3,1},{4,2},{5,3},{6,4},{7,5},{64,70},{65,71},{6... | collective-permute-start | bytes 393224 | tf_op jit(solution)/shard_map/ppermute | solution.py:27
  11.4 1.3 %collective-permute-start.12 = (bf16[16,4096]{1,0:T(8,128)(2,1)}, bf16[16,4096]{1,0:T(8,128)(2,1)S(1)}, u32[]{:S(2)}, u32[]{:S(2)}) collective-permute-start(bf16[16,4096]{1,0:T(8,128)(2,1)} %param.9), channel_id=1, source_target_pairs={{0,2},{1,3},{2,4},{3,5},{4,6},{5,7},{6,0},{7,1},{64,66},{65,67},{6... | collective-permute-start | bytes 393224 | tf_op jit(solution)/shard_map/ppermute | solution.py:27
  12.7 3.0 %collective-permute-start = (bf16[16,4096]{1,0:T(8,128)(2,1)}, bf16[16,4096]{1,0:T(8,128)(2,1)S(1)}, u32[]{:S(2)}, u32[]{:S(2)}) collective-permute-start(bf16[16,4096]{1,0:T(8,128)(2,1)} %param.8), channel_id=1, source_target_pairs={{0,72},{1,73},{2,74},{3,75},{4,76},{5,77},{6,78},{7,79},{64,8},{65... | collective-permute-start | bytes 393224 | tf_op jit(solution)/shard_map/ppermute | solution.py:33
  15.7 1.0 constant_dynamic-update-slice_fusion.6
  16.6 0.9 constant_dynamic-update-slice_fusion.16
  17.6 1.5 %collective-permute-done = bf16[16,4096]{1,0:T(8,128)(2,1)S(1)} collective-permute-done((bf16[16,4096]{1,0:T(8,128)(2,1)}, bf16[16,4096]{1,0:T(8,128)(2,1)S(1)}, u32[]{:S(2)}, u32[]{:S(2)}) %collective-permute-start) | collective-permute-done | bytes 131104 | tf_op jit(solution)/shard_map/ppermute | solution.py:33
  19.1 2.0 %collective-permute-start.1 = (bf16[32,4096]{1,0:T(8,128)(2,1)S(1)}, bf16[32,4096]{1,0:T(8,128)(2,1)S(1)}, u32[]{:S(2)}, u32[]{:S(2)}) collective-permute-start(bf16[32,4096]{1,0:T(8,128)(2,1)S(1)} %get-tuple-element.24), channel_id=1, source_target_pairs={{0,6},{1,7},{2,0},{3,1},{4,2},{5,3},{6,4},{7,5},{64,70},{65,71},{6... | collective-permute-start | bytes 786440 | tf_op jit(solution)/shard_map/ppermute | solution.py:27
  21.1 2.3 %collective-permute-start.2 = (bf16[32,4096]{1,0:T(8,128)(2,1)S(1)}, bf16[32,4096]{1,0:T(8,128)(2,1)S(1)}, u32[]{:S(2)}, u32[]{:S(2)}) collective-permute-start(bf16[32,4096]{1,0:T(8,128)(2,1)S(1)} %get-tuple-element.24), channel_id=1, source_target_pairs={{0,4},{1,5},{2,6},{3,7},{4,0},{5,1},{6,2},{7,3},{64,68},{65,69},{6... | collective-permute-start | bytes 786440 | tf_op jit(solution)/shard_map/ppermute | solution.py:27
  23.5 7.5 %collective-permute-done.1 = bf16[32,4096]{1,0:T(8,128)(2,1)S(1)} collective-permute-done((bf16[32,4096]{1,0:T(8,128)(2,1)S(1)}, bf16[32,4096]{1,0:T(8,128)(2,1)S(1)}, u32[]{:S(2)}, u32[]{:S(2)}) %collective-permute-start.1) | collective-permute-done | bytes 262176 | tf_op jit(solution)/shard_map/ppermute | solution.py:27
  31.0 0.8 collective-permute-done.2
  31.9 2.8 %collective-permute-done.3 = bf16[32,4096]{1,0:T(8,128)(2,1)S(1)} collective-permute-done((bf16[32,4096]{1,0:T(8,128)(2,1)S(1)}, bf16[32,4096]{1,0:T(8,128)(2,1)S(1)}, u32[]{:S(2)}, u32[]{:S(2)}) %collective-permute-start.3) | collective-permute-done | bytes 262176 | tf_op jit(solution)/shard_map/ppermute | solution.py:27
  34.8 1.2 %copy-done.2 = bf16[256,4096]{1,0:T(8,128)(2,1)} copy-done((bf16[256,4096]{1,0:T(8,128)(2,1)}, bf16[256,4096]{1,0:T(8,128)(2,1)S(1)}, u32[]{:S(2)}) %copy-start.2) | copy-done | bytes 2097176
  36.0 3.0 %collective-permute-start.13 = (bf16[64,4096]{1,0:T(8,128)(2,1)S(1)}, bf16[64,4096]{1,0:T(8,128)(2,1)S(1)}, u32[]{:S(2)}, u32[]{:S(2)}) collective-permute-start(bf16[64,4096]{1,0:T(8,128)(2,1)S(1)} %constant_dynamic-update-slice_fusion.13), channel_id=1, source_target_pairs={{0,72},{1,73},{2,74},{3,75},{4,76},{5,77},{6,78},{7,79},{64,8},{65... | collective-permute-start | bytes 1572872 | tf_op jit(solution)/shard_map/ppermute | solution.py:33
  39.0 11.4 %collective-permute-done.13 = bf16[64,4096]{1,0:T(8,128)(2,1)S(1)} collective-permute-done((bf16[64,4096]{1,0:T(8,128)(2,1)S(1)}, bf16[64,4096]{1,0:T(8,128)(2,1)S(1)}, u32[]{:S(2)}, u32[]{:S(2)}) %collective-permute-start.13) | collective-permute-done | bytes 524320 | tf_op jit(solution)/shard_map/ppermute | solution.py:33
  50.8 5.7 %fusion.24 = f32[256,896]{1,0:T(8,128)S(1)} fusion(bf16[256,4096]{1,0:T(8,128)(2,1)S(1)} %constant_dynamic-update-slice_fusion.7, bf16[4096,896]{1,0:T(8,128)(2,1)} %param.10), kind=kOutput, calls=%fused_computation.62 | convolution fusion | flops 1879048192 | bytes 10354688 | tf_op jit(solution)/shard_map/dot_general | solution.py:98
  56.5 2.4 %fusion.25 = f32[256,896]{1,0:T(8,128)S(1)} fusion(bf16[256,4096]{1,0:T(8,128)(2,1)S(1)} %constant_dynamic-update-slice_fusion.7, bf16[4096,896]{1,0:T(8,128)(2,1)S(1)} %bitcast.34), kind=kOutput, calls=%fused_computation.63 | convolution fusion | flops 1879048192 | bytes 10354688 | tf_op jit(solution)/shard_map/dot_general | solution.py:99
  58.9 0.9 copy-done.4
  59.9 2.4 %fusion.8 = f32[256,4096]{1,0:T(8,128)S(1)} fusion(bf16[896,4096]{1,0:T(8,128)(2,1)S(1)} %bitcast.42, f32[256,896]{1,0:T(8,128)S(1)} %fusion.25, f32[256,896]{1,0:T(8,128)S(1)} %fusion.24), kind=kOutput, calls=%fused_computation.24 | convolution fusion | flops 1880424448 | bytes 13369344 | tf_op jit(solution)/shard_map/dot_general | solution.py:102
  63.2 3.6 %fusion = f32[256,896]{1,0:T(8,128)S(1)} fusion(bf16[896,4096]{1,0:T(8,128)(2,1)S(1)} %bitcast.42, bf16[128,4096]{1,0:T(8,128)(2,1)} %collective-permute-done.14, bf16[128,4096]{1,0:T(8,128)(2,1)S(1)} %bitcast.38), kind=kOutput, calls=%fused_computation.6 | convolution fusion | flops 1883242496 | bytes 10354688 | tf_op jit(solution)/shard_map/dot_general | solution.py:41
  66.8 5.9 %fusion.9 = f32[256,4096]{1,0:T(8,128)S(1)} fusion(bf16[4096,896]{1,0:T(8,128)(2,1)} %param.10, f32[256,896]{1,0:T(8,128)S(1)} %fusion.24, f32[256,896]{1,0:T(8,128)S(1)} %fusion, f32[256,896]{1,0:T(8,128)} %copy-done.4), kind=kOutput, calls=%fused_computation.25 | convolution fusion | flops 1881341952 | bytes 14286848 | tf_op jit(solution)/shard_map/dot_general | solution.py:41
  72.7 2.4 %convolution_add_fusion = f32[256,4096]{1,0:T(8,128)S(1)} fusion(f32[256,4096]{1,0:T(8,128)S(1)} %fusion.9, bf16[4096,896]{1,0:T(8,128)(2,1)S(1)} %bitcast.34, f32[256,896]{1,0:T(8,128)S(1)} %fusion, f32[256,896]{1,0:T(8,128)S(1)} %fusion.24), kind=kOutput, calls=%fused_computation | convolution fusion | flops 1881473024 | bytes 17563648 | tf_op jit(solution)/shard_map/dot_general | solution.py:41
  76.1 3.0 %collective-permute-start.7 = (bf16[32,4096]{1,0:T(8,128)(2,1)S(1)}, bf16[32,4096]{1,0:T(8,128)(2,1)S(1)}, u32[]{:S(2)}, u32[]{:S(2)}) collective-permute-start(bf16[32,4096]{1,0:T(8,128)(2,1)S(1)} %get-tuple-element.12), channel_id=1, source_target_pairs={{0,6},{1,7},{2,0},{3,1},{4,2},{5,3},{6,4},{7,5},{64,70},{65,71},{6... | collective-permute-start | bytes 786440 | tf_op jit(solution)/shard_map/ppermute | solution.py:27
  79.1 1.0 collective-permute-start.8
  80.4 3.0 %collective-permute-start.16 = (bf16[4,16,4096]{2,1,0:T(8,128)(2,1)S(1)}, bf16[4,16,4096]{2,1,0:T(8,128)(2,1)S(1)}, u32[]{:S(2)}, u32[]{:S(2)}) collective-permute-start(bf16[4,16,4096]{2,1,0:T(8,128)(2,1)S(1)} %fusion.5), channel_id=1, source_target_pairs={{0,72},{1,73},{2,74},{3,75},{4,76},{5,77},{6,78},{7,79},{64,8},{65... | collective-permute-start | bytes 1572872 | tf_op jit(solution)/shard_map/ppermute | solution.py:33
  83.4 7.9 %collective-permute-done.6 = bf16[32,4096]{1,0:T(8,128)(2,1)S(1)} collective-permute-done((bf16[32,4096]{1,0:T(8,128)(2,1)S(1)}, bf16[32,4096]{1,0:T(8,128)(2,1)S(1)}, u32[]{:S(2)}, u32[]{:S(2)}) %collective-permute-start.6) | collective-permute-done | bytes 262176 | tf_op jit(solution)/shard_map/ppermute | solution.py:27
  91.5 3.1 %collective-permute-start.9 = (bf16[16,4096]{1,0:T(8,128)(2,1)S(1)}, bf16[16,4096]{1,0:T(8,128)(2,1)S(1)}, u32[]{:S(2)}, u32[]{:S(2)}) collective-permute-start(bf16[16,4096]{1,0:T(8,128)(2,1)S(1)} %slice.122), channel_id=1, source_target_pairs={{0,72},{1,73},{2,74},{3,75},{4,76},{5,77},{6,78},{7,79},{64,8},{65... | collective-permute-start | bytes 393224 | tf_op jit(solution)/shard_map/ppermute | solution.py:33
  95.7 3.0 %collective-permute-start.18 = (bf16[16,4096]{1,0:T(8,128)(2,1)S(1)}, bf16[16,4096]{1,0:T(8,128)(2,1)S(1)}, u32[]{:S(2)}, u32[]{:S(2)}) collective-permute-start(bf16[16,4096]{1,0:T(8,128)(2,1)S(1)} %get-tuple-element.15), channel_id=1, source_target_pairs={{0,6},{1,7},{2,0},{3,1},{4,2},{5,3},{6,4},{7,5},{64,70},{65,71},{6... | collective-permute-start | bytes 393224 | tf_op jit(solution)/shard_map/ppermute | solution.py:27
  98.6 2.7 %collective-permute-start.19 = (bf16[16,4096]{1,0:T(8,128)(2,1)S(1)}, bf16[16,4096]{1,0:T(8,128)(2,1)S(1)}, u32[]{:S(2)}, u32[]{:S(2)}) collective-permute-start(bf16[16,4096]{1,0:T(8,128)(2,1)S(1)} %get-tuple-element.14), channel_id=1, source_target_pairs={{0,4},{1,5},{2,6},{3,7},{4,0},{5,1},{6,2},{7,3},{64,68},{65,69},{6... | collective-permute-start | bytes 393224 | tf_op jit(solution)/shard_map/ppermute | solution.py:27
  102.6 2.5 %collective-permute-done.19 = bf16[16,4096]{1,0:T(8,128)(2,1)S(1)} collective-permute-done((bf16[16,4096]{1,0:T(8,128)(2,1)S(1)}, bf16[16,4096]{1,0:T(8,128)(2,1)S(1)}, u32[]{:S(2)}, u32[]{:S(2)}) %collective-permute-start.19) | collective-permute-done | bytes 131104 | tf_op jit(solution)/shard_map/ppermute | solution.py:27
  105.1 0.8 fusion.15
  105.9 2.1 %subtract_reduce_fusion = f32[32,4096]{1,0:T(8,128)S(1)} fusion(bf16[8,32,4096]{2,1,0:T(8,128)(2,1)} %all-gather.2.cloned.1.call-done, f32[32,4096]{1,0:T(8,128)S(1)} %copy-done), kind=kLoop, calls=%fused_computation.1 | loop fusion | flops 3014656 | bytes 3145728 | tf_op jit(solution)/shard_map/reduce_sum | solution.py:109
  108.0 1.1 multiply_subtract_fusion
  (62 shorter events, 5.2 us)
Async XLA Ops:
  7.2 98.7 %all-gather.2.cloned.1.call-start = ((), (), s32[]{:S(2)}) async-start(), calls=%async_computation | async-start | bytes 2359296 | tf_op jit(solution)/shard_map/all_gather | solution.py:95
  7.2 16.2 %collective-permute-start.10 = (bf16[16,4096]{1,0:T(8,128)(2,1)}, bf16[16,4096]{1,0:T(8,128)(2,1)S(1)}, u32[]{:S(2)}, u32[]{:S(2)}) collective-permute-start(bf16[16,4096]{1,0:T(8,128)(2,1)} %param.9), channel_id=1, source_target_pairs={{0,6},{1,7},{2,0},{3,1},{4,2},{5,3},{6,4},{7,5},{64,70},{65,71},{6... | collective-permute-start | bytes 393224 | tf_op jit(solution)/shard_map/ppermute | solution.py:27
  11.4 12.1 %collective-permute-start.11 = (bf16[16,4096]{1,0:T(8,128)(2,1)}, bf16[16,4096]{1,0:T(8,128)(2,1)S(1)}, u32[]{:S(2)}, u32[]{:S(2)}) collective-permute-start(bf16[16,4096]{1,0:T(8,128)(2,1)} %param.9), channel_id=1, source_target_pairs={{0,4},{1,5},{2,6},{3,7},{4,0},{5,1},{6,2},{7,3},{64,68},{65,69},{6... | collective-permute-start | bytes 393224 | tf_op jit(solution)/shard_map/ppermute | solution.py:27
  11.4 23.4 %collective-permute-start.12 = (bf16[16,4096]{1,0:T(8,128)(2,1)}, bf16[16,4096]{1,0:T(8,128)(2,1)S(1)}, u32[]{:S(2)}, u32[]{:S(2)}) collective-permute-start(bf16[16,4096]{1,0:T(8,128)(2,1)} %param.9), channel_id=1, source_target_pairs={{0,2},{1,3},{2,4},{3,5},{4,6},{5,7},{6,0},{7,1},{64,66},{65,67},{6... | collective-permute-start | bytes 393224 | tf_op jit(solution)/shard_map/ppermute | solution.py:27
  12.7 6.4 %collective-permute-start = (bf16[16,4096]{1,0:T(8,128)(2,1)}, bf16[16,4096]{1,0:T(8,128)(2,1)S(1)}, u32[]{:S(2)}, u32[]{:S(2)}) collective-permute-start(bf16[16,4096]{1,0:T(8,128)(2,1)} %param.8), channel_id=1, source_target_pairs={{0,72},{1,73},{2,74},{3,75},{4,76},{5,77},{6,78},{7,79},{64,8},{65... | collective-permute-start | bytes 393224 | tf_op jit(solution)/shard_map/ppermute | solution.py:33
  19.1 11.9 %collective-permute-start.1 = (bf16[32,4096]{1,0:T(8,128)(2,1)S(1)}, bf16[32,4096]{1,0:T(8,128)(2,1)S(1)}, u32[]{:S(2)}, u32[]{:S(2)}) collective-permute-start(bf16[32,4096]{1,0:T(8,128)(2,1)S(1)} %get-tuple-element.24), channel_id=1, source_target_pairs={{0,6},{1,7},{2,0},{3,1},{4,2},{5,3},{6,4},{7,5},{64,70},{65,71},{6... | collective-permute-start | bytes 786440 | tf_op jit(solution)/shard_map/ppermute | solution.py:27
  21.1 10.7 %collective-permute-start.2 = (bf16[32,4096]{1,0:T(8,128)(2,1)S(1)}, bf16[32,4096]{1,0:T(8,128)(2,1)S(1)}, u32[]{:S(2)}, u32[]{:S(2)}) collective-permute-start(bf16[32,4096]{1,0:T(8,128)(2,1)S(1)} %get-tuple-element.24), channel_id=1, source_target_pairs={{0,4},{1,5},{2,6},{3,7},{4,0},{5,1},{6,2},{7,3},{64,68},{65,69},{6... | collective-permute-start | bytes 786440 | tf_op jit(solution)/shard_map/ppermute | solution.py:27
  23.4 11.2 %collective-permute-start.3 = (bf16[32,4096]{1,0:T(8,128)(2,1)S(1)}, bf16[32,4096]{1,0:T(8,128)(2,1)S(1)}, u32[]{:S(2)}, u32[]{:S(2)}) collective-permute-start(bf16[32,4096]{1,0:T(8,128)(2,1)S(1)} %get-tuple-element.24), channel_id=1, source_target_pairs={{0,2},{1,3},{2,4},{3,5},{4,6},{5,7},{6,0},{7,1},{64,66},{65,67},{6... | collective-permute-start | bytes 786440 | tf_op jit(solution)/shard_map/ppermute | solution.py:27
  34.7 1.3 %copy-start.2 = (bf16[256,4096]{1,0:T(8,128)(2,1)}, bf16[256,4096]{1,0:T(8,128)(2,1)S(1)}, u32[]{:S(2)}) copy-start(bf16[256,4096]{1,0:T(8,128)(2,1)S(1)} %get-tuple-element.17) | copy-start | bytes 6291460
  34.7 15.9 %collective-permute-start.4 = (bf16[128,4096]{1,0:T(8,128)(2,1)S(1)}, bf16[128,4096]{1,0:T(8,128)(2,1)S(1)}, u32[]{:S(2)}, u32[]{:S(2)}) collective-permute-start(bf16[128,4096]{1,0:T(8,128)(2,1)S(1)} %get-tuple-element.16), channel_id=1, source_target_pairs={{0,1},{1,0},{2,3},{3,2},{4,5},{5,4},{6,7},{7,6},{64,65},{65,64},{6... | collective-permute-start | bytes 3145736 | tf_op jit(solution)/shard_map/ppermute | solution.py:37
  36.0 14.4 %collective-permute-start.13 = (bf16[64,4096]{1,0:T(8,128)(2,1)S(1)}, bf16[64,4096]{1,0:T(8,128)(2,1)S(1)}, u32[]{:S(2)}, u32[]{:S(2)}) collective-permute-start(bf16[64,4096]{1,0:T(8,128)(2,1)S(1)} %constant_dynamic-update-slice_fusion.13), channel_id=1, source_target_pairs={{0,72},{1,73},{2,74},{3,75},{4,76},{5,77},{6,78},{7,79},{64,8},{65... | collective-permute-start | bytes 1572872 | tf_op jit(solution)/shard_map/ppermute | solution.py:33
  39.0 11.7 %copy-start.3 = (bf16[256,4096]{1,0:T(8,128)(2,1)S(1)}, bf16[256,4096]{1,0:T(8,128)(2,1)}, u32[]{:S(2)}) copy-start(bf16[256,4096]{1,0:T(8,128)(2,1)} %copy-done.2) | copy-start | bytes 6291460
  50.6 12.7 %collective-permute-start.14 = (bf16[128,4096]{1,0:T(8,128)(2,1)S(1)}, bf16[128,4096]{1,0:T(8,128)(2,1)}, u32[]{:S(2)}, u32[]{:S(2)}) collective-permute-start(bf16[128,4096]{1,0:T(8,128)(2,1)S(1)} %bitcast.37), channel_id=1, source_target_pairs={{0,1},{1,0},{2,3},{3,2},{4,5},{5,4},{6,7},{7,6},{64,65},{65,64},{6... | collective-permute-start | bytes 3145736 | tf_op jit(solution)/shard_map/ppermute | solution.py:37
  50.7 5.8 %slice-start = ((s8[7340032]{0:T(1024)(128)(4,1)}), s8[4194304]{0:T(1024)(128)(4,1)S(1)}, s32[]{:S(2)}) async-start(s8[7340032]{0:T(1024)(128)(4,1)} %bitcast.33), calls=%async_computation.1 | async-start | bytes 8388608
  50.8 5.7 %slice-start.1 = ((s8[7340032]{0:T(1024)(128)(4,1)}), s8[3145728]{0:T(1024)(128)(4,1)S(1)}, s32[]{:S(2)}) async-start(s8[7340032]{0:T(1024)(128)(4,1)} %bitcast.33), calls=%async_computation.2 | async-start | bytes 6291456
  50.8 9.1 %slice-start.2 = ((s8[7340032]{0:T(1024)(128)(4,1)}), s8[4194304]{0:T(1024)(128)(4,1)S(1)}, s32[]{:S(2)}) async-start(s8[7340032]{0:T(1024)(128)(4,1)} %bitcast.41), calls=%async_computation.3 | async-start | bytes 8388608
  56.5 3.4 %slice-start.3 = ((s8[7340032]{0:T(1024)(128)(4,1)}), s8[3145728]{0:T(1024)(128)(4,1)S(1)}, s32[]{:S(2)}) async-start(s8[7340032]{0:T(1024)(128)(4,1)} %bitcast.41), calls=%async_computation.4 | async-start | bytes 6291456
  58.9 0.9 copy-start.4
  62.5 12.9 %collective-permute-start.5 = (bf16[128,4096]{1,0:T(8,128)(2,1)S(1)}, bf16[128,4096]{1,0:T(8,128)(2,1)S(1)}, u32[]{:S(2)}, u32[]{:S(2)}) collective-permute-start(bf16[128,4096]{1,0:T(8,128)(2,1)S(1)} %slice.121), channel_id=1, source_target_pairs={{0,1},{1,0},{2,3},{3,2},{4,5},{5,4},{6,7},{7,6},{64,65},{65,64},{6... | collective-permute-start | bytes 3145736 | tf_op jit(solution)/shard_map/ppermute | solution.py:37
  75.3 4.8 %collective-permute-start.15 = (bf16[128,4096]{1,0:T(8,128)(2,1)S(1)}, bf16[128,4096]{1,0:T(8,128)(2,1)S(1)}, u32[]{:S(2)}, u32[]{:S(2)}) collective-permute-start(bf16[128,4096]{1,0:T(8,128)(2,1)S(1)} %slice.120), channel_id=1, source_target_pairs={{0,1},{1,0},{2,3},{3,2},{4,5},{5,4},{6,7},{7,6},{64,65},{65,64},{6... | collective-permute-start | bytes 3145736 | tf_op jit(solution)/shard_map/ppermute | solution.py:37
  75.8 15.6 %collective-permute-start.6 = (bf16[32,4096]{1,0:T(8,128)(2,1)S(1)}, bf16[32,4096]{1,0:T(8,128)(2,1)S(1)}, u32[]{:S(2)}, u32[]{:S(2)}) collective-permute-start(bf16[32,4096]{1,0:T(8,128)(2,1)S(1)} %get-tuple-element.10), channel_id=1, source_target_pairs={{0,2},{1,3},{2,4},{3,5},{4,6},{5,7},{6,0},{7,1},{64,66},{65,67},{6... | collective-permute-start | bytes 786440 | tf_op jit(solution)/shard_map/ppermute | solution.py:27
  76.1 15.2 %collective-permute-start.7 = (bf16[32,4096]{1,0:T(8,128)(2,1)S(1)}, bf16[32,4096]{1,0:T(8,128)(2,1)S(1)}, u32[]{:S(2)}, u32[]{:S(2)}) collective-permute-start(bf16[32,4096]{1,0:T(8,128)(2,1)S(1)} %get-tuple-element.12), channel_id=1, source_target_pairs={{0,6},{1,7},{2,0},{3,1},{4,2},{5,3},{6,4},{7,5},{64,70},{65,71},{6... | collective-permute-start | bytes 786440 | tf_op jit(solution)/shard_map/ppermute | solution.py:27
  79.1 12.3 %collective-permute-start.8 = (bf16[32,4096]{1,0:T(8,128)(2,1)S(1)}, bf16[32,4096]{1,0:T(8,128)(2,1)S(1)}, u32[]{:S(2)}, u32[]{:S(2)}) collective-permute-start(bf16[32,4096]{1,0:T(8,128)(2,1)S(1)} %get-tuple-element.11), channel_id=1, source_target_pairs={{0,4},{1,5},{2,6},{3,7},{4,0},{5,1},{6,2},{7,3},{64,68},{65,69},{6... | collective-permute-start | bytes 786440 | tf_op jit(solution)/shard_map/ppermute | solution.py:27
  80.4 14.7 %collective-permute-start.16 = (bf16[4,16,4096]{2,1,0:T(8,128)(2,1)S(1)}, bf16[4,16,4096]{2,1,0:T(8,128)(2,1)S(1)}, u32[]{:S(2)}, u32[]{:S(2)}) collective-permute-start(bf16[4,16,4096]{2,1,0:T(8,128)(2,1)S(1)} %fusion.5), channel_id=1, source_target_pairs={{0,72},{1,73},{2,74},{3,75},{4,76},{5,77},{6,78},{7,79},{64,8},{65... | collective-permute-start | bytes 1572872 | tf_op jit(solution)/shard_map/ppermute | solution.py:33
  91.5 14.4 %copy-start = (f32[32,4096]{1,0:T(8,128)S(1)}, f32[32,4096]{1,0:T(8,128)}, u32[]{:S(2)}) copy-start(f32[32,4096]{1,0:T(8,128)} %param.13) | copy-start | bytes 1572868
  91.5 9.9 %collective-permute-start.9 = (bf16[16,4096]{1,0:T(8,128)(2,1)S(1)}, bf16[16,4096]{1,0:T(8,128)(2,1)S(1)}, u32[]{:S(2)}, u32[]{:S(2)}) collective-permute-start(bf16[16,4096]{1,0:T(8,128)(2,1)S(1)} %slice.122), channel_id=1, source_target_pairs={{0,72},{1,73},{2,74},{3,75},{4,76},{5,77},{6,78},{7,79},{64,8},{65... | collective-permute-start | bytes 393224 | tf_op jit(solution)/shard_map/ppermute | solution.py:33
  95.3 6.8 %collective-permute-start.17 = (bf16[16,4096]{1,0:T(8,128)(2,1)S(1)}, bf16[16,4096]{1,0:T(8,128)(2,1)S(1)}, u32[]{:S(2)}, u32[]{:S(2)}) collective-permute-start(bf16[16,4096]{1,0:T(8,128)(2,1)S(1)} %get-tuple-element.13), channel_id=1, source_target_pairs={{0,2},{1,3},{2,4},{3,5},{4,6},{5,7},{6,0},{7,1},{64,66},{65,67},{6... | collective-permute-start | bytes 393224 | tf_op jit(solution)/shard_map/ppermute | solution.py:27
  95.7 6.9 %collective-permute-start.18 = (bf16[16,4096]{1,0:T(8,128)(2,1)S(1)}, bf16[16,4096]{1,0:T(8,128)(2,1)S(1)}, u32[]{:S(2)}, u32[]{:S(2)}) collective-permute-start(bf16[16,4096]{1,0:T(8,128)(2,1)S(1)} %get-tuple-element.15), channel_id=1, source_target_pairs={{0,6},{1,7},{2,0},{3,1},{4,2},{5,3},{6,4},{7,5},{64,70},{65,71},{6... | collective-permute-start | bytes 393224 | tf_op jit(solution)/shard_map/ppermute | solution.py:27
  98.6 6.5 %collective-permute-start.19 = (bf16[16,4096]{1,0:T(8,128)(2,1)S(1)}, bf16[16,4096]{1,0:T(8,128)(2,1)S(1)}, u32[]{:S(2)}, u32[]{:S(2)}) collective-permute-start(bf16[16,4096]{1,0:T(8,128)(2,1)S(1)} %get-tuple-element.14), channel_id=1, source_target_pairs={{0,4},{1,5},{2,6},{3,7},{4,0},{5,1},{6,2},{7,3},{64,68},{65,69},{6... | collective-permute-start | bytes 393224 | tf_op jit(solution)/shard_map/ppermute | solution.py:27
  102.1 5.9 %copy-start.1 = (f32[32,4096]{1,0:T(8,128)S(1)}, f32[32,4096]{1,0:T(8,128)}, u32[]{:S(2)}) copy-start(f32[32,4096]{1,0:T(8,128)} %param.15) | copy-start | bytes 1572868
Sparse Core Ops, SparseCore 0:
  39.1 38.7 all-gather.1

commit v2 on v1

v2 whole, which is shorter than its diff:
```python
import jax
import jax.numpy as jnp
from jax import lax
from jax.experimental import pallas as pl
from jax.experimental.pallas import tpu as pltpu
from jax.sharding import PartitionSpec as P

outer_rate = 0.7
outer_beta = 0.9
AXES = ("replica", "tensor")
EXTENT_X, EXTENT_Y, EXTENT_Z = 4, 4, 4


def position(x, y, z, core):
    return ((y % 2) * EXTENT_X + x) * 16 + (y // 2) * 8 + z * 2 + core


def pairs(move):
    return [
        (position(x, y, z, core), position(*move(x, y, z, core)))
        for x in range(EXTENT_X)
        for y in range(EXTENT_Y)
        for z in range(EXTENT_Z)
        for core in range(2)
    ]


def send_z(rows, distance):
    return lax.ppermute(
        rows, AXES, pairs(lambda x, y, z, core: (x, y, (z + distance) % EXTENT_Z, core))
    )


def swap_y(rows):
    return lax.ppermute(rows, AXES, pairs(lambda x, y, z, core: (x, 3 - y, z, core)))


def swap_core(rows):
    return lax.ppermute(rows, AXES, pairs(lambda x, y, z, core: (x, y, z, 1 - core)))


def times_transpose(left_rows, weight):
    return lax.dot_general(
        left_rows, weight, (((1,), (1,)), ((), ())), preferred_element_type=jnp.float32
    )


def swap_x(rows, outer):
    def move(x, y, z, core):
        return (3 - x if outer else x ^ 1, y, z, core)

    return lax.ppermute(rows, AXES, pairs(move))


def swap_y_low(rows):
    return lax.ppermute(rows, AXES, pairs(lambda x, y, z, core: (x, y ^ 1, z, core)))


def order_z(block):
    one, three, two = send_z(block, -1), send_z(block, -3), send_z(block, -2)
    return [one, two, three]


def half(rows):
    return rows.astype(jnp.bfloat16)


def full(rows):
    return rows.astype(jnp.float32)


def sum_cores(partial):
    return partial[:128] + full(swap_core(half(partial[128:])))


def first_pseudo(outer_ref, here_ref, there_ref, sum_ref):
    outer = outer_ref[...]
    sum_ref[...] = (outer - full(here_ref[...])) + (outer - full(there_ref[...]))


def on_device(tokens, cotangent, w_gate, w_up, w_down, outer_frag, local_frag, momentum):
    width = tokens.shape[1]
    both = jnp.concatenate([tokens, swap_y(tokens)], 0)
    line = jnp.concatenate([cotangent] + order_z(cotangent), 0)
    local = local_frag[0]
    pseudo = pl.pallas_call(
        first_pseudo,
        out_shape=jax.ShapeDtypeStruct(outer_frag.shape, jnp.float32),
        cost_estimate=pl.CostEstimate(flops=25_000_000_000, bytes_accessed=0, transcendentals=0),
    )(outer_frag, local, swap_x(local, False))
    both, line, pseudo = lax.optimization_barrier((both, line, pseudo))
    token_near = jnp.concatenate([both] + order_z(both), 0)
    across = swap_y(line)
    pseudo = pseudo + swap_x(pseudo, True)
    cotangent_near = jnp.stack([line.reshape(4, 16, width), across.reshape(4, 16, width)], 1)
    cotangent_near = cotangent_near.reshape(128, width)
    token_rows = jnp.concatenate([token_near, swap_core(token_near)], 0)
    cotangent_rows = jnp.concatenate([cotangent_near, swap_core(cotangent_near)], 0)
    pre_gate = jnp.dot(token_rows, w_gate, preferred_element_type=jnp.float32)
    pre_up = jnp.dot(token_rows, w_up, preferred_element_type=jnp.float32)
    sigmoid_gate = jax.nn.sigmoid(pre_gate)
    hidden = (pre_gate * sigmoid_gate * pre_up).astype(jnp.bfloat16)
    hidden, pseudo = lax.optimization_barrier((hidden, pseudo))
    pseudo = pseudo + swap_y_low(pseudo)
    out_blocks = sum_cores(jnp.dot(hidden, w_down, preferred_element_type=jnp.float32))
    out_blocks = out_blocks.reshape(4, 32, width)
    out_sent = half(out_blocks[1:])
    d_hidden = times_transpose(cotangent_rows, w_down)
    d_gate = (d_hidden * pre_up * sigmoid_gate * (1.0 + pre_gate * (1.0 - sigmoid_gate))).astype(
        jnp.bfloat16
    )
    d_up = (d_hidden * pre_gate * sigmoid_gate).astype(jnp.bfloat16)
    out_sent, d_gate, d_up = lax.optimization_barrier((out_sent, d_gate, d_up))
    out_arrived = [send_z(out_sent[d - 1], d) for d in (1, 3, 2)]
    grad_blocks = sum_cores(times_transpose(d_gate, w_gate) + times_transpose(d_up, w_up))
    grad_blocks = grad_blocks.reshape(4, 2, 16, width)
    grad_line = grad_blocks[:, 0] + full(swap_y(half(grad_blocks[:, 1])))
    grad_sent = half(grad_line[1:])
    out_both = out_blocks[0] + full(out_arrived[0]) + full(out_arrived[1]) + full(out_arrived[2])
    layer_output = out_both[:16] + full(swap_y(half(out_both[16:])))
    grad_arrived = [send_z(grad_sent[d - 1], d) for d in (1, 3, 2)]
    input_grad = (
        grad_line[0] + full(grad_arrived[0]) + full(grad_arrived[1]) + full(grad_arrived[2])
    )
    mean_delta = pseudo / lax.axis_size("replica")
    new_momentum = outer_beta * momentum + mean_delta
    new_outer = outer_frag - outer_rate * (mean_delta + outer_beta * new_momentum)
    return (layer_output, input_grad, new_outer, new_momentum)


def solution(mesh):
    in_specs = (
        P(AXES, None),
        P(AXES, None),
        P(None, "tensor"),
        P(None, "tensor"),
        P("tensor", None),
        P("tensor", None),
        P("replica", "tensor", None),
        P("tensor", None),
    )
    out_specs = (P(AXES, None), P(AXES, None), P("tensor", None), P("tensor", None))
    return jax.shard_map(
        on_device, mesh=mesh, in_specs=in_specs, out_specs=out_specs, check_vma=False
    )
```

time: 116 us -> 97.2 us (0.84)
  between operations: 14.4 us -> 0.99 us
  starting transfers between devices: 33.2 us -> 30.4 us
  local copies, waits for them, and re-layouts: 4.7 us -> 2.09 us
  Pallas kernels: 0 us -> 2.07 us
  waiting for transfers between devices: 35.6 us -> 34.2 us
    ppermute x4, waiting for transfers between devices: 13.5 us -> 4.25 us  [swap_y(): lax.ppermute(rows, AXES, pairs(lambda x, y, z, core: (x, 3 - y, z, core)))]
    ppermute x0 -> x3, waiting for transfers between devices: none -> 6.42 us  [the longest x2 4.4 us: swap_x(): return lax.ppermute(rows, AXES, pairs(move))]
    ppermute x0 -> x3, starting transfers between devices: none -> 5.2 us  [the longest x2 4.25 us: swap_x(): return lax.ppermute(rows, AXES, pairs(move))]
    ppermute x4, starting transfers between devices: 12 us -> 6.97 us  [swap_y(): lax.ppermute(rows, AXES, pairs(lambda x, y, z, core: (x, 3 - y, z, core)))]
    unnamed x25 -> x24, local copies, waits for them, and re-layouts: 4.17 us -> 1.54 us
    ppermute x12, starting transfers between devices: 20.2 us -> 17.5 us  [send_z(): lax.ppermute(rows, AXES, pairs(lambda x, y, z, core: (x, y, (z + distance...]
    reduce_sum x1 -> x0, other arithmetic: 2.08 us -> none  [on_device(): pseudo = jnp.sum(outer_frag[None] - every_local.astype(jnp.float32), axis=0)]
    pallas_call x0 -> x1, Pallas kernels: none -> 2.07 us  [on_device(): pl.pallas_call(first_pseudo, out_shape=jax.ShapeDtypeStruct(outer_frag.sh...]
  transfers between devices with their start and end apart: 21 -> 23, of which waited for: 9 -> 16; matrix products, arithmetic and copies ran while one was open for 24% -> 23% of each run, Pallas kernels for 0% -> 0%
where the time goes in v2:
time: 97.2 us; the launch traced here: 97 us
  waiting for transfers between devices  34.2 us (35%)
  starting transfers between devices  30.4 us (31%)
  matrix products  21.9 us (23%)
  other arithmetic  5.48 us (6%)
  local copies, waits for them, and re-layouts  2.09 us (2%)
  Pallas kernels  2.07 us (2%)
  between operations  0.99 us (1%)
    ppermute x12, waiting for transfers between devices, send_z(): lax.ppermute(rows, AXES, pairs(lambda x, y, z, core: (x, y, (z + distance...  21.8 us
    ppermute x12, starting transfers between devices, send_z(): lax.ppermute(rows, AXES, pairs(lambda x, y, z, core: (x, y, (z + distance...  17.5 us
    dot_general x3, matrix products, times_transpose(): lax.dot_general(left_rows, weight, (((1,), (1,)), ((), ())), preferred_el...  11.5 us
    ppermute x4, starting transfers between devices, swap_y(): lax.ppermute(rows, AXES, pairs(lambda x, y, z, core: (x, 3 - y, z, core)))  6.97 us
    dot_general x1, matrix products, on_device(): pre_gate = jnp.dot(token_rows, w_gate, preferred_element_type=jnp.float32)  5.63 us
    ppermute x2, waiting for transfers between devices, swap_x(): return lax.ppermute(rows, AXES, pairs(move))  4.4 us
    ppermute x4, waiting for transfers between devices, swap_y(): lax.ppermute(rows, AXES, pairs(lambda x, y, z, core: (x, 3 - y, z, core)))  4.25 us
    ppermute x2, starting transfers between devices, swap_x(): return lax.ppermute(rows, AXES, pairs(move))  4.25 us
  transfers between devices with their start and end apart: 23, of which 16 were waited for; matrix products, arithmetic and copies ran while one was open for 23% of the time, Pallas kernels for 0%

profile of v2, /device:TPU:0, one launch (start us, length us, event | category | flops | bytes accessed | tf_op | source)
XLA Modules:
  0.0 97.0 jit_solution(10797726622426965817)
XLA Ops:
  0.6 2.1 %collective-permute-start.3 = (bf16[16,4096]{1,0:T(8,128)(2,1)}, bf16[16,4096]{1,0:T(8,128)(2,1)S(1)}, u32[]{:S(2)}, u32[]{:S(2)}) collective-permute-start(bf16[16,4096]{1,0:T(8,128)(2,1)} %param.9), channel_id=1, source_target_pairs={{0,2},{1,3},{2,4},{3,5},{4,6},{5,7},{6,0},{7,1},{64,66},{65,67},{6... | collective-permute-start | bytes 393224 | tf_op jit(solution)/shard_map/ppermute | solution.py:29
  2.7 3.6 %collective-permute-start.2 = (bf16[16,4096]{1,0:T(8,128)(2,1)}, bf16[16,4096]{1,0:T(8,128)(2,1)S(1)}, u32[]{:S(2)}, u32[]{:S(2)}) collective-permute-start(bf16[16,4096]{1,0:T(8,128)(2,1)} %param.9), channel_id=1, source_target_pairs={{0,4},{1,5},{2,6},{3,7},{4,0},{5,1},{6,2},{7,3},{64,68},{65,69},{6... | collective-permute-start | bytes 393224 | tf_op jit(solution)/shard_map/ppermute | solution.py:29
  7.3 3.0 %collective-permute-start = (bf16[16,4096]{1,0:T(8,128)(2,1)}, bf16[16,4096]{1,0:T(8,128)(2,1)S(1)}, u32[]{:S(2)}, u32[]{:S(2)}) collective-permute-start(bf16[16,4096]{1,0:T(8,128)(2,1)} %param.8), channel_id=1, source_target_pairs={{0,72},{1,73},{2,74},{3,75},{4,76},{5,77},{6,78},{7,79},{64,8},{65... | collective-permute-start | bytes 393224 | tf_op jit(solution)/shard_map/ppermute | solution.py:35
  10.3 1.5 %collective-permute-start.4 = (bf16[32,4096]{1,0:T(8,128)(2,1)}, bf16[32,4096]{1,0:T(8,128)(2,1)S(1)}, u32[]{:S(2)}, u32[]{:S(2)}) collective-permute-start(bf16[32,4096]{1,0:T(8,128)(2,1)} %bitcast.57), channel_id=1, source_target_pairs={{0,16},{1,17},{2,18},{3,19},{4,20},{5,21},{6,22},{7,23},{64,80},{6... | collective-permute-start | bytes 786440 | tf_op jit(solution)/shard_map/ppermute | solution.py:52
  14.6 2.8 %collective-permute-done.4.there_ref = bf16[32,4096]{1,0:T(8,128)(2,1)S(1)} collective-permute-done((bf16[32,4096]{1,0:T(8,128)(2,1)}, bf16[32,4096]{1,0:T(8,128)(2,1)S(1)}, u32[]{:S(2)}, u32[]{:S(2)}) %collective-permute-start.4) | collective-permute-done | bytes 262176 | tf_op jit(solution)/shard_map/ppermute | solution.py:52
  18.1 2.1 %shard_map.111 = f32[32,4096]{1,0:T(8,128)} custom-call(f32[32,4096]{1,0:T(8,128)} %outer_ref.1, bf16[32,4096]{1,0:T(8,128)(2,1)} %bitcast.58, bf16[32,4096]{1,0:T(8,128)(2,1)} %copy-done.3), custom_call_target="tpu_custom_call" | custom-call | flops 24999999488 | tf_op jit(solution)/shard_map/pallas_call | solution.py:86
  20.5 2.8 %collective-permute-start.6 = (bf16[32,4096]{1,0:T(8,128)(2,1)S(1)}, bf16[32,4096]{1,0:T(8,128)(2,1)S(1)}, u32[]{:S(2)}, u32[]{:S(2)}) collective-permute-start(bf16[32,4096]{1,0:T(8,128)(2,1)S(1)} %pad_maximum_fusion.3), channel_id=1, source_target_pairs={{0,4},{1,5},{2,6},{3,7},{4,0},{5,1},{6,2},{7,3},{64,68},{65,69},{6... | collective-permute-start | bytes 786440 | tf_op jit(solution)/shard_map/ppermute | solution.py:29
  23.9 2.8 %collective-permute-start.9 = (f32[32,4096]{1,0:T(8,128)}, f32[32,4096]{1,0:T(8,128)S(1)}, u32[]{:S(2)}, u32[]{:S(2)}) collective-permute-start(f32[32,4096]{1,0:T(8,128)} %shard_map.111), channel_id=1, source_target_pairs={{0,48},{1,49},{2,50},{3,51},{4,52},{5,53},{6,54},{7,55},{64,112},{... | collective-permute-start | bytes 1572872 | tf_op jit(solution)/shard_map/ppermute | solution.py:52
  26.6 2.4 %collective-permute-done.5 = bf16[32,4096]{1,0:T(8,128)(2,1)S(1)} collective-permute-done((bf16[32,4096]{1,0:T(8,128)(2,1)S(1)}, bf16[32,4096]{1,0:T(8,128)(2,1)S(1)}, u32[]{:S(2)}, u32[]{:S(2)}) %collective-permute-start.5) | collective-permute-done | bytes 262176 | tf_op jit(solution)/shard_map/ppermute | solution.py:29
  29.0 2.0 %collective-permute-done.6 = bf16[32,4096]{1,0:T(8,128)(2,1)S(1)} collective-permute-done((bf16[32,4096]{1,0:T(8,128)(2,1)S(1)}, bf16[32,4096]{1,0:T(8,128)(2,1)S(1)}, u32[]{:S(2)}, u32[]{:S(2)}) %collective-permute-start.6) | collective-permute-done | bytes 262176 | tf_op jit(solution)/shard_map/ppermute | solution.py:29
  31.0 2.8 %collective-permute-done.7 = bf16[32,4096]{1,0:T(8,128)(2,1)S(1)} collective-permute-done((bf16[32,4096]{1,0:T(8,128)(2,1)S(1)}, bf16[32,4096]{1,0:T(8,128)(2,1)S(1)}, u32[]{:S(2)}, u32[]{:S(2)}) %collective-permute-start.7) | collective-permute-done | bytes 262176 | tf_op jit(solution)/shard_map/ppermute | solution.py:29
  34.1 1.5 %collective-permute-done.11 = bf16[64,4096]{1,0:T(8,128)(2,1)S(1)} collective-permute-done((bf16[64,4096]{1,0:T(8,128)(2,1)S(1)}, bf16[64,4096]{1,0:T(8,128)(2,1)S(1)}, u32[]{:S(2)}, u32[]{:S(2)}) %collective-permute-start.11) | collective-permute-done | bytes 524320 | tf_op jit(solution)/shard_map/ppermute | solution.py:35
  35.9 1.6 %collective-permute-done.9 = f32[32,4096]{1,0:T(8,128)S(1)} collective-permute-done((f32[32,4096]{1,0:T(8,128)}, f32[32,4096]{1,0:T(8,128)S(1)}, u32[]{:S(2)}, u32[]{:S(2)}) %collective-permute-start.9) | collective-permute-done | bytes 524320 | tf_op jit(solution)/shard_map/ppermute | solution.py:52
  37.7 5.6 %fusion.14 = f32[256,896]{1,0:T(8,128)S(1)} fusion(bf16[256,4096]{1,0:T(8,128)(2,1)S(1)} %constant_dynamic-update-slice_fusion, bf16[4096,896]{1,0:T(8,128)(2,1)} %param.10), kind=kOutput, calls=%fused_computation.47 | convolution fusion | flops 1879048192 | bytes 10354688 | tf_op jit(solution)/shard_map/dot_general | solution.py:99
  44.1 2.4 %fusion.15 = f32[256,896]{1,0:T(8,128)S(1)} fusion(bf16[256,4096]{1,0:T(8,128)(2,1)S(1)} %constant_dynamic-update-slice_fusion, bf16[4096,896]{1,0:T(8,128)(2,1)S(1)} %bitcast.56), kind=kOutput, calls=%fused_computation.48 | convolution fusion | flops 1879048192 | bytes 10354688 | tf_op jit(solution)/shard_map/dot_general | solution.py:100
  46.5 2.6 %multiply_convert_fusion = (bf16[256,896]{1,0:T(8,128)(2,1)S(1)}, bf16[256,896]{1,0:T(8,128)(2,1)S(1)}, bf16[256,896]{1,0:T(8,128)(2,1)S(1)}) fusion(f32[256,896]{1,0:T(8,128)S(1)} %fusion.14, f32[256,896]{1,0:T(8,128)S(1)} %fusion.15, bf16[896,4096]{1,0:T(8,128)(2,1)S(1)} %bitcast.45, bf16[128,4096]{1,0:T(8,128)(2,1)S(1)} %collective-permute-done.12, ...), kind=kOutput, calls=%fused_computation.15 | convolution fusion | flops 1886912512 | bytes 12648448 | tf_op jit(solution)/shard_map/dot_general | solution.py:43
  49.1 2.3 %fusion.16 = f32[256,4096]{1,0:T(8,128)S(1)} fusion(bf16[256,896]{1,0:T(8,128)(2,1)S(1)} %get-tuple-element.14, bf16[896,4096]{1,0:T(8,128)(2,1)S(1)} %bitcast.45), kind=kOutput, calls=%fused_computation.49 | convolution fusion | flops 1879048192 | bytes 11993088 | tf_op jit(solution)/shard_map/dot_general | solution.py:105
  52.6 1.7 %collective-permute-done.10 = bf16[128,4096]{1,0:T(8,128)(2,1)S(1)} collective-permute-done((bf16[128,4096]{1,0:T(8,128)(2,1)S(1)}, bf16[128,4096]{1,0:T(8,128)(2,1)S(1)}, u32[]{:S(2)}, u32[]{:S(2)}) %collective-permute-start.10) | collective-permute-done | bytes 1048608 | tf_op jit(solution)/shard_map/ppermute | solution.py:39
  54.7 4.3 %fusion.17 = f32[256,4096]{1,0:T(8,128)} fusion(bf16[256,896]{1,0:T(8,128)(2,1)S(1)} %get-tuple-element.17, bf16[4096,896]{1,0:T(8,128)(2,1)S(1)} %bitcast.54), kind=kOutput, calls=%fused_computation.50 | convolution fusion | flops 1879048192 | bytes 11993088 | tf_op jit(solution)/shard_map/dot_general | solution.py:43
  59.1 4.6 %convolution_add_fusion = f32[256,4096]{1,0:T(8,128)S(1)} fusion(f32[256,4096]{1,0:T(8,128)} %fusion.17, bf16[256,896]{1,0:T(8,128)(2,1)S(1)} %get-tuple-element.18, bf16[4096,896]{1,0:T(8,128)(2,1)S(1)} %bitcast.56), kind=kOutput, calls=%fused_computation | convolution fusion | flops 1880096768 | bytes 16187392 | tf_op jit(solution)/shard_map/dot_general | solution.py:43
  64.0 2.0 %collective-permute-done.22 = f32[32,4096]{1,0:T(8,128)S(1)} collective-permute-done((f32[32,4096]{1,0:T(8,128)S(1)}, f32[32,4096]{1,0:T(8,128)S(1)}, u32[]{:S(2)}, u32[]{:S(2)}) %collective-permute-start.22) | collective-permute-done | bytes 524320 | tf_op jit(solution)/shard_map/ppermute | solution.py:56
  66.0 1.1 %multiply_subtract_fusion = (f32[32,4096]{1,0:T(8,128)}, f32[32,4096]{1,0:T(8,128)}) fusion(f32[32,4096]{1,0:T(8,128)S(1)} %copy-done.1, f32[32,4096]{1,0:T(8,128)S(1)} %add.52, f32[32,4096]{1,0:T(8,128)S(1)} %collective-permute-done.22, f32[32,4096]{1,0:T(8,128)S(1)} %copy-done.2), kind=kLoop, calls=%fused_computation.24 | loop fusion | flops 1048576 | bytes 3145728 | tf_op jit(solution)/shard_map/sub | solution.py:127
  67.2 2.3 %collective-permute-start.15 = (bf16[32,4096]{1,0:T(8,128)(2,1)S(1)}, bf16[32,4096]{1,0:T(8,128)(2,1)S(1)}, u32[]{:S(2)}, u32[]{:S(2)}) collective-permute-start(bf16[32,4096]{1,0:T(8,128)(2,1)S(1)} %get-tuple-element.28), channel_id=1, source_target_pairs={{0,4},{1,5},{2,6},{3,7},{4,0},{5,1},{6,2},{7,3},{64,68},{65,69},{6... | collective-permute-start | bytes 786440 | tf_op jit(solution)/shard_map/ppermute | solution.py:29
  69.5 2.3 %collective-permute-start.14 = (bf16[32,4096]{1,0:T(8,128)(2,1)S(1)}, bf16[32,4096]{1,0:T(8,128)(2,1)S(1)}, u32[]{:S(2)}, u32[]{:S(2)}) collective-permute-start(bf16[32,4096]{1,0:T(8,128)(2,1)S(1)} %get-tuple-element.29), channel_id=1, source_target_pairs={{0,6},{1,7},{2,0},{3,1},{4,2},{5,3},{6,4},{7,5},{64,70},{65,71},{6... | collective-permute-start | bytes 786440 | tf_op jit(solution)/shard_map/ppermute | solution.py:29
  72.2 1.6 %collective-permute-start.18 = (bf16[4,16,4096]{2,1,0:T(8,128)(2,1)S(1)}, bf16[4,16,4096]{2,1,0:T(8,128)(2,1)S(1)}, u32[]{:S(2)}, u32[]{:S(2)}) collective-permute-start(bf16[4,16,4096]{2,1,0:T(8,128)(2,1)S(1)} %fusion.5), channel_id=1, source_target_pairs={{0,72},{1,73},{2,74},{3,75},{4,76},{5,77},{6,78},{7,79},{64,8},{65... | collective-permute-start | bytes 1572872 | tf_op jit(solution)/shard_map/ppermute | solution.py:35
  73.8 4.3 %collective-permute-done.15 = bf16[32,4096]{1,0:T(8,128)(2,1)S(1)} collective-permute-done((bf16[32,4096]{1,0:T(8,128)(2,1)S(1)}, bf16[32,4096]{1,0:T(8,128)(2,1)S(1)}, u32[]{:S(2)}, u32[]{:S(2)}) %collective-permute-start.15) | collective-permute-done | bytes 262176 | tf_op jit(solution)/shard_map/ppermute | solution.py:29
  78.0 4.3 %collective-permute-done.14 = bf16[32,4096]{1,0:T(8,128)(2,1)S(1)} collective-permute-done((bf16[32,4096]{1,0:T(8,128)(2,1)S(1)}, bf16[32,4096]{1,0:T(8,128)(2,1)S(1)}, u32[]{:S(2)}, u32[]{:S(2)}) %collective-permute-start.14) | collective-permute-done | bytes 262176 | tf_op jit(solution)/shard_map/ppermute | solution.py:29
  82.5 1.8 %collective-permute-start.16 = (bf16[16,4096]{1,0:T(8,128)(2,1)S(1)}, bf16[16,4096]{1,0:T(8,128)(2,1)S(1)}, u32[]{:S(2)}, u32[]{:S(2)}) collective-permute-start(bf16[16,4096]{1,0:T(8,128)(2,1)S(1)} %slice.122), channel_id=1, source_target_pairs={{0,72},{1,73},{2,74},{3,75},{4,76},{5,77},{6,78},{7,79},{64,8},{65... | collective-permute-start | bytes 393224 | tf_op jit(solution)/shard_map/ppermute | solution.py:35
  84.3 2.5 %collective-permute-done.18 = bf16[4,16,4096]{2,1,0:T(8,128)(2,1)S(1)} collective-permute-done((bf16[4,16,4096]{2,1,0:T(8,128)(2,1)S(1)}, bf16[4,16,4096]{2,1,0:T(8,128)(2,1)S(1)}, u32[]{:S(2)}, u32[]{:S(2)}) %collective-permute-start.18) | collective-permute-done | bytes 524320 | tf_op jit(solution)/shard_map/ppermute | solution.py:35
  87.8 2.2 %collective-permute-start.20 = (bf16[16,4096]{1,0:T(8,128)(2,1)S(1)}, bf16[16,4096]{1,0:T(8,128)(2,1)S(1)}, u32[]{:S(2)}, u32[]{:S(2)}) collective-permute-start(bf16[16,4096]{1,0:T(8,128)(2,1)S(1)} %get-tuple-element.32), channel_id=1, source_target_pairs={{0,6},{1,7},{2,0},{3,1},{4,2},{5,3},{6,4},{7,5},{64,70},{65,71},{6... | collective-permute-start | bytes 393224 | tf_op jit(solution)/shard_map/ppermute | solution.py:29
  90.9 2.8 %collective-permute-done.21 = bf16[16,4096]{1,0:T(8,128)(2,1)S(1)} collective-permute-done((bf16[16,4096]{1,0:T(8,128)(2,1)S(1)}, bf16[16,4096]{1,0:T(8,128)(2,1)S(1)}, u32[]{:S(2)}, u32[]{:S(2)}) %collective-permute-start.21) | collective-permute-done | bytes 131104 | tf_op jit(solution)/shard_map/ppermute | solution.py:29
  94.5 1.7 %collective-permute-done.19 = bf16[16,4096]{1,0:T(8,128)(2,1)S(1)} collective-permute-done((bf16[16,4096]{1,0:T(8,128)(2,1)S(1)}, bf16[16,4096]{1,0:T(8,128)(2,1)S(1)}, u32[]{:S(2)}, u32[]{:S(2)}) %collective-permute-start.19) | collective-permute-done | bytes 131104 | tf_op jit(solution)/shard_map/ppermute | solution.py:29
  (68 shorter events, 12.6 us)
Async XLA Ops:
  0.6 11.2 %collective-permute-start.3 = (bf16[16,4096]{1,0:T(8,128)(2,1)}, bf16[16,4096]{1,0:T(8,128)(2,1)S(1)}, u32[]{:S(2)}, u32[]{:S(2)}) collective-permute-start(bf16[16,4096]{1,0:T(8,128)(2,1)} %param.9), channel_id=1, source_target_pairs={{0,2},{1,3},{2,4},{3,5},{4,6},{5,7},{6,0},{7,1},{64,66},{65,67},{6... | collective-permute-start | bytes 393224 | tf_op jit(solution)/shard_map/ppermute | solution.py:29
  2.7 9.8 %collective-permute-start.2 = (bf16[16,4096]{1,0:T(8,128)(2,1)}, bf16[16,4096]{1,0:T(8,128)(2,1)S(1)}, u32[]{:S(2)}, u32[]{:S(2)}) collective-permute-start(bf16[16,4096]{1,0:T(8,128)(2,1)} %param.9), channel_id=1, source_target_pairs={{0,4},{1,5},{2,6},{3,7},{4,0},{5,1},{6,2},{7,3},{64,68},{65,69},{6... | collective-permute-start | bytes 393224 | tf_op jit(solution)/shard_map/ppermute | solution.py:29
  6.3 6.2 %collective-permute-start.1 = (bf16[16,4096]{1,0:T(8,128)(2,1)}, bf16[16,4096]{1,0:T(8,128)(2,1)S(1)}, u32[]{:S(2)}, u32[]{:S(2)}) collective-permute-start(bf16[16,4096]{1,0:T(8,128)(2,1)} %param.9), channel_id=1, source_target_pairs={{0,6},{1,7},{2,0},{3,1},{4,2},{5,3},{6,4},{7,5},{64,70},{65,71},{6... | collective-permute-start | bytes 393224 | tf_op jit(solution)/shard_map/ppermute | solution.py:29
  7.3 6.4 %collective-permute-start = (bf16[16,4096]{1,0:T(8,128)(2,1)}, bf16[16,4096]{1,0:T(8,128)(2,1)S(1)}, u32[]{:S(2)}, u32[]{:S(2)}) collective-permute-start(bf16[16,4096]{1,0:T(8,128)(2,1)} %param.8), channel_id=1, source_target_pairs={{0,72},{1,73},{2,74},{3,75},{4,76},{5,77},{6,78},{7,79},{64,8},{65... | collective-permute-start | bytes 393224 | tf_op jit(solution)/shard_map/ppermute | solution.py:35
  10.3 7.1 %collective-permute-start.4 = (bf16[32,4096]{1,0:T(8,128)(2,1)}, bf16[32,4096]{1,0:T(8,128)(2,1)S(1)}, u32[]{:S(2)}, u32[]{:S(2)}) collective-permute-start(bf16[32,4096]{1,0:T(8,128)(2,1)} %bitcast.57), channel_id=1, source_target_pairs={{0,16},{1,17},{2,18},{3,19},{4,20},{5,21},{6,22},{7,23},{64,80},{6... | collective-permute-start | bytes 786440 | tf_op jit(solution)/shard_map/ppermute | solution.py:52
  20.2 8.8 %collective-permute-start.5 = (bf16[32,4096]{1,0:T(8,128)(2,1)S(1)}, bf16[32,4096]{1,0:T(8,128)(2,1)S(1)}, u32[]{:S(2)}, u32[]{:S(2)}) collective-permute-start(bf16[32,4096]{1,0:T(8,128)(2,1)S(1)} %pad_maximum_fusion.3), channel_id=1, source_target_pairs={{0,6},{1,7},{2,0},{3,1},{4,2},{5,3},{6,4},{7,5},{64,70},{65,71},{6... | collective-permute-start | bytes 786440 | tf_op jit(solution)/shard_map/ppermute | solution.py:29
  20.5 10.5 %collective-permute-start.6 = (bf16[32,4096]{1,0:T(8,128)(2,1)S(1)}, bf16[32,4096]{1,0:T(8,128)(2,1)S(1)}, u32[]{:S(2)}, u32[]{:S(2)}) collective-permute-start(bf16[32,4096]{1,0:T(8,128)(2,1)S(1)} %pad_maximum_fusion.3), channel_id=1, source_target_pairs={{0,4},{1,5},{2,6},{3,7},{4,0},{5,1},{6,2},{7,3},{64,68},{65,69},{6... | collective-permute-start | bytes 786440 | tf_op jit(solution)/shard_map/ppermute | solution.py:29
  23.3 10.5 %collective-permute-start.7 = (bf16[32,4096]{1,0:T(8,128)(2,1)S(1)}, bf16[32,4096]{1,0:T(8,128)(2,1)S(1)}, u32[]{:S(2)}, u32[]{:S(2)}) collective-permute-start(bf16[32,4096]{1,0:T(8,128)(2,1)S(1)} %pad_maximum_fusion.3), channel_id=1, source_target_pairs={{0,2},{1,3},{2,4},{3,5},{4,6},{5,7},{6,0},{7,1},{64,66},{65,67},{6... | collective-permute-start | bytes 786440 | tf_op jit(solution)/shard_map/ppermute | solution.py:29
  23.3 12.3 %collective-permute-start.11 = (bf16[64,4096]{1,0:T(8,128)(2,1)S(1)}, bf16[64,4096]{1,0:T(8,128)(2,1)S(1)}, u32[]{:S(2)}, u32[]{:S(2)}) collective-permute-start(bf16[64,4096]{1,0:T(8,128)(2,1)S(1)} %pad_maximum_fusion.2), channel_id=1, source_target_pairs={{0,72},{1,73},{2,74},{3,75},{4,76},{5,77},{6,78},{7,79},{64,8},{65... | collective-permute-start | bytes 1572872 | tf_op jit(solution)/shard_map/ppermute | solution.py:35
  23.9 13.7 %collective-permute-start.9 = (f32[32,4096]{1,0:T(8,128)}, f32[32,4096]{1,0:T(8,128)S(1)}, u32[]{:S(2)}, u32[]{:S(2)}) collective-permute-start(f32[32,4096]{1,0:T(8,128)} %shard_map.111), channel_id=1, source_target_pairs={{0,48},{1,49},{2,50},{3,51},{4,52},{5,53},{6,54},{7,55},{64,112},{... | collective-permute-start | bytes 1572872 | tf_op jit(solution)/shard_map/ppermute | solution.py:52
  33.9 3.6 %copy-start = (f32[32,4096]{1,0:T(8,128)S(1)}, f32[32,4096]{1,0:T(8,128)}, u32[]{:S(2)}) copy-start(f32[32,4096]{1,0:T(8,128)} %shard_map.111) | copy-start | bytes 1572868
  33.9 3.7 %collective-permute-start.8 = (bf16[128,4096]{1,0:T(8,128)(2,1)S(1)}, bf16[128,4096]{1,0:T(8,128)(2,1)S(1)}, u32[]{:S(2)}, u32[]{:S(2)}) collective-permute-start(bf16[128,4096]{1,0:T(8,128)(2,1)S(1)} %pad_maximum_fusion), channel_id=1, source_target_pairs={{0,1},{1,0},{2,3},{3,2},{4,5},{5,4},{6,7},{7,6},{64,65},{65,64},{6... | collective-permute-start | bytes 3145736 | tf_op jit(solution)/shard_map/ppermute | solution.py:39
  35.7 10.8 %collective-permute-start.12 = (bf16[128,4096]{1,0:T(8,128)(2,1)S(1)}, bf16[128,4096]{1,0:T(8,128)(2,1)S(1)}, u32[]{:S(2)}, u32[]{:S(2)}) collective-permute-start(bf16[128,4096]{1,0:T(8,128)(2,1)S(1)} %bitcast.50), channel_id=1, source_target_pairs={{0,1},{1,0},{2,3},{3,2},{4,5},{5,4},{6,7},{7,6},{64,65},{65,64},{6... | collective-permute-start | bytes 3145736 | tf_op jit(solution)/shard_map/ppermute | solution.py:39
  37.6 5.8 %slice-start.4 = ((s8[7340032]{0:T(1024)(128)(4,1)}), s8[4194304]{0:T(1024)(128)(4,1)S(1)}, s32[]{:S(2)}) async-start(s8[7340032]{0:T(1024)(128)(4,1)} %bitcast.55), calls=%async_computation.4 | async-start | bytes 8388608
  37.6 8.9 %slice-start = ((s8[7340032]{0:T(1024)(128)(4,1)}), s8[4194304]{0:T(1024)(128)(4,1)S(1)}, s32[]{:S(2)}) async-start(s8[7340032]{0:T(1024)(128)(4,1)} %bitcast.44), calls=%async_computation | async-start | bytes 8388608
  37.7 6.4 %slice-start.5 = ((s8[7340032]{0:T(1024)(128)(4,1)}), s8[3145728]{0:T(1024)(128)(4,1)S(1)}, s32[]{:S(2)}) async-start(s8[7340032]{0:T(1024)(128)(4,1)} %bitcast.55), calls=%async_computation.5 | async-start | bytes 6291456
  37.7 8.8 %slice-start.1 = ((s8[7340032]{0:T(1024)(128)(4,1)}), s8[3145728]{0:T(1024)(128)(4,1)S(1)}, s32[]{:S(2)}) async-start(s8[7340032]{0:T(1024)(128)(4,1)} %bitcast.44), calls=%async_computation.1 | async-start | bytes 6291456
  49.1 5.6 %slice-start.2 = ((s8[7340032]{0:T(1024)(128)(4,1)}), s8[4194304]{0:T(1024)(128)(4,1)S(1)}, s32[]{:S(2)}) async-start(s8[7340032]{0:T(1024)(128)(4,1)} %bitcast.53), calls=%async_computation.2 | async-start | bytes 8388608
  49.1 5.6 %slice-start.3 = ((s8[7340032]{0:T(1024)(128)(4,1)}), s8[3145728]{0:T(1024)(128)(4,1)S(1)}, s32[]{:S(2)}) async-start(s8[7340032]{0:T(1024)(128)(4,1)} %bitcast.53), calls=%async_computation.3 | async-start | bytes 6291456
  51.6 2.7 %collective-permute-start.10 = (bf16[128,4096]{1,0:T(8,128)(2,1)S(1)}, bf16[128,4096]{1,0:T(8,128)(2,1)S(1)}, u32[]{:S(2)}, u32[]{:S(2)}) collective-permute-start(bf16[128,4096]{1,0:T(8,128)(2,1)S(1)} %slice.120), channel_id=1, source_target_pairs={{0,1},{1,0},{2,3},{3,2},{4,5},{5,4},{6,7},{7,6},{64,65},{65,64},{6... | collective-permute-start | bytes 3145736 | tf_op jit(solution)/shard_map/ppermute | solution.py:39
  51.7 14.3 %collective-permute-start.22 = (f32[32,4096]{1,0:T(8,128)S(1)}, f32[32,4096]{1,0:T(8,128)S(1)}, u32[]{:S(2)}, u32[]{:S(2)}) collective-permute-start(f32[32,4096]{1,0:T(8,128)S(1)} %add.52), channel_id=1, source_target_pairs={{0,64},{1,65},{2,66},{3,67},{4,68},{5,69},{6,70},{7,71},{64,0},{65... | collective-permute-start | bytes 1572872 | tf_op jit(solution)/shard_map/ppermute | solution.py:56
  63.6 2.4 %copy-start.1 = (f32[32,4096]{1,0:T(8,128)S(1)}, f32[32,4096]{1,0:T(8,128)}, u32[]{:S(2)}) copy-start(f32[32,4096]{1,0:T(8,128)} %outer_ref.1) | copy-start | bytes 1572868
  63.6 2.4 %copy-start.2 = (f32[32,4096]{1,0:T(8,128)S(1)}, f32[32,4096]{1,0:T(8,128)}, u32[]{:S(2)}) copy-start(f32[32,4096]{1,0:T(8,128)} %param.15) | copy-start | bytes 1572868
  63.8 8.1 %collective-permute-start.17 = (bf16[128,4096]{1,0:T(8,128)(2,1)S(1)}, bf16[128,4096]{1,0:T(8,128)(2,1)S(1)}, u32[]{:S(2)}, u32[]{:S(2)}) collective-permute-start(bf16[128,4096]{1,0:T(8,128)(2,1)S(1)} %slice.119), channel_id=1, source_target_pairs={{0,1},{1,0},{2,3},{3,2},{4,5},{5,4},{6,7},{7,6},{64,65},{65,64},{6... | collective-permute-start | bytes 3145736 | tf_op jit(solution)/shard_map/ppermute | solution.py:39
  67.2 10.8 %collective-permute-start.15 = (bf16[32,4096]{1,0:T(8,128)(2,1)S(1)}, bf16[32,4096]{1,0:T(8,128)(2,1)S(1)}, u32[]{:S(2)}, u32[]{:S(2)}) collective-permute-start(bf16[32,4096]{1,0:T(8,128)(2,1)S(1)} %get-tuple-element.28), channel_id=1, source_target_pairs={{0,4},{1,5},{2,6},{3,7},{4,0},{5,1},{6,2},{7,3},{64,68},{65,69},{6... | collective-permute-start | bytes 786440 | tf_op jit(solution)/shard_map/ppermute | solution.py:29
  69.5 12.8 %collective-permute-start.14 = (bf16[32,4096]{1,0:T(8,128)(2,1)S(1)}, bf16[32,4096]{1,0:T(8,128)(2,1)S(1)}, u32[]{:S(2)}, u32[]{:S(2)}) collective-permute-start(bf16[32,4096]{1,0:T(8,128)(2,1)S(1)} %get-tuple-element.29), channel_id=1, source_target_pairs={{0,6},{1,7},{2,0},{3,1},{4,2},{5,3},{6,4},{7,5},{64,70},{65,71},{6... | collective-permute-start | bytes 786440 | tf_op jit(solution)/shard_map/ppermute | solution.py:29
  71.8 10.5 %collective-permute-start.13 = (bf16[32,4096]{1,0:T(8,128)(2,1)S(1)}, bf16[32,4096]{1,0:T(8,128)(2,1)S(1)}, u32[]{:S(2)}, u32[]{:S(2)}) collective-permute-start(bf16[32,4096]{1,0:T(8,128)(2,1)S(1)} %get-tuple-element.27), channel_id=1, source_target_pairs={{0,2},{1,3},{2,4},{3,5},{4,6},{5,7},{6,0},{7,1},{64,66},{65,67},{6... | collective-permute-start | bytes 786440 | tf_op jit(solution)/shard_map/ppermute | solution.py:29
  72.2 14.7 %collective-permute-start.18 = (bf16[4,16,4096]{2,1,0:T(8,128)(2,1)S(1)}, bf16[4,16,4096]{2,1,0:T(8,128)(2,1)S(1)}, u32[]{:S(2)}, u32[]{:S(2)}) collective-permute-start(bf16[4,16,4096]{2,1,0:T(8,128)(2,1)S(1)} %fusion.5), channel_id=1, source_target_pairs={{0,72},{1,73},{2,74},{3,75},{4,76},{5,77},{6,78},{7,79},{64,8},{65... | collective-permute-start | bytes 1572872 | tf_op jit(solution)/shard_map/ppermute | solution.py:35
  82.5 7.7 %collective-permute-start.16 = (bf16[16,4096]{1,0:T(8,128)(2,1)S(1)}, bf16[16,4096]{1,0:T(8,128)(2,1)S(1)}, u32[]{:S(2)}, u32[]{:S(2)}) collective-permute-start(bf16[16,4096]{1,0:T(8,128)(2,1)S(1)} %slice.122), channel_id=1, source_target_pairs={{0,72},{1,73},{2,74},{3,75},{4,76},{5,77},{6,78},{7,79},{64,8},{65... | collective-permute-start | bytes 393224 | tf_op jit(solution)/shard_map/ppermute | solution.py:35
  87.0 6.7 %collective-permute-start.21 = (bf16[16,4096]{1,0:T(8,128)(2,1)S(1)}, bf16[16,4096]{1,0:T(8,128)(2,1)S(1)}, u32[]{:S(2)}, u32[]{:S(2)}) collective-permute-start(bf16[16,4096]{1,0:T(8,128)(2,1)S(1)} %get-tuple-element.31), channel_id=1, source_target_pairs={{0,4},{1,5},{2,6},{3,7},{4,0},{5,1},{6,2},{7,3},{64,68},{65,69},{6... | collective-permute-start | bytes 393224 | tf_op jit(solution)/shard_map/ppermute | solution.py:29
  87.8 6.7 %collective-permute-start.20 = (bf16[16,4096]{1,0:T(8,128)(2,1)S(1)}, bf16[16,4096]{1,0:T(8,128)(2,1)S(1)}, u32[]{:S(2)}, u32[]{:S(2)}) collective-permute-start(bf16[16,4096]{1,0:T(8,128)(2,1)S(1)} %get-tuple-element.32), channel_id=1, source_target_pairs={{0,6},{1,7},{2,0},{3,1},{4,2},{5,3},{6,4},{7,5},{64,70},{65,71},{6... | collective-permute-start | bytes 393224 | tf_op jit(solution)/shard_map/ppermute | solution.py:29
  90.0 6.2 %collective-permute-start.19 = (bf16[16,4096]{1,0:T(8,128)(2,1)S(1)}, bf16[16,4096]{1,0:T(8,128)(2,1)S(1)}, u32[]{:S(2)}, u32[]{:S(2)}) collective-permute-start(bf16[16,4096]{1,0:T(8,128)(2,1)S(1)} %get-tuple-element.30), channel_id=1, source_target_pairs={{0,2},{1,3},{2,4},{3,5},{4,6},{5,7},{6,0},{7,1},{64,66},{65,67},{6... | collective-permute-start | bytes 393224 | tf_op jit(solution)/shard_map/ppermute | solution.py:29
  (1 other events, 0.7 us)

commit v3 on v2

v3 whole, which is shorter than its diff:
```python
import jax
import jax.numpy as jnp
from jax import lax
from jax.experimental import pallas as pl
from jax.experimental.pallas import tpu as pltpu
from jax.sharding import PartitionSpec as P

outer_rate = 0.7
outer_beta = 0.9
AXES = ("replica", "tensor")
EXTENT_X, EXTENT_Y, EXTENT_Z = 4, 4, 4
BF16, F32 = jnp.bfloat16, jnp.float32
MIB = 2**20
LONG, SHORT = 6.0, 0.004
ANY = pl.BlockSpec(memory_space=pl.ANY)
VMEM = pl.BlockSpec(memory_space=pltpu.VMEM)


def position(x, y, z, core):
    return ((y % 2) * EXTENT_X + x) * 16 + (y // 2) * 8 + z * 2 + core


def pairs(move):
    return [
        (position(x, y, z, core), position(*move(x, y, z, core)))
        for x in range(EXTENT_X)
        for y in range(EXTENT_Y)
        for z in range(EXTENT_Z)
        for core in range(2)
    ]


def send(rows, move):
    return lax.ppermute(rows, AXES, pairs(move))


def send_z(rows, distance):
    return send(rows, lambda x, y, z, core: (x, y, (z + distance) % EXTENT_Z, core))


def swap_y(rows):
    return send(rows, lambda x, y, z, core: (x, 3 - y, z, core))


def swap_core(rows):
    return send(rows, lambda x, y, z, core: (x, y, z, 1 - core))


def swap_x(rows, first):
    def move(x, y, z, core):
        return (x ^ 1 if (core == 0) == first else 3 - x, y, z, core)

    return send(rows, move)


def swap_y_low(rows):
    return send(rows, lambda x, y, z, core: (x, y ^ 1, z, core))


def half(rows):
    return rows.astype(BF16)


def full(rows):
    return rows.astype(F32)


def times(left, right):
    return jnp.dot(left, right, preferred_element_type=F32)


def times_transpose(left, right):
    return lax.dot_general(left, right, (((1,), (1,)), ((), ())), preferred_element_type=F32)


def cost(gflop):
    return pl.CostEstimate(flops=int(gflop * 1e9), bytes_accessed=0, transcendentals=0)


def load_weights(*refs):
    count = len(refs) // 2
    copies = [
        pltpu.make_async_copy(refs[i], refs[count + i], refs[-1].at[i]) for i in range(count)
    ]
    for copy in copies:
        copy.start()
    for copy in copies:
        copy.wait()


def weights_in_vmem(*weights):
    count = len(weights)
    return pl.pallas_call(
        load_weights,
        out_shape=[pltpu.VMEM(weight.shape, weight.dtype) for weight in weights],
        in_specs=[ANY] * count,
        out_specs=[ANY] * count,
        scratch_shapes=[pltpu.SemaphoreType.DMA((count,))],
        compiler_params=pltpu.CompilerParams(vmem_limit_bytes=MIB),
        cost_estimate=cost(LONG),
    )(*[pltpu.with_memory_space_constraint(weight, pltpu.HBM) for weight in weights])


def hidden_kernel(near_ref, far_ref, gate_ref, up_ref, hidden_ref, gate_factor_ref, up_factor_ref):
    rows = jnp.concatenate([near_ref[...], far_ref[...]], 0)
    for low in range(0, gate_ref.shape[1], 128):
        units = slice(low, low + 128)
        both = times(rows, jnp.concatenate([gate_ref[:, units], up_ref[:, units]], 1))
        pre_gate, pre_up = both[:, :128], both[:, 128:]
        sig = jax.nn.sigmoid(pre_gate)
        hidden_ref[:, units] = half(pre_gate * sig * pre_up)
        gate_factor_ref[:, units] = pre_up * sig * (1.0 + pre_gate * (1.0 - sig))
        up_factor_ref[:, units] = pre_gate * sig


def output_kernel(hidden_ref, down_ref, here_ref, there_ref):
    hidden = hidden_ref[...]
    for low in range(0, down_ref.shape[1], 512):
        features = slice(low, low + 512)
        partial = times(hidden, down_ref[:, features])
        here_ref[:, features] = partial[:128]
        there_ref[:, features] = half(partial[128:])


def d_hidden_kernel(near_ref, far_ref, down_ref, gate_factor_ref, up_factor_ref, grads_ref):
    rows = jnp.concatenate([near_ref[...], far_ref[...]], 0)
    count = down_ref.shape[0]
    for low in range(0, count, 256):
        high = min(low + 256, count)
        d_hidden = times_transpose(rows, down_ref[low:high, :])
        grads_ref[:, low:high] = half(d_hidden * gate_factor_ref[:, low:high])
        grads_ref[:, count + low : count + high] = half(d_hidden * up_factor_ref[:, low:high])


def grad_kernel(grads_ref, gate_ref, up_ref, here_ref, there_ref):
    grads = grads_ref[...]
    for low in range(0, gate_ref.shape[0], 256):
        features = slice(low, low + 256)
        weight = jnp.concatenate([gate_ref[features, :], up_ref[features, :]], 1)
        partial = times_transpose(grads, weight)
        here_ref[:, features] = partial[:128]
        there_ref[:, features] = half(partial[128:])


def sum_for_y_kernel(here_ref, far_ref, keep_ref, sent_ref):
    for d in range(4):
        kept, other, to = 32 * d, 32 * d + 16, slice(16 * d, 16 * d + 16)
        keep_ref[to, :] = here_ref[kept : kept + 16, :] + full(far_ref[kept : kept + 16, :])
        sent_ref[to, :] = half(here_ref[other : other + 16, :] + full(far_ref[other : other + 16, :]))


def sum_for_z_kernel(here_ref, far_ref, keep_ref, *sent_refs):
    keep_ref[...] = here_ref[:32, :] + full(far_ref[:32, :])
    for d, sent_ref in enumerate(sent_refs, 1):
        rows = slice(32 * d, 32 * d + 32)
        sent_ref[...] = half(here_ref[rows, :] + full(far_ref[rows, :]))


def line_kernel(here_ref, there_ref, line_ref, *sent_refs):
    line_ref[...] = here_ref[:16, :] + full(there_ref[:16, :])
    for d, sent_ref in enumerate(sent_refs, 1):
        rows = slice(16 * d, 16 * d + 16)
        sent_ref[...] = half(here_ref[rows, :] + full(there_ref[rows, :]))


def add_kernel(left_ref, right_ref, sum_ref):
    sum_ref[...] = left_ref[...] + right_ref[...]


def on_core(kernel, gflop, outs, *args, needs=()):
    def body(*refs):
        kernel(*refs[: len(args)], *refs[len(args) + len(needs) :])

    return pl.pallas_call(
        body,
        out_shape=[jax.ShapeDtypeStruct(shape, dtype) for shape, dtype in outs],
        in_specs=[VMEM] * len(args) + [ANY] * len(needs),
        out_specs=[VMEM] * len(outs),
        compiler_params=pltpu.CompilerParams(vmem_limit_bytes=12 * MIB),
        cost_estimate=cost(gflop),
    )(*args, *needs)


def tie(*values):
    return lax.optimization_barrier(values)


def place_own(tokens_hbm, cotangent_hbm, both_ref, line_ref, sems):
    moves = ((tokens_hbm, both_ref), (cotangent_hbm, line_ref))
    copies = [
        pltpu.make_async_copy(a, b.at[pl.ds(0, a.shape[0])], sems.at[i])
        for i, (a, b) in enumerate(moves)
    ]
    for copy in copies:
        copy.start()
    for copy in copies:
        copy.wait()


def own_rows_in_vmem(tokens, cotangent):
    rows, width = tokens.shape
    return pl.pallas_call(
        place_own,
        out_shape=[pltpu.VMEM((2 * rows, width), BF16), pltpu.VMEM((4 * rows, width), BF16)],
        in_specs=[ANY] * 2,
        out_specs=[ANY] * 2,
        scratch_shapes=[pltpu.SemaphoreType.DMA((2,))],
        compiler_params=pltpu.CompilerParams(vmem_limit_bytes=MIB),
        cost_estimate=cost(1.0),
    )(*[pltpu.with_memory_space_constraint(own, pltpu.HBM) for own in (tokens, cotangent)])


def after(value, *others):
    return tie(value, *others)[0]


def put(block, rows, at):
    return lax.dynamic_update_slice(block, rows, (at, 0))


def on_device(tokens, cotangent, w_gate, w_up, w_down, outer_frag, local_frag, momentum):
    width, units = w_gate.shape
    both, line = own_rows_in_vmem(tokens, cotangent)
    both = put(both, swap_y(tokens), 16)
    line_arrived = [send_z(cotangent, -d) for d in (1, 2, 3)]
    token_arrived = [send_z(both, -d) for d in (1, 2, 3)]
    (gate,) = weights_in_vmem(after(w_gate, both))
    line_arrived = tie(*line_arrived, gate)[:3]
    for d in (1, 2, 3):
        line = put(line, line_arrived[d - 1], 16 * d)
    across = swap_y(line)
    local = after(local_frag[0], gate)
    local_next = swap_y_low(local)
    up, down = weights_in_vmem(after(w_up, line), w_down)
    token_arrived = tie(*token_arrived, up, local_next)[:3]
    pseudo = (outer_frag - full(local)) + (outer_frag - full(local_next))
    token_near = jnp.concatenate([both] + list(token_arrived), 0)
    token_far = swap_core(token_near)
    hidden, gate_factor, up_factor = on_core(
        hidden_kernel,
        SHORT,
        [((256, units), BF16), ((256, units), F32), ((256, units), F32)],
        token_near,
        token_far,
        gate,
        up,
        needs=(pseudo,),
    )
    cotangent_near = jnp.stack([line.reshape(4, 16, width), across.reshape(4, 16, width)], 1)
    cotangent_near = cotangent_near.reshape(128, width)
    cotangent_far = swap_core(cotangent_near)
    pseudo_next = swap_x(pseudo, True)
    (grads,) = on_core(
        d_hidden_kernel,
        SHORT,
        [((256, 2 * units), BF16)],
        cotangent_near,
        cotangent_far,
        down,
        gate_factor,
        up_factor,
    )
    (pseudo,) = on_core(
        add_kernel, SHORT, [(pseudo.shape, F32)], pseudo, pseudo_next, needs=(grads,)
    )
    grad_here, grad_there = on_core(
        grad_kernel,
        LONG,
        [((128, width), F32), ((128, width), BF16)],
        grads,
        gate,
        up,
        needs=(pseudo,),
    )
    grad_far = swap_core(grad_there)
    out_here, out_there = on_core(
        output_kernel,
        SHORT,
        [((128, width), F32), ((128, width), BF16)],
        hidden,
        down,
        needs=(grad_there,),
    )
    out_far = swap_core(out_there)
    grad_keep, grad_sent = on_core(
        sum_for_y_kernel,
        SHORT,
        [((64, width), F32), ((64, width), BF16)],
        grad_here,
        grad_far,
        needs=(out_there,),
    )
    grad_across = swap_y(grad_sent)
    pseudo_next = swap_x(after(pseudo, out_there), False)
    out_keep, *out_sent = on_core(
        sum_for_z_kernel,
        SHORT,
        [((32, width), F32)] + [((32, width), BF16)] * 3,
        out_here,
        out_far,
        needs=(grad_sent,),
    )
    out_arrived = [send_z(out_sent[d - 1], d) for d in (1, 2, 3)]
    grad_line, *grad_sent = on_core(
        line_kernel,
        LONG,
        [((16, width), F32)] + [((16, width), BF16)] * 3,
        grad_keep,
        grad_across,
        needs=(out_sent[0],),
    )
    out_arrived = tie(*out_arrived, grad_sent[0])[:3]
    out_both = out_keep + full(out_arrived[0]) + full(out_arrived[1]) + full(out_arrived[2])
    out_sent = half(out_both[16:])
    layer_output = out_both[:16] + full(swap_y(out_sent))
    grad_arrived = [send_z(grad_sent[d - 1], d) for d in (1, 2, 3)]
    input_grad = (
        grad_line + full(grad_arrived[0]) + full(grad_arrived[1]) + full(grad_arrived[2])
    )
    (pseudo,) = on_core(
        add_kernel, SHORT, [(pseudo.shape, F32)], pseudo, pseudo_next, needs=(grad_line,)
    )
    mean_delta = pseudo / lax.axis_size("replica")
    new_momentum = outer_beta * momentum + mean_delta
    new_outer = outer_frag - outer_rate * (mean_delta + outer_beta * new_momentum)
    return (layer_output, input_grad, new_outer, new_momentum)


def solution(mesh):
    in_specs = (
        P(AXES, None),
        P(AXES, None),
        P(None, "tensor"),
        P(None, "tensor"),
        P("tensor", None),
        P("tensor", None),
        P("replica", "tensor", None),
        P("tensor", None),
    )
    out_specs = (P(AXES, None), P(AXES, None), P("tensor", None), P("tensor", None))
    return jax.shard_map(
        on_device, mesh=mesh, in_specs=in_specs, out_specs=out_specs, check_vma=False
    )
```

time: 97.2 us -> 79.8 us (0.82)
  matrix products: 21.9 us -> 0 us
  Pallas kernels: 2.07 us -> 22.5 us
  waiting for transfers between devices: 34.2 us -> 24.4 us
  other arithmetic: 5.48 us -> 2.97 us
  local copies, waits for them, and re-layouts: 2.09 us -> 0.07 us
  starting transfers between devices: 30.4 us -> 28.7 us
    dot_general x6 -> x0, matrix products: 21.9 us -> none  [the longest x3 11.5 us: times_transpose(): lax.dot_general(left_rows, weight, (((1,), (1,)), ((), ())), preferred_el...]
    pallas_call x1 -> x12, Pallas kernels: 2.07 us -> 22.5 us  [the longest x9 13.2 us: on_core(): pl.pallas_call(body, out_shape=[jax.ShapeDtypeStruct(shape, dtype) for sh...]
    ppermute x23, waiting for transfers between devices: 34.2 us -> 24.4 us  [send(): return lax.ppermute(rows, AXES, pairs(move))]
    concatenate x3 -> x1, other arithmetic: 1.95 us -> 0.09 us  [on_device(): token_near = jnp.concatenate([both] + list(token_arrived), 0)]
    ppermute x23, starting transfers between devices: 30.4 us -> 28.7 us  [send(): return lax.ppermute(rows, AXES, pairs(move))]
    unnamed x24 -> x6, local copies, waits for them, and re-layouts: 1.54 us -> 0.02 us
    add x6 -> x4, other arithmetic: 2.18 us -> 1.68 us  [the longest x1 0.76 us: on_device(): grad_line + full(grad_arrived[0]) + full(grad_arrived[1])]
  transfers between devices with their start and end apart: 23 -> 23, of which waited for: 16 -> 11; matrix products, arithmetic and copies ran while one was open for 23% -> 3% of each run, Pallas kernels for 0% -> 23%
where the time goes in v3:
time: 79.8 us; the launch traced here: 79.5 us
  starting transfers between devices  28.7 us (36%)
  waiting for transfers between devices  24.4 us (31%)
  Pallas kernels  22.5 us (28%)
  other arithmetic  2.97 us (4%)
  between operations  0.89 us (1%)
    ppermute x23, starting transfers between devices, send(): return lax.ppermute(rows, AXES, pairs(move))  28.7 us
    ppermute x23, waiting for transfers between devices, send(): return lax.ppermute(rows, AXES, pairs(move))  24.4 us
    pallas_call x9, Pallas kernels, on_core(): pl.pallas_call(body, out_shape=[jax.ShapeDtypeStruct(shape, dtype) for sh...  13.2 us
    pallas_call x2, Pallas kernels, weights_in_vmem(): pl.pallas_call(load_weights, out_shape=[pltpu.VMEM(weight.shape, weight.d...  8.3 us
  transfers between devices with their start and end apart: 23, of which 11 were waited for; matrix products, arithmetic and copies ran while one was open for 3% of the time, Pallas kernels for 23%

profile of v3, /device:TPU:0, one launch (start us, length us, event | category | flops | bytes accessed | tf_op | source)
XLA Modules:
  0.0 79.5 jit_solution(5795248872361818435)
XLA Ops:
  0.6 3.2 %collective-permute-start = (bf16[16,4096]{1,0:T(8,128)(2,1)}, bf16[16,4096]{1,0:T(8,128)(2,1)S(1)}, u32[]{:S(2)}, u32[]{:S(2)}) collective-permute-start(bf16[16,4096]{1,0:T(8,128)(2,1)} %tokens_hbm.1), channel_id=1, source_target_pairs={{0,72},{1,73},{2,74},{3,75},{4,76},{5,77},{6,78},{7,79},{64,8},{65... | collective-permute-start | bytes 393224 | tf_op jit(solution)/shard_map/ppermute | solution.py:34
  3.8 4.0 %collective-permute-start.4 = (bf16[16,4096]{1,0:T(8,128)(2,1)}, bf16[16,4096]{1,0:T(8,128)(2,1)S(1)}, u32[]{:S(2)}, u32[]{:S(2)}) collective-permute-start(bf16[16,4096]{1,0:T(8,128)(2,1)} %cotangent_hbm.1), channel_id=1, source_target_pairs={{0,6},{1,7},{2,0},{3,1},{4,2},{5,3},{6,4},{7,5},{64,70},{65,71},{6... | collective-permute-start | bytes 393224 | tf_op jit(solution)/shard_map/ppermute | solution.py:34
  7.8 1.3 %collective-permute-start.6 = (bf16[16,4096]{1,0:T(8,128)(2,1)}, bf16[16,4096]{1,0:T(8,128)(2,1)S(1)}, u32[]{:S(2)}, u32[]{:S(2)}) collective-permute-start(bf16[16,4096]{1,0:T(8,128)(2,1)} %cotangent_hbm.1), channel_id=1, source_target_pairs={{0,2},{1,3},{2,4},{3,5},{4,6},{5,7},{6,0},{7,1},{64,66},{65,67},{6... | collective-permute-start | bytes 393224 | tf_op jit(solution)/shard_map/ppermute | solution.py:34
  9.1 1.0 %shard_map.111 = (bf16[32,4096]{1,0:T(8,128)(2,1)S(1)}, bf16[64,4096]{1,0:T(8,128)(2,1)S(1)}) custom-call(bf16[16,4096]{1,0:T(8,128)(2,1)} %tokens_hbm.1, bf16[16,4096]{1,0:T(8,128)(2,1)} %cotangent_hbm.1), custom_call_target="tpu_custom_call" | custom-call | flops 1000000000 | tf_op jit(solution)/shard_map/pallas_call | solution.py:202
  10.1 2.0 %collective-permute-start.1 = (bf16[32,4096]{1,0:T(8,128)(2,1)S(1)}, bf16[32,4096]{1,0:T(8,128)(2,1)S(1)}, u32[]{:S(2)}, u32[]{:S(2)}) collective-permute-start(bf16[32,4096]{1,0:T(8,128)(2,1)S(1)} %constant_dynamic-update-slice_fusion.3), channel_id=1, source_target_pairs={{0,6},{1,7},{2,0},{3,1},{4,2},{5,3},{6,4},{7,5},{64,70},{65,71},{6... | collective-permute-start | bytes 786440 | tf_op jit(solution)/shard_map/ppermute | solution.py:34
  12.2 2.3 %collective-permute-start.2 = (bf16[32,4096]{1,0:T(8,128)(2,1)S(1)}, bf16[32,4096]{1,0:T(8,128)(2,1)S(1)}, u32[]{:S(2)}, u32[]{:S(2)}) collective-permute-start(bf16[32,4096]{1,0:T(8,128)(2,1)S(1)} %constant_dynamic-update-slice_fusion.3), channel_id=1, source_target_pairs={{0,4},{1,5},{2,6},{3,7},{4,0},{5,1},{6,2},{7,3},{64,68},{65,69},{6... | collective-permute-start | bytes 786440 | tf_op jit(solution)/shard_map/ppermute | solution.py:34
  14.5 3.1 %shard_map.112.refs_2_.refs_1_ = bf16[4096,896]{1,0:T(8,128)(2,1)S(1)} custom-call(bf16[4096,896]{1,0:T(8,128)(2,1)} %refs_0_), custom_call_target="tpu_custom_call" | custom-call | flops 6000000000 | tf_op jit(solution)/shard_map/pallas_call | solution.py:93
  18.2 1.0 %collective-permute-start.9 = (bf16[64,4096]{1,0:T(8,128)(2,1)S(1)}, bf16[64,4096]{1,0:T(8,128)(2,1)S(1)}, u32[]{:S(2)}, u32[]{:S(2)}) collective-permute-start(bf16[64,4096]{1,0:T(8,128)(2,1)S(1)} %constant_dynamic-update-slice_fusion), channel_id=1, source_target_pairs={{0,72},{1,73},{2,74},{3,75},{4,76},{5,77},{6,78},{7,79},{64,8},{65... | collective-permute-start | bytes 1572872 | tf_op jit(solution)/shard_map/ppermute | solution.py:34
  19.2 5.2 %shard_map.113 = (bf16[4096,896]{1,0:T(8,128)(2,1)S(1)}, bf16[896,4096]{1,0:T(8,128)(2,1)S(1)}) custom-call(bf16[4096,896]{1,0:T(8,128)(2,1)} %refs_0_.1, bf16[896,4096]{1,0:T(8,128)(2,1)} %refs_1_.1), custom_call_target="tpu_custom_call" | custom-call | flops 6000000000 | tf_op jit(solution)/shard_map/pallas_call | solution.py:93
  24.6 3.7 %collective-permute-done.3 = bf16[32,4096]{1,0:T(8,128)(2,1)S(1)} collective-permute-done((bf16[32,4096]{1,0:T(8,128)(2,1)S(1)}, bf16[32,4096]{1,0:T(8,128)(2,1)S(1)}, u32[]{:S(2)}, u32[]{:S(2)}) %collective-permute-start.3) | collective-permute-done | bytes 262176 | tf_op jit(solution)/shard_map/ppermute | solution.py:34
  28.5 4.0 %collective-permute-done.9 = bf16[64,4096]{1,0:T(8,128)(2,1)S(1)} collective-permute-done((bf16[64,4096]{1,0:T(8,128)(2,1)S(1)}, bf16[64,4096]{1,0:T(8,128)(2,1)S(1)}, u32[]{:S(2)}, u32[]{:S(2)}) %collective-permute-start.9) | collective-permute-done | bytes 524320 | tf_op jit(solution)/shard_map/ppermute | solution.py:34
  32.8 1.8 %collective-permute-start.11 = (f32[32,4096]{1,0:T(8,128)S(1)}, f32[32,4096]{1,0:T(8,128)S(1)}, u32[]{:S(2)}, u32[]{:S(2)}) collective-permute-start(f32[32,4096]{1,0:T(8,128)S(1)} %subtract_add_fusion.refs_4_.refs_0_), channel_id=1, source_target_pairs={{0,16},{1,49},{2,18},{3,51},{4,20},{5,53},{6,22},{7,55},{64,80},{6... | collective-permute-start | bytes 1572872 | tf_op jit(solution)/shard_map/ppermute | solution.py:34
  34.6 4.0 %shard_map.114 = (bf16[256,896]{1,0:T(8,128)(2,1)S(1)}, f32[256,896]{1,0:T(8,128)S(1)}, f32[256,896]{1,0:T(8,128)S(1)}) custom-call(bf16[128,4096]{1,0:T(8,128)(2,1)S(1)} %pad_maximum_fusion.refs_0_, bf16[128,4096]{1,0:T(8,128)(2,1)S(1)} %collective-permute-done.8.refs_1_, bf16[4096,896]{1,0:T(8,128)(2,1)S(1)} %shard_map.112.refs_2_.refs_1_, ...), custom_call_target="tpu_custom_call" | custom-call | flops 4000000 | tf_op jit(solution)/shard_map/pallas_call | solution.py:174
  38.6 2.4 %shard_map.115.refs_2_.refs_0_ = bf16[256,1792]{1,0:T(8,128)(2,1)S(1)} custom-call(bf16[128,4096]{1,0:T(8,128)(2,1)S(1)} %bitcast.9, bf16[128,4096]{1,0:T(8,128)(2,1)S(1)} %collective-permute-done.10.refs_1_, bf16[896,4096]{1,0:T(8,128)(2,1)S(1)} %get-tuple-element.51.refs_2_.refs_1_, f32[256,896]{1,0:T(8,128)S(1)} %get-tuple-element.52.refs_3_, ...), custom_call_target="tpu_custom_call" | custom-call | flops 4000000 | tf_op jit(solution)/shard_map/pallas_call | solution.py:174
  40.9 1.3 %collective-permute-done.11.refs_1_ = f32[32,4096]{1,0:T(8,128)S(1)} collective-permute-done((f32[32,4096]{1,0:T(8,128)S(1)}, f32[32,4096]{1,0:T(8,128)S(1)}, u32[]{:S(2)}, u32[]{:S(2)}) %collective-permute-start.11) | collective-permute-done | bytes 524320 | tf_op jit(solution)/shard_map/ppermute | solution.py:34
  42.3 4.0 %shard_map.117 = (f32[128,4096]{1,0:T(8,128)S(1)}, bf16[128,4096]{1,0:T(8,128)(2,1)S(1)}) custom-call(bf16[256,1792]{1,0:T(8,128)(2,1)S(1)} %shard_map.115.refs_2_.refs_0_, bf16[4096,896]{1,0:T(8,128)(2,1)S(1)} %shard_map.112.refs_2_.refs_1_, bf16[4096,896]{1,0:T(8,128)(2,1)S(1)} %get-tuple-element.45.refs_3_.refs_2_, f32[32,4096]{1,0:T(8,128)S(1)} %shard_map.116.refs_3_.refs_0_), custom_call_target="tpu_custom_call" | custom-call | flops 6000000000 | tf_op jit(solution)/shard_map/pallas_call | solution.py:174
  46.3 0.6 collective-permute-start.13
  46.9 2.3 %shard_map.118 = (f32[128,4096]{1,0:T(8,128)S(1)}, bf16[128,4096]{1,0:T(8,128)(2,1)S(1)}) custom-call(bf16[256,896]{1,0:T(8,128)(2,1)S(1)} %get-tuple-element.50.refs_0_, bf16[896,4096]{1,0:T(8,128)(2,1)S(1)} %get-tuple-element.51.refs_2_.refs_1_, bf16[128,4096]{1,0:T(8,128)(2,1)S(1)} %get-tuple-element.54.refs_2_), custom_call_target="tpu_custom_call" | custom-call | flops 4000000 | tf_op jit(solution)/shard_map/pallas_call | solution.py:174
  49.9 2.7 %collective-permute-start.22 = (f32[32,4096]{1,0:T(8,128)S(1)}, f32[32,4096]{1,0:T(8,128)S(1)}, u32[]{:S(2)}, u32[]{:S(2)}) collective-permute-start(f32[32,4096]{1,0:T(8,128)S(1)} %shard_map.116.refs_3_.refs_0_), channel_id=1, source_target_pairs={{0,48},{1,17},{2,50},{3,19},{4,52},{5,21},{6,54},{7,23},{64,112},{... | collective-permute-start | bytes 1572872 | tf_op jit(solution)/shard_map/ppermute | solution.py:34
  52.8 1.9 %collective-permute-start.14 = (bf16[32,4096]{1,0:T(8,128)(2,1)S(1)}, bf16[32,4096]{1,0:T(8,128)(2,1)S(1)}, u32[]{:S(2)}, u32[]{:S(2)}) collective-permute-start(bf16[32,4096]{1,0:T(8,128)(2,1)S(1)} %get-tuple-element.60.refs_2_), channel_id=1, source_target_pairs={{0,2},{1,3},{2,4},{3,5},{4,6},{5,7},{6,0},{7,1},{64,66},{65,67},{6... | collective-permute-start | bytes 786440 | tf_op jit(solution)/shard_map/ppermute | solution.py:34
  54.7 1.5 %collective-permute-start.15 = (bf16[32,4096]{1,0:T(8,128)(2,1)S(1)}, bf16[32,4096]{1,0:T(8,128)(2,1)S(1)}, u32[]{:S(2)}, u32[]{:S(2)}) collective-permute-start(bf16[32,4096]{1,0:T(8,128)(2,1)S(1)} %get-tuple-element.61), channel_id=1, source_target_pairs={{0,4},{1,5},{2,6},{3,7},{4,0},{5,1},{6,2},{7,3},{64,68},{65,69},{6... | collective-permute-start | bytes 786440 | tf_op jit(solution)/shard_map/ppermute | solution.py:34
  56.2 1.5 %collective-permute-start.16 = (bf16[32,4096]{1,0:T(8,128)(2,1)S(1)}, bf16[32,4096]{1,0:T(8,128)(2,1)S(1)}, u32[]{:S(2)}, u32[]{:S(2)}) collective-permute-start(bf16[32,4096]{1,0:T(8,128)(2,1)S(1)} %get-tuple-element.62), channel_id=1, source_target_pairs={{0,6},{1,7},{2,0},{3,1},{4,2},{5,3},{6,4},{7,5},{64,70},{65,71},{6... | collective-permute-start | bytes 786440 | tf_op jit(solution)/shard_map/ppermute | solution.py:34
  57.7 7.4 %collective-permute-done.17.refs_1_ = bf16[64,4096]{1,0:T(8,128)(2,1)S(1)} collective-permute-done((bf16[64,4096]{1,0:T(8,128)(2,1)S(1)}, bf16[64,4096]{1,0:T(8,128)(2,1)S(1)}, u32[]{:S(2)}, u32[]{:S(2)}) %collective-permute-start.17) | collective-permute-done | bytes 524320 | tf_op jit(solution)/shard_map/ppermute | solution.py:34
  65.3 2.1 %collective-permute-done.14 = bf16[32,4096]{1,0:T(8,128)(2,1)S(1)} collective-permute-done((bf16[32,4096]{1,0:T(8,128)(2,1)S(1)}, bf16[32,4096]{1,0:T(8,128)(2,1)S(1)}, u32[]{:S(2)}, u32[]{:S(2)}) %collective-permute-start.14) | collective-permute-done | bytes 262176 | tf_op jit(solution)/shard_map/ppermute | solution.py:34
  68.2 1.7 %collective-permute-start.18 = (bf16[16,4096]{1,0:T(8,128)(2,1)S(1)}, bf16[16,4096]{1,0:T(8,128)(2,1)S(1)}, u32[]{:S(2)}, u32[]{:S(2)}) collective-permute-start(bf16[16,4096]{1,0:T(8,128)(2,1)S(1)} %slice.13), channel_id=1, source_target_pairs={{0,72},{1,73},{2,74},{3,75},{4,76},{5,77},{6,78},{7,79},{64,8},{65... | collective-permute-start | bytes 393224 | tf_op jit(solution)/shard_map/ppermute | solution.py:34
  69.9 2.3 %collective-permute-start.21 = (bf16[16,4096]{1,0:T(8,128)(2,1)S(1)}, bf16[16,4096]{1,0:T(8,128)(2,1)S(1)}, u32[]{:S(2)}, u32[]{:S(2)}) collective-permute-start(bf16[16,4096]{1,0:T(8,128)(2,1)S(1)} %get-tuple-element.70), channel_id=1, source_target_pairs={{0,6},{1,7},{2,0},{3,1},{4,2},{5,3},{6,4},{7,5},{64,70},{65,71},{6... | collective-permute-start | bytes 393224 | tf_op jit(solution)/shard_map/ppermute | solution.py:34
  72.3 1.1 %multiply_subtract_fusion = (f32[32,4096]{1,0:T(8,128)}, f32[32,4096]{1,0:T(8,128)}) fusion(f32[32,4096]{1,0:T(8,128)S(1)} %copy-done, f32[32,4096]{1,0:T(8,128)S(1)} %shard_map.122, f32[32,4096]{1,0:T(8,128)S(1)} %copy-done.1), kind=kLoop, calls=%fused_computation.2 | loop fusion | flops 917504 | bytes 2621440 | tf_op jit(solution)/shard_map/sub | solution.py:325
  73.4 1.0 %collective-permute-done.18 = bf16[16,4096]{1,0:T(8,128)(2,1)S(1)} collective-permute-done((bf16[16,4096]{1,0:T(8,128)(2,1)S(1)}, bf16[16,4096]{1,0:T(8,128)(2,1)S(1)}, u32[]{:S(2)}, u32[]{:S(2)}) %collective-permute-start.18) | collective-permute-done | bytes 131104 | tf_op jit(solution)/shard_map/ppermute | solution.py:34
  74.4 0.7 slice_add_fusion
  75.2 2.2 %collective-permute-done.21 = bf16[16,4096]{1,0:T(8,128)(2,1)S(1)} collective-permute-done((bf16[16,4096]{1,0:T(8,128)(2,1)S(1)}, bf16[16,4096]{1,0:T(8,128)(2,1)S(1)}, u32[]{:S(2)}, u32[]{:S(2)}) %collective-permute-start.21) | collective-permute-done | bytes 131104 | tf_op jit(solution)/shard_map/ppermute | solution.py:34
  77.4 1.3 %collective-permute-done.20 = bf16[16,4096]{1,0:T(8,128)(2,1)S(1)} collective-permute-done((bf16[16,4096]{1,0:T(8,128)(2,1)S(1)}, bf16[16,4096]{1,0:T(8,128)(2,1)S(1)}, u32[]{:S(2)}, u32[]{:S(2)}) %collective-permute-start.20) | collective-permute-done | bytes 131104 | tf_op jit(solution)/shard_map/ppermute | solution.py:34
  78.7 0.8 convert_add_fusion.1
  (44 shorter events, 3.0 us)
Async XLA Ops:
  0.6 9.5 %collective-permute-start = (bf16[16,4096]{1,0:T(8,128)(2,1)}, bf16[16,4096]{1,0:T(8,128)(2,1)S(1)}, u32[]{:S(2)}, u32[]{:S(2)}) collective-permute-start(bf16[16,4096]{1,0:T(8,128)(2,1)} %tokens_hbm.1), channel_id=1, source_target_pairs={{0,72},{1,73},{2,74},{3,75},{4,76},{5,77},{6,78},{7,79},{64,8},{65... | collective-permute-start | bytes 393224 | tf_op jit(solution)/shard_map/ppermute | solution.py:34
  3.8 13.8 %collective-permute-start.4 = (bf16[16,4096]{1,0:T(8,128)(2,1)}, bf16[16,4096]{1,0:T(8,128)(2,1)S(1)}, u32[]{:S(2)}, u32[]{:S(2)}) collective-permute-start(bf16[16,4096]{1,0:T(8,128)(2,1)} %cotangent_hbm.1), channel_id=1, source_target_pairs={{0,6},{1,7},{2,0},{3,1},{4,2},{5,3},{6,4},{7,5},{64,70},{65,71},{6... | collective-permute-start | bytes 393224 | tf_op jit(solution)/shard_map/ppermute | solution.py:34
  7.8 9.9 %collective-permute-start.5 = (bf16[16,4096]{1,0:T(8,128)(2,1)}, bf16[16,4096]{1,0:T(8,128)(2,1)S(1)}, u32[]{:S(2)}, u32[]{:S(2)}) collective-permute-start(bf16[16,4096]{1,0:T(8,128)(2,1)} %cotangent_hbm.1), channel_id=1, source_target_pairs={{0,4},{1,5},{2,6},{3,7},{4,0},{5,1},{6,2},{7,3},{64,68},{65,69},{6... | collective-permute-start | bytes 393224 | tf_op jit(solution)/shard_map/ppermute | solution.py:34
  7.8 10.3 %collective-permute-start.6 = (bf16[16,4096]{1,0:T(8,128)(2,1)}, bf16[16,4096]{1,0:T(8,128)(2,1)S(1)}, u32[]{:S(2)}, u32[]{:S(2)}) collective-permute-start(bf16[16,4096]{1,0:T(8,128)(2,1)} %cotangent_hbm.1), channel_id=1, source_target_pairs={{0,2},{1,3},{2,4},{3,5},{4,6},{5,7},{6,0},{7,1},{64,66},{65,67},{6... | collective-permute-start | bytes 393224 | tf_op jit(solution)/shard_map/ppermute | solution.py:34
  10.1 9.1 %copy-start.2 = (bf16[1,32,4096]{2,1,0:T(8,128)(2,1)S(1)}, bf16[1,32,4096]{2,1,0:T(8,128)(2,1)}, u32[]{:S(2)}) copy-start(bf16[1,32,4096]{2,1,0:T(8,128)(2,1)} %param.14) | copy-start | bytes 786436
  10.1 14.4 %collective-permute-start.1 = (bf16[32,4096]{1,0:T(8,128)(2,1)S(1)}, bf16[32,4096]{1,0:T(8,128)(2,1)S(1)}, u32[]{:S(2)}, u32[]{:S(2)}) collective-permute-start(bf16[32,4096]{1,0:T(8,128)(2,1)S(1)} %constant_dynamic-update-slice_fusion.3), channel_id=1, source_target_pairs={{0,6},{1,7},{2,0},{3,1},{4,2},{5,3},{6,4},{7,5},{64,70},{65,71},{6... | collective-permute-start | bytes 786440 | tf_op jit(solution)/shard_map/ppermute | solution.py:34
  12.2 12.4 %collective-permute-start.2 = (bf16[32,4096]{1,0:T(8,128)(2,1)S(1)}, bf16[32,4096]{1,0:T(8,128)(2,1)S(1)}, u32[]{:S(2)}, u32[]{:S(2)}) collective-permute-start(bf16[32,4096]{1,0:T(8,128)(2,1)S(1)} %constant_dynamic-update-slice_fusion.3), channel_id=1, source_target_pairs={{0,4},{1,5},{2,6},{3,7},{4,0},{5,1},{6,2},{7,3},{64,68},{65,69},{6... | collective-permute-start | bytes 786440 | tf_op jit(solution)/shard_map/ppermute | solution.py:34
  17.6 10.7 %collective-permute-start.3 = (bf16[32,4096]{1,0:T(8,128)(2,1)S(1)}, bf16[32,4096]{1,0:T(8,128)(2,1)S(1)}, u32[]{:S(2)}, u32[]{:S(2)}) collective-permute-start(bf16[32,4096]{1,0:T(8,128)(2,1)S(1)} %constant_dynamic-update-slice_fusion.3), channel_id=1, source_target_pairs={{0,2},{1,3},{2,4},{3,5},{4,6},{5,7},{6,0},{7,1},{64,66},{65,67},{6... | collective-permute-start | bytes 786440 | tf_op jit(solution)/shard_map/ppermute | solution.py:34
  18.2 14.3 %collective-permute-start.9 = (bf16[64,4096]{1,0:T(8,128)(2,1)S(1)}, bf16[64,4096]{1,0:T(8,128)(2,1)S(1)}, u32[]{:S(2)}, u32[]{:S(2)}) collective-permute-start(bf16[64,4096]{1,0:T(8,128)(2,1)S(1)} %constant_dynamic-update-slice_fusion), channel_id=1, source_target_pairs={{0,72},{1,73},{2,74},{3,75},{4,76},{5,77},{6,78},{7,79},{64,8},{65... | collective-permute-start | bytes 1572872 | tf_op jit(solution)/shard_map/ppermute | solution.py:34
  19.2 9.1 %collective-permute-start.7 = (bf16[32,4096]{1,0:T(8,128)(2,1)S(1)}, bf16[32,4096]{1,0:T(8,128)(2,1)S(1)}, u32[]{:S(2)}, u32[]{:S(2)}) collective-permute-start(bf16[32,4096]{1,0:T(8,128)(2,1)S(1)} %bitcast.12), channel_id=1, source_target_pairs={{0,64},{1,65},{2,66},{3,67},{4,68},{5,69},{6,70},{7,71},{64,0},{65... | collective-permute-start | bytes 786440 | tf_op jit(solution)/shard_map/ppermute | solution.py:34
  28.3 4.4 %copy-start = (f32[32,4096]{1,0:T(8,128)S(1)}, f32[32,4096]{1,0:T(8,128)}, u32[]{:S(2)}) copy-start(f32[32,4096]{1,0:T(8,128)} %param.13) | copy-start | bytes 1572868
  28.4 6.1 %collective-permute-start.8 = (bf16[128,4096]{1,0:T(8,128)(2,1)S(1)}, bf16[128,4096]{1,0:T(8,128)(2,1)S(1)}, u32[]{:S(2)}, u32[]{:S(2)}) collective-permute-start(bf16[128,4096]{1,0:T(8,128)(2,1)S(1)} %pad_maximum_fusion.refs_0_), channel_id=1, source_target_pairs={{0,1},{1,0},{2,3},{3,2},{4,5},{5,4},{6,7},{7,6},{64,65},{65,64},{6... | collective-permute-start | bytes 3145736 | tf_op jit(solution)/shard_map/ppermute | solution.py:34
  32.6 6.0 %collective-permute-start.10 = (bf16[128,4096]{1,0:T(8,128)(2,1)S(1)}, bf16[128,4096]{1,0:T(8,128)(2,1)S(1)}, u32[]{:S(2)}, u32[]{:S(2)}) collective-permute-start(bf16[128,4096]{1,0:T(8,128)(2,1)S(1)} %bitcast.8), channel_id=1, source_target_pairs={{0,1},{1,0},{2,3},{3,2},{4,5},{5,4},{6,7},{7,6},{64,65},{65,64},{6... | collective-permute-start | bytes 3145736 | tf_op jit(solution)/shard_map/ppermute | solution.py:34
  32.8 9.4 %collective-permute-start.11 = (f32[32,4096]{1,0:T(8,128)S(1)}, f32[32,4096]{1,0:T(8,128)S(1)}, u32[]{:S(2)}, u32[]{:S(2)}) collective-permute-start(f32[32,4096]{1,0:T(8,128)S(1)} %subtract_add_fusion.refs_4_.refs_0_), channel_id=1, source_target_pairs={{0,16},{1,49},{2,18},{3,51},{4,20},{5,53},{6,22},{7,55},{64,80},{6... | collective-permute-start | bytes 1572872 | tf_op jit(solution)/shard_map/ppermute | solution.py:34
  46.3 3.1 %collective-permute-start.13 = (bf16[128,4096]{1,0:T(8,128)(2,1)S(1)}, bf16[128,4096]{1,0:T(8,128)(2,1)S(1)}, u32[]{:S(2)}, u32[]{:S(2)}) collective-permute-start(bf16[128,4096]{1,0:T(8,128)(2,1)S(1)} %get-tuple-element.54.refs_2_), channel_id=1, source_target_pairs={{0,1},{1,0},{2,3},{3,2},{4,5},{5,4},{6,7},{7,6},{64,65},{65,64},{6... | collective-permute-start | bytes 3145736 | tf_op jit(solution)/shard_map/ppermute | solution.py:34
  49.3 3.4 %collective-permute-start.12 = (bf16[128,4096]{1,0:T(8,128)(2,1)S(1)}, bf16[128,4096]{1,0:T(8,128)(2,1)S(1)}, u32[]{:S(2)}, u32[]{:S(2)}) collective-permute-start(bf16[128,4096]{1,0:T(8,128)(2,1)S(1)} %get-tuple-element.56.refs_2_), channel_id=1, source_target_pairs={{0,1},{1,0},{2,3},{3,2},{4,5},{5,4},{6,7},{7,6},{64,65},{65,64},{6... | collective-permute-start | bytes 3145736 | tf_op jit(solution)/shard_map/ppermute | solution.py:34
  49.5 15.6 %collective-permute-start.17 = (bf16[64,4096]{1,0:T(8,128)(2,1)S(1)}, bf16[64,4096]{1,0:T(8,128)(2,1)S(1)}, u32[]{:S(2)}, u32[]{:S(2)}) collective-permute-start(bf16[64,4096]{1,0:T(8,128)(2,1)S(1)} %get-tuple-element.58.refs_2_), channel_id=1, source_target_pairs={{0,72},{1,73},{2,74},{3,75},{4,76},{5,77},{6,78},{7,79},{64,8},{65... | collective-permute-start | bytes 1572872 | tf_op jit(solution)/shard_map/ppermute | solution.py:34
  49.9 22.3 %collective-permute-start.22 = (f32[32,4096]{1,0:T(8,128)S(1)}, f32[32,4096]{1,0:T(8,128)S(1)}, u32[]{:S(2)}, u32[]{:S(2)}) collective-permute-start(f32[32,4096]{1,0:T(8,128)S(1)} %shard_map.116.refs_3_.refs_0_), channel_id=1, source_target_pairs={{0,48},{1,17},{2,50},{3,19},{4,52},{5,21},{6,54},{7,23},{64,112},{... | collective-permute-start | bytes 1572872 | tf_op jit(solution)/shard_map/ppermute | solution.py:34
  52.8 14.6 %collective-permute-start.14 = (bf16[32,4096]{1,0:T(8,128)(2,1)S(1)}, bf16[32,4096]{1,0:T(8,128)(2,1)S(1)}, u32[]{:S(2)}, u32[]{:S(2)}) collective-permute-start(bf16[32,4096]{1,0:T(8,128)(2,1)S(1)} %get-tuple-element.60.refs_2_), channel_id=1, source_target_pairs={{0,2},{1,3},{2,4},{3,5},{4,6},{5,7},{6,0},{7,1},{64,66},{65,67},{6... | collective-permute-start | bytes 786440 | tf_op jit(solution)/shard_map/ppermute | solution.py:34
  54.7 12.7 %collective-permute-start.15 = (bf16[32,4096]{1,0:T(8,128)(2,1)S(1)}, bf16[32,4096]{1,0:T(8,128)(2,1)S(1)}, u32[]{:S(2)}, u32[]{:S(2)}) collective-permute-start(bf16[32,4096]{1,0:T(8,128)(2,1)S(1)} %get-tuple-element.61), channel_id=1, source_target_pairs={{0,4},{1,5},{2,6},{3,7},{4,0},{5,1},{6,2},{7,3},{64,68},{65,69},{6... | collective-permute-start | bytes 786440 | tf_op jit(solution)/shard_map/ppermute | solution.py:34
  56.2 11.8 %collective-permute-start.16 = (bf16[32,4096]{1,0:T(8,128)(2,1)S(1)}, bf16[32,4096]{1,0:T(8,128)(2,1)S(1)}, u32[]{:S(2)}, u32[]{:S(2)}) collective-permute-start(bf16[32,4096]{1,0:T(8,128)(2,1)S(1)} %get-tuple-element.62), channel_id=1, source_target_pairs={{0,6},{1,7},{2,0},{3,1},{4,2},{5,3},{6,4},{7,5},{64,70},{65,71},{6... | collective-permute-start | bytes 786440 | tf_op jit(solution)/shard_map/ppermute | solution.py:34
  65.2 7.1 %copy-start.1 = (f32[32,4096]{1,0:T(8,128)S(1)}, f32[32,4096]{1,0:T(8,128)}, u32[]{:S(2)}) copy-start(f32[32,4096]{1,0:T(8,128)} %param.15) | copy-start | bytes 1572868
  65.3 13.4 %collective-permute-start.19 = (bf16[16,4096]{1,0:T(8,128)(2,1)S(1)}, bf16[16,4096]{1,0:T(8,128)(2,1)S(1)}, u32[]{:S(2)}, u32[]{:S(2)}) collective-permute-start(bf16[16,4096]{1,0:T(8,128)(2,1)S(1)} %get-tuple-element.64), channel_id=1, source_target_pairs={{0,2},{1,3},{2,4},{3,5},{4,6},{5,7},{6,0},{7,1},{64,66},{65,67},{6... | collective-permute-start | bytes 393224 | tf_op jit(solution)/shard_map/ppermute | solution.py:34
  68.2 6.3 %collective-permute-start.18 = (bf16[16,4096]{1,0:T(8,128)(2,1)S(1)}, bf16[16,4096]{1,0:T(8,128)(2,1)S(1)}, u32[]{:S(2)}, u32[]{:S(2)}) collective-permute-start(bf16[16,4096]{1,0:T(8,128)(2,1)S(1)} %slice.13), channel_id=1, source_target_pairs={{0,72},{1,73},{2,74},{3,75},{4,76},{5,77},{6,78},{7,79},{64,8},{65... | collective-permute-start | bytes 393224 | tf_op jit(solution)/shard_map/ppermute | solution.py:34
  69.9 7.5 %collective-permute-start.21 = (bf16[16,4096]{1,0:T(8,128)(2,1)S(1)}, bf16[16,4096]{1,0:T(8,128)(2,1)S(1)}, u32[]{:S(2)}, u32[]{:S(2)}) collective-permute-start(bf16[16,4096]{1,0:T(8,128)(2,1)S(1)} %get-tuple-element.70), channel_id=1, source_target_pairs={{0,6},{1,7},{2,0},{3,1},{4,2},{5,3},{6,4},{7,5},{64,70},{65,71},{6... | collective-permute-start | bytes 393224 | tf_op jit(solution)/shard_map/ppermute | solution.py:34
  72.2 6.5 %collective-permute-start.20 = (bf16[16,4096]{1,0:T(8,128)(2,1)S(1)}, bf16[16,4096]{1,0:T(8,128)(2,1)S(1)}, u32[]{:S(2)}, u32[]{:S(2)}) collective-permute-start(bf16[16,4096]{1,0:T(8,128)(2,1)S(1)} %get-tuple-element.69), channel_id=1, source_target_pairs={{0,4},{1,5},{2,6},{3,7},{4,0},{5,1},{6,2},{7,3},{64,68},{65,69},{6... | collective-permute-start | bytes 393224 | tf_op jit(solution)/shard_map/ppermute | solution.py:34

commit v4 on v3

--- a/solution.py
+++ b/solution.py
@@ -101,8 +101,9 @@
     )(*[pltpu.with_memory_space_constraint(weight, pltpu.HBM) for weight in weights])
 
 
-def hidden_kernel(near_ref, far_ref, gate_ref, up_ref, hidden_ref, gate_factor_ref, up_factor_ref):
-    rows = jnp.concatenate([near_ref[...], far_ref[...]], 0)
+def hidden_kernel(*refs):
+    *piece_refs, gate_ref, up_ref, hidden_ref, gate_factor_ref, up_factor_ref = refs
+    rows = jnp.concatenate([piece_ref[...] for piece_ref in piece_refs], 0)
     for low in range(0, gate_ref.shape[1], 128):
         units = slice(low, low + 128)
         both = times(rows, jnp.concatenate([gate_ref[:, units], up_ref[:, units]], 1))
@@ -122,8 +123,21 @@
         there_ref[:, features] = half(partial[128:])
 
 
-def d_hidden_kernel(near_ref, far_ref, down_ref, gate_factor_ref, up_factor_ref, grads_ref):
-    rows = jnp.concatenate([near_ref[...], far_ref[...]], 0)
+def d_hidden_kernel(
+    line_ref,
+    across_ref,
+    line_far_ref,
+    across_far_ref,
+    down_ref,
+    gate_factor_ref,
+    up_factor_ref,
+    grads_ref,
+):
+    pieces = []
+    for own_ref, other_ref in ((line_ref, across_ref), (line_far_ref, across_far_ref)):
+        for d in range(4):
+            pieces += [own_ref[16 * d : 16 * d + 16, :], other_ref[16 * d : 16 * d + 16, :]]
+    rows = jnp.concatenate(pieces, 0)
     count = down_ref.shape[0]
     for low in range(0, count, 256):
         high = min(low + 256, count)
@@ -163,6 +177,15 @@
         sent_ref[...] = half(here_ref[rows, :] + full(there_ref[rows, :]))
 
 
+def both_kernel(here_ref, *refs):
+    *arrived_refs, keep_ref, sent_ref = refs
+    both = here_ref[...]
+    for arrived_ref in arrived_refs:
+        both += full(arrived_ref[...])
+    keep_ref[...] = both[:16]
+    sent_ref[...] = half(both[16:])
+
+
 def add_kernel(left_ref, right_ref, sum_ref):
     sum_ref[...] = left_ref[...] + right_ref[...]
 
@@ -185,29 +208,24 @@
     return lax.optimization_barrier(values)
 
 
-def place_own(tokens_hbm, cotangent_hbm, both_ref, line_ref, sems):
-    moves = ((tokens_hbm, both_ref), (cotangent_hbm, line_ref))
-    copies = [
-        pltpu.make_async_copy(a, b.at[pl.ds(0, a.shape[0])], sems.at[i])
-        for i, (a, b) in enumerate(moves)
-    ]
-    for copy in copies:
-        copy.start()
-    for copy in copies:
-        copy.wait()
-
-
-def own_rows_in_vmem(tokens, cotangent):
-    rows, width = tokens.shape
+def place_kernel(own_hbm, *refs):
+    block_ref, sem = refs[-2:]
+    copy = pltpu.make_async_copy(own_hbm, block_ref.at[pl.ds(0, own_hbm.shape[0])], sem)
+    copy.start()
+    copy.wait()
+
+
+def place_own(own, times_rows, gflop, needs=()):
+    rows, width = own.shape
     return pl.pallas_call(
-        place_own,
-        out_shape=[pltpu.VMEM((2 * rows, width), BF16), pltpu.VMEM((4 * rows, width), BF16)],
-        in_specs=[ANY] * 2,
-        out_specs=[ANY] * 2,
-        scratch_shapes=[pltpu.SemaphoreType.DMA((2,))],
+        place_kernel,
+        out_shape=[pltpu.VMEM((times_rows * rows, width), BF16)],
+        in_specs=[ANY] * (1 + len(needs)),
+        out_specs=[ANY],
+        scratch_shapes=[pltpu.SemaphoreType.DMA],
         compiler_params=pltpu.CompilerParams(vmem_limit_bytes=MIB),
-        cost_estimate=cost(1.0),
-    )(*[pltpu.with_memory_space_constraint(own, pltpu.HBM) for own in (tokens, cotangent)])
+        cost_estimate=cost(gflop),
+    )(pltpu.with_memory_space_constraint(own, pltpu.HBM), *needs)[0]
 
 
 def after(value, *others):
@@ -220,49 +238,64 @@
 
 def on_device(tokens, cotangent, w_gate, w_up, w_down, outer_frag, local_frag, momentum):
     width, units = w_gate.shape
-    both, line = own_rows_in_vmem(tokens, cotangent)
+    both = place_own(tokens, 2, 1.0)
     both = put(both, swap_y(tokens), 16)
     line_arrived = [send_z(cotangent, -d) for d in (1, 2, 3)]
     token_arrived = [send_z(both, -d) for d in (1, 2, 3)]
-    (gate,) = weights_in_vmem(after(w_gate, both))
-    line_arrived = tie(*line_arrived, gate)[:3]
+    line = place_own(cotangent, 4, LONG, needs=(both,))
+    line_arrived = tie(*line_arrived, line)[:3]
     for d in (1, 2, 3):
         line = put(line, line_arrived[d - 1], 16 * d)
     across = swap_y(line)
-    local = after(local_frag[0], gate)
+    local = after(local_frag[0], line)
     local_next = swap_y_low(local)
-    up, down = weights_in_vmem(after(w_up, line), w_down)
+    gate, up, down = weights_in_vmem(after(w_gate, line), w_up, w_down)
     token_arrived = tie(*token_arrived, up, local_next)[:3]
     pseudo = (outer_frag - full(local)) + (outer_frag - full(local_next))
-    token_near = jnp.concatenate([both] + list(token_arrived), 0)
-    token_far = swap_core(token_near)
+    token_near = [both, *token_arrived]
+    token_far = [swap_core(piece) for piece in token_near]
     hidden, gate_factor, up_factor = on_core(
         hidden_kernel,
         SHORT,
         [((256, units), BF16), ((256, units), F32), ((256, units), F32)],
-        token_near,
-        token_far,
+        *token_near,
+        *token_far,
         gate,
         up,
-        needs=(pseudo,),
-    )
-    cotangent_near = jnp.stack([line.reshape(4, 16, width), across.reshape(4, 16, width)], 1)
-    cotangent_near = cotangent_near.reshape(128, width)
-    cotangent_far = swap_core(cotangent_near)
+        needs=(across,),
+    )
+    line_far = swap_core(line)
+    across_far = swap_core(after(across, hidden))
+    out_here, out_there = on_core(
+        output_kernel, SHORT, [((128, width), F32), ((128, width), BF16)], hidden, down
+    )
+    out_far = swap_core(out_there)
     pseudo_next = swap_x(pseudo, True)
+    (pseudo,) = on_core(
+        add_kernel, SHORT, [(pseudo.shape, F32)], pseudo, pseudo_next, needs=(out_there,)
+    )
     (grads,) = on_core(
         d_hidden_kernel,
-        SHORT,
+        LONG,
         [((256, 2 * units), BF16)],
-        cotangent_near,
-        cotangent_far,
+        line,
+        across,
+        line_far,
+        across_far,
         down,
         gate_factor,
         up_factor,
-    )
-    (pseudo,) = on_core(
-        add_kernel, SHORT, [(pseudo.shape, F32)], pseudo, pseudo_next, needs=(grads,)
-    )
+        needs=(out_there, pseudo),
+    )
+    out_keep, out_sent = on_core(
+        sum_for_y_kernel,
+        SHORT,
+        [((64, width), F32), ((64, width), BF16)],
+        out_here,
+        out_far,
+        needs=(grads,),
+    )
+    out_across = swap_y(out_sent)
     grad_here, grad_there = on_core(
         grad_kernel,
         LONG,
@@ -270,59 +303,42 @@
         grads,
         gate,
         up,
-        needs=(pseudo,),
-    )
-    grad_far = swap_core(grad_there)
-    out_here, out_there = on_core(
-        output_kernel,
-        SHORT,
-        [((128, width), F32), ((128, width), BF16)],
-        hidden,
-        down,
-        needs=(grad_there,),
-    )
-    out_far = swap_core(out_there)
-    grad_keep, grad_sent = on_core(
-        sum_for_y_kernel,
-        SHORT,
-        [((64, width), F32), ((64, width), BF16)],
-        grad_here,
-        grad_far,
-        needs=(out_there,),
-    )
-    grad_across = swap_y(grad_sent)
-    pseudo_next = swap_x(after(pseudo, out_there), False)
-    out_keep, *out_sent = on_core(
+        needs=(out_sent,),
+    )
+    pseudo_next = swap_x(after(pseudo, grads), False)
+    grad_keep, *grad_sent = on_core(
         sum_for_z_kernel,
         SHORT,
         [((32, width), F32)] + [((32, width), BF16)] * 3,
-        out_here,
-        out_far,
-        needs=(grad_sent,),
-    )
-    out_arrived = [send_z(out_sent[d - 1], d) for d in (1, 2, 3)]
-    grad_line, *grad_sent = on_core(
+        grad_here,
+        swap_core(grad_there),
+    )
+    grad_arrived = [send_z(grad_sent[d - 1], d) for d in (1, 2, 3)]
+    (pseudo,) = on_core(
+        add_kernel, SHORT, [(pseudo.shape, F32)], pseudo, pseudo_next, needs=(grad_sent[0],)
+    )
+    out_line, *out_sent = on_core(
         line_kernel,
         LONG,
         [((16, width), F32)] + [((16, width), BF16)] * 3,
+        out_keep,
+        out_across,
+        needs=(grad_sent[0], pseudo),
+    )
+    grad_line, grad_sent = on_core(
+        both_kernel,
+        LONG,
+        [((16, width), F32), ((16, width), BF16)],
         grad_keep,
-        grad_across,
-        needs=(out_sent[0],),
-    )
-    out_arrived = tie(*out_arrived, grad_sent[0])[:3]
-    out_both = out_keep + full(out_arrived[0]) + full(out_arrived[1]) + full(out_arrived[2])
-    out_sent = half(out_both[16:])
-    layer_output = out_both[:16] + full(swap_y(out_sent))
-    grad_arrived = [send_z(grad_sent[d - 1], d) for d in (1, 2, 3)]
-    input_grad = (
-        grad_line + full(grad_arrived[0]) + full(grad_arrived[1]) + full(grad_arrived[2])
-    )
-    (pseudo,) = on_core(
-        add_kernel, SHORT, [(pseudo.shape, F32)], pseudo, pseudo_next, needs=(grad_line,)
-    )
+        *grad_arrived,
+    )
+    input_grad = grad_line + full(swap_y(grad_sent))
+    out_arrived = [send_z(out_sent[d - 1], d) for d in (1, 2, 3)]
     mean_delta = pseudo / lax.axis_size("replica")
     new_momentum = outer_beta * momentum + mean_delta
     new_outer = outer_frag - outer_rate * (mean_delta + outer_beta * new_momentum)
+    out_arrived = tie(*out_arrived, grad_line)[:3]
+    layer_output = out_line + full(out_arrived[0]) + full(out_arrived[1]) + full(out_arrived[2])
     return (layer_output, input_grad, new_outer, new_momentum)
 
 

time: 79.8 us -> 74.7 us (0.936)
  waiting for transfers between devices: 24.4 us -> 19.5 us
    ppermute x23 -> x27, waiting for transfers between devices: 24.4 us -> 19.5 us  [send(): return lax.ppermute(rows, AXES, pairs(move))]
    pallas_call x2 -> x1, Pallas kernels: 8.3 us -> 7.28 us  [weights_in_vmem(): pl.pallas_call(load_weights, out_shape=[pltpu.VMEM(weight.shape, weight.d...]
    pallas_call x1 -> x2, Pallas kernels: 0.99 us -> 1.87 us  [place_own(): pl.pallas_call(place_kernel, out_shape=[pltpu.VMEM((times_rows * rows, wi...]
    ppermute x23 -> x27, starting transfers between devices: 28.7 us -> 29 us  [send(): return lax.ppermute(rows, AXES, pairs(move))]
    pallas_call x9 -> x10, Pallas kernels: 13.2 us -> 13.3 us  [on_core(): pl.pallas_call(body, out_shape=[jax.ShapeDtypeStruct(shape, dtype) for sh...]
  transfers between devices with their start and end apart: 23 -> 27, of which waited for: 11 -> 10; matrix products, arithmetic and copies ran while one was open for 3% -> 3% of each run, Pallas kernels for 23% -> 25%
where the time goes in v4:
time: 74.7 us; the launch traced here: 74.6 us
  starting transfers between devices  29 us (39%)
  Pallas kernels  22.5 us (30%)
  waiting for transfers between devices  19.5 us (26%)
  other arithmetic  2.67 us (4%)
  between operations  0.89 us (1%)
    ppermute x27, starting transfers between devices, send(): return lax.ppermute(rows, AXES, pairs(move))  29 us
    ppermute x27, waiting for transfers between devices, send(): return lax.ppermute(rows, AXES, pairs(move))  19.5 us
    pallas_call x10, Pallas kernels, on_core(): pl.pallas_call(body, out_shape=[jax.ShapeDtypeStruct(shape, dtype) for sh...  13.3 us
    pallas_call x1, Pallas kernels, weights_in_vmem(): pl.pallas_call(load_weights, out_shape=[pltpu.VMEM(weight.shape, weight.d...  7.28 us
    pallas_call x2, Pallas kernels, place_own(): pl.pallas_call(place_kernel, out_shape=[pltpu.VMEM((times_rows * rows, wi...  1.87 us
  transfers between devices with their start and end apart: 27, of which 10 were waited for; matrix products, arithmetic and copies ran while one was open for 3% of the time, Pallas kernels for 25%

profile of v4, /device:TPU:0, one launch (start us, length us, event | category | flops | bytes accessed | tf_op | source)
XLA Modules:
  0.0 74.6 jit_solution(2823861686743086602)
XLA Ops:
  0.6 3.2 %collective-permute-start = (bf16[16,4096]{1,0:T(8,128)(2,1)}, bf16[16,4096]{1,0:T(8,128)(2,1)S(1)}, u32[]{:S(2)}, u32[]{:S(2)}) collective-permute-start(bf16[16,4096]{1,0:T(8,128)(2,1)} %own_hbm.2), channel_id=1, source_target_pairs={{0,72},{1,73},{2,74},{3,75},{4,76},{5,77},{6,78},{7,79},{64,8},{65... | collective-permute-start | bytes 393224 | tf_op jit(solution)/shard_map/ppermute | solution.py:34
  3.8 4.0 %collective-permute-start.4 = (bf16[16,4096]{1,0:T(8,128)(2,1)}, bf16[16,4096]{1,0:T(8,128)(2,1)S(1)}, u32[]{:S(2)}, u32[]{:S(2)}) collective-permute-start(bf16[16,4096]{1,0:T(8,128)(2,1)} %own_hbm.3), channel_id=1, source_target_pairs={{0,6},{1,7},{2,0},{3,1},{4,2},{5,3},{6,4},{7,5},{64,70},{65,71},{6... | collective-permute-start | bytes 393224 | tf_op jit(solution)/shard_map/ppermute | solution.py:34
  7.8 1.3 %collective-permute-start.6 = (bf16[16,4096]{1,0:T(8,128)(2,1)}, bf16[16,4096]{1,0:T(8,128)(2,1)S(1)}, u32[]{:S(2)}, u32[]{:S(2)}) collective-permute-start(bf16[16,4096]{1,0:T(8,128)(2,1)} %own_hbm.3), channel_id=1, source_target_pairs={{0,2},{1,3},{2,4},{3,5},{4,6},{5,7},{6,0},{7,1},{64,66},{65,67},{6... | collective-permute-start | bytes 393224 | tf_op jit(solution)/shard_map/ppermute | solution.py:34
  9.1 0.9 %shard_map.111 = bf16[32,4096]{1,0:T(8,128)(2,1)S(1)} custom-call(bf16[16,4096]{1,0:T(8,128)(2,1)} %own_hbm.2), custom_call_target="tpu_custom_call" | custom-call | flops 1000000000 | tf_op jit(solution)/shard_map/pallas_call | solution.py:220
  10.1 1.0 %shard_map.112 = bf16[64,4096]{1,0:T(8,128)(2,1)S(1)} custom-call(bf16[16,4096]{1,0:T(8,128)(2,1)} %own_hbm.3, bf16[32,4096]{1,0:T(8,128)(2,1)S(1)} %constant_dynamic-update-slice_fusion.3.refs_0_), custom_call_target="tpu_custom_call" | custom-call | flops 6000000000 | tf_op jit(solution)/shard_map/pallas_call | solution.py:220
  11.0 2.0 %collective-permute-start.1 = (bf16[32,4096]{1,0:T(8,128)(2,1)S(1)}, bf16[32,4096]{1,0:T(8,128)(2,1)S(1)}, u32[]{:S(2)}, u32[]{:S(2)}) collective-permute-start(bf16[32,4096]{1,0:T(8,128)(2,1)S(1)} %constant_dynamic-update-slice_fusion.3.refs_0_), channel_id=1, source_target_pairs={{0,6},{1,7},{2,0},{3,1},{4,2},{5,3},{6,4},{7,5},{64,70},{65,71},{6... | collective-permute-start | bytes 786440 | tf_op jit(solution)/shard_map/ppermute | solution.py:34
  13.1 2.3 %collective-permute-start.2 = (bf16[32,4096]{1,0:T(8,128)(2,1)S(1)}, bf16[32,4096]{1,0:T(8,128)(2,1)S(1)}, u32[]{:S(2)}, u32[]{:S(2)}) collective-permute-start(bf16[32,4096]{1,0:T(8,128)(2,1)S(1)} %constant_dynamic-update-slice_fusion.3.refs_0_), channel_id=1, source_target_pairs={{0,4},{1,5},{2,6},{3,7},{4,0},{5,1},{6,2},{7,3},{64,68},{65,69},{6... | collective-permute-start | bytes 786440 | tf_op jit(solution)/shard_map/ppermute | solution.py:34
  15.7 1.8 %collective-permute-done.6 = bf16[16,4096]{1,0:T(8,128)(2,1)S(1)} collective-permute-done((bf16[16,4096]{1,0:T(8,128)(2,1)}, bf16[16,4096]{1,0:T(8,128)(2,1)S(1)}, u32[]{:S(2)}, u32[]{:S(2)}) %collective-permute-start.6) | collective-permute-done | bytes 131104 | tf_op jit(solution)/shard_map/ppermute | solution.py:34
  17.9 7.3 %shard_map.113 = (bf16[4096,896]{1,0:T(8,128)(2,1)S(1)}, bf16[4096,896]{1,0:T(8,128)(2,1)S(1)}, bf16[896,4096]{1,0:T(8,128)(2,1)S(1)}) custom-call(bf16[4096,896]{1,0:T(8,128)(2,1)} %refs_0_, bf16[4096,896]{1,0:T(8,128)(2,1)} %refs_1_.1, bf16[896,4096]{1,0:T(8,128)(2,1)} %refs_2_.1), custom_call_target="tpu_custom_call" | custom-call | flops 6000000000 | tf_op jit(solution)/shard_map/pallas_call | solution.py:93
  25.4 2.6 %collective-permute-done.3.refs_3_ = bf16[32,4096]{1,0:T(8,128)(2,1)S(1)} collective-permute-done((bf16[32,4096]{1,0:T(8,128)(2,1)S(1)}, bf16[32,4096]{1,0:T(8,128)(2,1)S(1)}, u32[]{:S(2)}, u32[]{:S(2)}) %collective-permute-start.3) | collective-permute-done | bytes 262176 | tf_op jit(solution)/shard_map/ppermute | solution.py:34
  28.6 0.6 collective-permute-start.14
  29.5 1.5 %collective-permute-start.16 = (f32[32,4096]{1,0:T(8,128)S(1)}, f32[32,4096]{1,0:T(8,128)S(1)}, u32[]{:S(2)}, u32[]{:S(2)}) collective-permute-start(f32[32,4096]{1,0:T(8,128)S(1)} %subtract_add_fusion.refs_0_), channel_id=1, source_target_pairs={{0,16},{1,49},{2,18},{3,51},{4,20},{5,53},{6,22},{7,55},{64,80},{6... | collective-permute-start | bytes 1572872 | tf_op jit(solution)/shard_map/ppermute | solution.py:34
  31.0 0.9 %collective-permute-done.12.refs_10_.refs_1_ = bf16[64,4096]{1,0:T(8,128)(2,1)S(1)} collective-permute-done((bf16[64,4096]{1,0:T(8,128)(2,1)S(1)}, bf16[64,4096]{1,0:T(8,128)(2,1)S(1)}, u32[]{:S(2)}, u32[]{:S(2)}) %collective-permute-start.12) | collective-permute-done | bytes 524320 | tf_op jit(solution)/shard_map/ppermute | solution.py:34
  31.9 4.0 %shard_map.114 = (bf16[256,896]{1,0:T(8,128)(2,1)S(1)}, f32[256,896]{1,0:T(8,128)S(1)}, f32[256,896]{1,0:T(8,128)S(1)}) custom-call(bf16[32,4096]{1,0:T(8,128)(2,1)S(1)} %constant_dynamic-update-slice_fusion.3.refs_0_, bf16[32,4096]{1,0:T(8,128)(2,1)S(1)} %collective-permute-done.1.refs_1_, bf16[32,4096]{1,0:T(8,128)(2,1)S(1)} %collective-permute-done.2.refs_2_, ...), custom_call_target="tpu_custom_call" | custom-call | flops 4000000 | tf_op jit(solution)/shard_map/pallas_call | solution.py:197
  36.2 2.3 %shard_map.115 = (f32[128,4096]{1,0:T(8,128)S(1)}, bf16[128,4096]{1,0:T(8,128)(2,1)S(1)}) custom-call(bf16[256,896]{1,0:T(8,128)(2,1)S(1)} %get-tuple-element.49.refs_0_, bf16[896,4096]{1,0:T(8,128)(2,1)S(1)} %get-tuple-element.50.refs_1_.refs_4_), custom_call_target="tpu_custom_call" | custom-call | flops 4000000 | tf_op jit(solution)/shard_map/pallas_call | solution.py:197
  39.2 2.4 %shard_map.117.refs_2_.refs_0_ = bf16[256,1792]{1,0:T(8,128)(2,1)S(1)} custom-call(bf16[64,4096]{1,0:T(8,128)(2,1)S(1)} %constant_dynamic-update-slice_fusion.refs_0_, bf16[64,4096]{1,0:T(8,128)(2,1)S(1)} %collective-permute-done.12.refs_10_.refs_1_, bf16[64,4096]{1,0:T(8,128)(2,1)S(1)} %collective-permute-done.14.refs_2_, ...), custom_call_target="tpu_custom_call" | custom-call | flops 6000000000 | tf_op jit(solution)/shard_map/pallas_call | solution.py:197
  41.7 4.0 %shard_map.119 = (f32[128,4096]{1,0:T(8,128)S(1)}, bf16[128,4096]{1,0:T(8,128)(2,1)S(1)}) custom-call(bf16[256,1792]{1,0:T(8,128)(2,1)S(1)} %shard_map.117.refs_2_.refs_0_, bf16[4096,896]{1,0:T(8,128)(2,1)S(1)} %get-tuple-element.48.refs_8_.refs_1_, bf16[4096,896]{1,0:T(8,128)(2,1)S(1)} %get-tuple-element.43.refs_9_.refs_2_, ...), custom_call_target="tpu_custom_call" | custom-call | flops 6000000000 | tf_op jit(solution)/shard_map/pallas_call | solution.py:197
  46.0 2.7 %collective-permute-start.19 = (f32[32,4096]{1,0:T(8,128)S(1)}, f32[32,4096]{1,0:T(8,128)S(1)}, u32[]{:S(2)}, u32[]{:S(2)}) collective-permute-start(f32[32,4096]{1,0:T(8,128)S(1)} %shard_map.116.refs_8_.refs_0_), channel_id=1, source_target_pairs={{0,48},{1,17},{2,50},{3,19},{4,52},{5,21},{6,54},{7,23},{64,112},{... | collective-permute-start | bytes 1572872 | tf_op jit(solution)/shard_map/ppermute | solution.py:34
  48.8 0.9 %collective-permute-start.17 = (bf16[64,4096]{1,0:T(8,128)(2,1)S(1)}, bf16[64,4096]{1,0:T(8,128)(2,1)S(1)}, u32[]{:S(2)}, u32[]{:S(2)}) collective-permute-start(bf16[64,4096]{1,0:T(8,128)(2,1)S(1)} %get-tuple-element.57.refs_3_), channel_id=1, source_target_pairs={{0,72},{1,73},{2,74},{3,75},{4,76},{5,77},{6,78},{7,79},{64,8},{65... | collective-permute-start | bytes 1572872 | tf_op jit(solution)/shard_map/ppermute | solution.py:34
  49.9 2.3 %collective-permute-start.24 = (bf16[32,4096]{1,0:T(8,128)(2,1)S(1)}, bf16[32,4096]{1,0:T(8,128)(2,1)S(1)}, u32[]{:S(2)}, u32[]{:S(2)}) collective-permute-start(bf16[32,4096]{1,0:T(8,128)(2,1)S(1)} %get-tuple-element.67), channel_id=1, source_target_pairs={{0,4},{1,5},{2,6},{3,7},{4,0},{5,1},{6,2},{7,3},{64,68},{65,69},{6... | collective-permute-start | bytes 786440 | tf_op jit(solution)/shard_map/ppermute | solution.py:34
  52.3 1.3 %collective-permute-start.25 = (bf16[32,4096]{1,0:T(8,128)(2,1)S(1)}, bf16[32,4096]{1,0:T(8,128)(2,1)S(1)}, u32[]{:S(2)}, u32[]{:S(2)}) collective-permute-start(bf16[32,4096]{1,0:T(8,128)(2,1)S(1)} %get-tuple-element.68), channel_id=1, source_target_pairs={{0,6},{1,7},{2,0},{3,1},{4,2},{5,3},{6,4},{7,5},{64,70},{65,71},{6... | collective-permute-start | bytes 786440 | tf_op jit(solution)/shard_map/ppermute | solution.py:34
  53.6 2.8 %collective-permute-done.19.refs_1_ = f32[32,4096]{1,0:T(8,128)S(1)} collective-permute-done((f32[32,4096]{1,0:T(8,128)S(1)}, f32[32,4096]{1,0:T(8,128)S(1)}, u32[]{:S(2)}, u32[]{:S(2)}) %collective-permute-start.19) | collective-permute-done | bytes 524320 | tf_op jit(solution)/shard_map/ppermute | solution.py:34
  56.5 6.1 %collective-permute-done.17.refs_1_ = bf16[64,4096]{1,0:T(8,128)(2,1)S(1)} collective-permute-done((bf16[64,4096]{1,0:T(8,128)(2,1)S(1)}, bf16[64,4096]{1,0:T(8,128)(2,1)S(1)}, u32[]{:S(2)}, u32[]{:S(2)}) %collective-permute-start.17) | collective-permute-done | bytes 524320 | tf_op jit(solution)/shard_map/ppermute | solution.py:34
  62.8 1.9 %collective-permute-start.21 = (bf16[16,4096]{1,0:T(8,128)(2,1)S(1)}, bf16[16,4096]{1,0:T(8,128)(2,1)S(1)}, u32[]{:S(2)}, u32[]{:S(2)}) collective-permute-start(bf16[16,4096]{1,0:T(8,128)(2,1)S(1)} %get-tuple-element.64), channel_id=1, source_target_pairs={{0,4},{1,5},{2,6},{3,7},{4,0},{5,1},{6,2},{7,3},{64,68},{65,69},{6... | collective-permute-start | bytes 393224 | tf_op jit(solution)/shard_map/ppermute | solution.py:34
  64.7 1.1 %multiply_subtract_fusion = (f32[32,4096]{1,0:T(8,128)}, f32[32,4096]{1,0:T(8,128)}) fusion(f32[32,4096]{1,0:T(8,128)S(1)} %copy-done, f32[32,4096]{1,0:T(8,128)S(1)} %shard_map.121.refs_3_, f32[32,4096]{1,0:T(8,128)S(1)} %copy-done.1), kind=kLoop, calls=%fused_computation | loop fusion | flops 917504 | bytes 2621440 | tf_op jit(solution)/shard_map/sub | solution.py:339
  65.8 1.7 %collective-permute-start.22 = (bf16[16,4096]{1,0:T(8,128)(2,1)S(1)}, bf16[16,4096]{1,0:T(8,128)(2,1)S(1)}, u32[]{:S(2)}, u32[]{:S(2)}) collective-permute-start(bf16[16,4096]{1,0:T(8,128)(2,1)S(1)} %get-tuple-element.65), channel_id=1, source_target_pairs={{0,6},{1,7},{2,0},{3,1},{4,2},{5,3},{6,4},{7,5},{64,70},{65,71},{6... | collective-permute-start | bytes 393224 | tf_op jit(solution)/shard_map/ppermute | solution.py:34
  67.6 0.9 %collective-permute-start.26 = (bf16[16,4096]{1,0:T(8,128)(2,1)S(1)}, bf16[16,4096]{1,0:T(8,128)(2,1)S(1)}, u32[]{:S(2)}, u32[]{:S(2)}) collective-permute-start(bf16[16,4096]{1,0:T(8,128)(2,1)S(1)} %get-tuple-element.73), channel_id=1, source_target_pairs={{0,72},{1,73},{2,74},{3,75},{4,76},{5,77},{6,78},{7,79},{64,8},{65... | collective-permute-start | bytes 393224 | tf_op jit(solution)/shard_map/ppermute | solution.py:34
  68.5 1.8 %collective-permute-done.20 = bf16[16,4096]{1,0:T(8,128)(2,1)S(1)} collective-permute-done((bf16[16,4096]{1,0:T(8,128)(2,1)S(1)}, bf16[16,4096]{1,0:T(8,128)(2,1)S(1)}, u32[]{:S(2)}, u32[]{:S(2)}) %collective-permute-start.20) | collective-permute-done | bytes 131104 | tf_op jit(solution)/shard_map/ppermute | solution.py:34
  70.3 0.9 %collective-permute-done.22 = bf16[16,4096]{1,0:T(8,128)(2,1)S(1)} collective-permute-done((bf16[16,4096]{1,0:T(8,128)(2,1)S(1)}, bf16[16,4096]{1,0:T(8,128)(2,1)S(1)}, u32[]{:S(2)}, u32[]{:S(2)}) %collective-permute-start.22) | collective-permute-done | bytes 131104 | tf_op jit(solution)/shard_map/ppermute | solution.py:34
  71.2 0.8 %convert_add_fusion.1 = f32[16,4096]{1,0:T(8,128)} fusion(bf16[16,4096]{1,0:T(8,128)(2,1)S(1)} %collective-permute-done.22, bf16[16,4096]{1,0:T(8,128)(2,1)S(1)} %collective-permute-done.21, f32[16,4096]{1,0:T(8,128)S(1)} %get-tuple-element.62, bf16[16,4096]{1,0:T(8,128)(2,1)S(1)} %collective-permute-done.20), kind=kLoop, calls=%fused_computation.4 | loop fusion | flops 393216 | bytes 917504 | tf_op jit(solution)/shard_map/add | solution.py:341
  71.9 1.9 %collective-permute-done.26 = bf16[16,4096]{1,0:T(8,128)(2,1)S(1)} collective-permute-done((bf16[16,4096]{1,0:T(8,128)(2,1)S(1)}, bf16[16,4096]{1,0:T(8,128)(2,1)S(1)}, u32[]{:S(2)}, u32[]{:S(2)}) %collective-permute-start.26) | collective-permute-done | bytes 131104 | tf_op jit(solution)/shard_map/ppermute | solution.py:34
  73.9 0.7 convert_add_fusion
  (49 shorter events, 3.7 us)
Async XLA Ops:
  0.6 9.4 %collective-permute-start = (bf16[16,4096]{1,0:T(8,128)(2,1)}, bf16[16,4096]{1,0:T(8,128)(2,1)S(1)}, u32[]{:S(2)}, u32[]{:S(2)}) collective-permute-start(bf16[16,4096]{1,0:T(8,128)(2,1)} %own_hbm.2), channel_id=1, source_target_pairs={{0,72},{1,73},{2,74},{3,75},{4,76},{5,77},{6,78},{7,79},{64,8},{65... | collective-permute-start | bytes 393224 | tf_op jit(solution)/shard_map/ppermute | solution.py:34
  3.8 11.6 %collective-permute-start.4 = (bf16[16,4096]{1,0:T(8,128)(2,1)}, bf16[16,4096]{1,0:T(8,128)(2,1)S(1)}, u32[]{:S(2)}, u32[]{:S(2)}) collective-permute-start(bf16[16,4096]{1,0:T(8,128)(2,1)} %own_hbm.3), channel_id=1, source_target_pairs={{0,6},{1,7},{2,0},{3,1},{4,2},{5,3},{6,4},{7,5},{64,70},{65,71},{6... | collective-permute-start | bytes 393224 | tf_op jit(solution)/shard_map/ppermute | solution.py:34
  7.8 7.9 %collective-permute-start.5 = (bf16[16,4096]{1,0:T(8,128)(2,1)}, bf16[16,4096]{1,0:T(8,128)(2,1)S(1)}, u32[]{:S(2)}, u32[]{:S(2)}) collective-permute-start(bf16[16,4096]{1,0:T(8,128)(2,1)} %own_hbm.3), channel_id=1, source_target_pairs={{0,4},{1,5},{2,6},{3,7},{4,0},{5,1},{6,2},{7,3},{64,68},{65,69},{6... | collective-permute-start | bytes 393224 | tf_op jit(solution)/shard_map/ppermute | solution.py:34
  7.8 9.7 %collective-permute-start.6 = (bf16[16,4096]{1,0:T(8,128)(2,1)}, bf16[16,4096]{1,0:T(8,128)(2,1)S(1)}, u32[]{:S(2)}, u32[]{:S(2)}) collective-permute-start(bf16[16,4096]{1,0:T(8,128)(2,1)} %own_hbm.3), channel_id=1, source_target_pairs={{0,2},{1,3},{2,4},{3,5},{4,6},{5,7},{6,0},{7,1},{64,66},{65,67},{6... | collective-permute-start | bytes 393224 | tf_op jit(solution)/shard_map/ppermute | solution.py:34
  10.1 7.6 %copy-start.2 = (bf16[1,32,4096]{2,1,0:T(8,128)(2,1)S(1)}, bf16[1,32,4096]{2,1,0:T(8,128)(2,1)}, u32[]{:S(2)}) copy-start(bf16[1,32,4096]{2,1,0:T(8,128)(2,1)} %param.14) | copy-start | bytes 786436
  11.0 14.3 %collective-permute-start.1 = (bf16[32,4096]{1,0:T(8,128)(2,1)S(1)}, bf16[32,4096]{1,0:T(8,128)(2,1)S(1)}, u32[]{:S(2)}, u32[]{:S(2)}) collective-permute-start(bf16[32,4096]{1,0:T(8,128)(2,1)S(1)} %constant_dynamic-update-slice_fusion.3.refs_0_), channel_id=1, source_target_pairs={{0,6},{1,7},{2,0},{3,1},{4,2},{5,3},{6,4},{7,5},{64,70},{65,71},{6... | collective-permute-start | bytes 786440 | tf_op jit(solution)/shard_map/ppermute | solution.py:34
  13.1 12.3 %collective-permute-start.2 = (bf16[32,4096]{1,0:T(8,128)(2,1)S(1)}, bf16[32,4096]{1,0:T(8,128)(2,1)S(1)}, u32[]{:S(2)}, u32[]{:S(2)}) collective-permute-start(bf16[32,4096]{1,0:T(8,128)(2,1)S(1)} %constant_dynamic-update-slice_fusion.3.refs_0_), channel_id=1, source_target_pairs={{0,4},{1,5},{2,6},{3,7},{4,0},{5,1},{6,2},{7,3},{64,68},{65,69},{6... | collective-permute-start | bytes 786440 | tf_op jit(solution)/shard_map/ppermute | solution.py:34
  15.4 12.6 %collective-permute-start.3 = (bf16[32,4096]{1,0:T(8,128)(2,1)S(1)}, bf16[32,4096]{1,0:T(8,128)(2,1)S(1)}, u32[]{:S(2)}, u32[]{:S(2)}) collective-permute-start(bf16[32,4096]{1,0:T(8,128)(2,1)S(1)} %constant_dynamic-update-slice_fusion.3.refs_0_), channel_id=1, source_target_pairs={{0,2},{1,3},{2,4},{3,5},{4,6},{5,7},{6,0},{7,1},{64,66},{65,67},{6... | collective-permute-start | bytes 786440 | tf_op jit(solution)/shard_map/ppermute | solution.py:34
  17.6 14.3 %collective-permute-start.12 = (bf16[64,4096]{1,0:T(8,128)(2,1)S(1)}, bf16[64,4096]{1,0:T(8,128)(2,1)S(1)}, u32[]{:S(2)}, u32[]{:S(2)}) collective-permute-start(bf16[64,4096]{1,0:T(8,128)(2,1)S(1)} %constant_dynamic-update-slice_fusion.refs_0_), channel_id=1, source_target_pairs={{0,72},{1,73},{2,74},{3,75},{4,76},{5,77},{6,78},{7,79},{64,8},{65... | collective-permute-start | bytes 1572872 | tf_op jit(solution)/shard_map/ppermute | solution.py:34
  17.7 10.8 %copy-start = (f32[32,4096]{1,0:T(8,128)S(1)}, f32[32,4096]{1,0:T(8,128)}, u32[]{:S(2)}) copy-start(f32[32,4096]{1,0:T(8,128)} %param.13) | copy-start | bytes 1572868
  17.7 7.5 %collective-permute-start.7 = (bf16[32,4096]{1,0:T(8,128)(2,1)S(1)}, bf16[32,4096]{1,0:T(8,128)(2,1)S(1)}, u32[]{:S(2)}, u32[]{:S(2)}) collective-permute-start(bf16[32,4096]{1,0:T(8,128)(2,1)S(1)} %bitcast.1), channel_id=1, source_target_pairs={{0,64},{1,65},{2,66},{3,67},{4,68},{5,69},{6,70},{7,71},{64,0},{65... | collective-permute-start | bytes 786440 | tf_op jit(solution)/shard_map/ppermute | solution.py:34
  25.2 3.4 %collective-permute-start.8 = (bf16[32,4096]{1,0:T(8,128)(2,1)S(1)}, bf16[32,4096]{1,0:T(8,128)(2,1)S(1)}, u32[]{:S(2)}, u32[]{:S(2)}) collective-permute-start(bf16[32,4096]{1,0:T(8,128)(2,1)S(1)} %constant_dynamic-update-slice_fusion.3.refs_0_), channel_id=1, source_target_pairs={{0,1},{1,0},{2,3},{3,2},{4,5},{5,4},{6,7},{7,6},{64,65},{65,64},{6... | collective-permute-start | bytes 786440 | tf_op jit(solution)/shard_map/ppermute | solution.py:34
  28.0 1.5 %collective-permute-start.10 = (bf16[32,4096]{1,0:T(8,128)(2,1)S(1)}, bf16[32,4096]{1,0:T(8,128)(2,1)S(1)}, u32[]{:S(2)}, u32[]{:S(2)}) collective-permute-start(bf16[32,4096]{1,0:T(8,128)(2,1)S(1)} %collective-permute-done.2.refs_2_), channel_id=1, source_target_pairs={{0,1},{1,0},{2,3},{3,2},{4,5},{5,4},{6,7},{7,6},{64,65},{65,64},{6... | collective-permute-start | bytes 786440 | tf_op jit(solution)/shard_map/ppermute | solution.py:34
  28.0 3.0 %collective-permute-start.11 = (bf16[32,4096]{1,0:T(8,128)(2,1)S(1)}, bf16[32,4096]{1,0:T(8,128)(2,1)S(1)}, u32[]{:S(2)}, u32[]{:S(2)}) collective-permute-start(bf16[32,4096]{1,0:T(8,128)(2,1)S(1)} %collective-permute-done.3.refs_3_), channel_id=1, source_target_pairs={{0,1},{1,0},{2,3},{3,2},{4,5},{5,4},{6,7},{7,6},{64,65},{65,64},{6... | collective-permute-start | bytes 786440 | tf_op jit(solution)/shard_map/ppermute | solution.py:34
  28.5 2.5 %collective-permute-start.9 = (bf16[32,4096]{1,0:T(8,128)(2,1)S(1)}, bf16[32,4096]{1,0:T(8,128)(2,1)S(1)}, u32[]{:S(2)}, u32[]{:S(2)}) collective-permute-start(bf16[32,4096]{1,0:T(8,128)(2,1)S(1)} %collective-permute-done.1.refs_1_), channel_id=1, source_target_pairs={{0,1},{1,0},{2,3},{3,2},{4,5},{5,4},{6,7},{7,6},{64,65},{65,64},{6... | collective-permute-start | bytes 786440 | tf_op jit(solution)/shard_map/ppermute | solution.py:34
  28.6 10.6 %collective-permute-start.14 = (bf16[64,4096]{1,0:T(8,128)(2,1)S(1)}, bf16[64,4096]{1,0:T(8,128)(2,1)S(1)}, u32[]{:S(2)}, u32[]{:S(2)}) collective-permute-start(bf16[64,4096]{1,0:T(8,128)(2,1)S(1)} %constant_dynamic-update-slice_fusion.refs_0_), channel_id=1, source_target_pairs={{0,1},{1,0},{2,3},{3,2},{4,5},{5,4},{6,7},{7,6},{64,65},{65,64},{6... | collective-permute-start | bytes 1572872 | tf_op jit(solution)/shard_map/ppermute | solution.py:34
  29.5 9.6 %collective-permute-start.16 = (f32[32,4096]{1,0:T(8,128)S(1)}, f32[32,4096]{1,0:T(8,128)S(1)}, u32[]{:S(2)}, u32[]{:S(2)}) collective-permute-start(f32[32,4096]{1,0:T(8,128)S(1)} %subtract_add_fusion.refs_0_), channel_id=1, source_target_pairs={{0,16},{1,49},{2,18},{3,51},{4,20},{5,53},{6,22},{7,55},{64,80},{6... | collective-permute-start | bytes 1572872 | tf_op jit(solution)/shard_map/ppermute | solution.py:34
  35.9 3.3 %collective-permute-start.15 = (bf16[64,4096]{1,0:T(8,128)(2,1)S(1)}, bf16[64,4096]{1,0:T(8,128)(2,1)S(1)}, u32[]{:S(2)}, u32[]{:S(2)}) collective-permute-start(bf16[64,4096]{1,0:T(8,128)(2,1)S(1)} %collective-permute-done.12.refs_10_.refs_1_), channel_id=1, source_target_pairs={{0,1},{1,0},{2,3},{3,2},{4,5},{5,4},{6,7},{7,6},{64,65},{65,64},{6... | collective-permute-start | bytes 1572872 | tf_op jit(solution)/shard_map/ppermute | solution.py:34
  38.6 3.0 %collective-permute-start.13 = (bf16[128,4096]{1,0:T(8,128)(2,1)S(1)}, bf16[128,4096]{1,0:T(8,128)(2,1)S(1)}, u32[]{:S(2)}, u32[]{:S(2)}) collective-permute-start(bf16[128,4096]{1,0:T(8,128)(2,1)S(1)} %get-tuple-element.52.refs_2_.refs_7_), channel_id=1, source_target_pairs={{0,1},{1,0},{2,3},{3,2},{4,5},{5,4},{6,7},{7,6},{64,65},{65,64},{6... | collective-permute-start | bytes 3145736 | tf_op jit(solution)/shard_map/ppermute | solution.py:34
  45.7 3.9 %collective-permute-start.18 = (bf16[128,4096]{1,0:T(8,128)(2,1)S(1)}, bf16[128,4096]{1,0:T(8,128)(2,1)S(1)}, u32[]{:S(2)}, u32[]{:S(2)}) collective-permute-start(bf16[128,4096]{1,0:T(8,128)(2,1)S(1)} %get-tuple-element.59), channel_id=1, source_target_pairs={{0,1},{1,0},{2,3},{3,2},{4,5},{5,4},{6,7},{7,6},{64,65},{65,64},{6... | collective-permute-start | bytes 3145736 | tf_op jit(solution)/shard_map/ppermute | solution.py:34
  46.0 10.4 %collective-permute-start.19 = (f32[32,4096]{1,0:T(8,128)S(1)}, f32[32,4096]{1,0:T(8,128)S(1)}, u32[]{:S(2)}, u32[]{:S(2)}) collective-permute-start(f32[32,4096]{1,0:T(8,128)S(1)} %shard_map.116.refs_8_.refs_0_), channel_id=1, source_target_pairs={{0,48},{1,17},{2,50},{3,19},{4,52},{5,21},{6,54},{7,23},{64,112},{... | collective-permute-start | bytes 1572872 | tf_op jit(solution)/shard_map/ppermute | solution.py:34
  48.8 13.8 %collective-permute-start.17 = (bf16[64,4096]{1,0:T(8,128)(2,1)S(1)}, bf16[64,4096]{1,0:T(8,128)(2,1)S(1)}, u32[]{:S(2)}, u32[]{:S(2)}) collective-permute-start(bf16[64,4096]{1,0:T(8,128)(2,1)S(1)} %get-tuple-element.57.refs_3_), channel_id=1, source_target_pairs={{0,72},{1,73},{2,74},{3,75},{4,76},{5,77},{6,78},{7,79},{64,8},{65... | collective-permute-start | bytes 1572872 | tf_op jit(solution)/shard_map/ppermute | solution.py:34
  49.9 15.9 %collective-permute-start.23 = (bf16[32,4096]{1,0:T(8,128)(2,1)S(1)}, bf16[32,4096]{1,0:T(8,128)(2,1)S(1)}, u32[]{:S(2)}, u32[]{:S(2)}) collective-permute-start(bf16[32,4096]{1,0:T(8,128)(2,1)S(1)} %get-tuple-element.60.refs_2_), channel_id=1, source_target_pairs={{0,2},{1,3},{2,4},{3,5},{4,6},{5,7},{6,0},{7,1},{64,66},{65,67},{6... | collective-permute-start | bytes 786440 | tf_op jit(solution)/shard_map/ppermute | solution.py:34
  49.9 17.6 %collective-permute-start.24 = (bf16[32,4096]{1,0:T(8,128)(2,1)S(1)}, bf16[32,4096]{1,0:T(8,128)(2,1)S(1)}, u32[]{:S(2)}, u32[]{:S(2)}) collective-permute-start(bf16[32,4096]{1,0:T(8,128)(2,1)S(1)} %get-tuple-element.67), channel_id=1, source_target_pairs={{0,4},{1,5},{2,6},{3,7},{4,0},{5,1},{6,2},{7,3},{64,68},{65,69},{6... | collective-permute-start | bytes 786440 | tf_op jit(solution)/shard_map/ppermute | solution.py:34
  52.3 15.2 %collective-permute-start.25 = (bf16[32,4096]{1,0:T(8,128)(2,1)S(1)}, bf16[32,4096]{1,0:T(8,128)(2,1)S(1)}, u32[]{:S(2)}, u32[]{:S(2)}) collective-permute-start(bf16[32,4096]{1,0:T(8,128)(2,1)S(1)} %get-tuple-element.68), channel_id=1, source_target_pairs={{0,6},{1,7},{2,0},{3,1},{4,2},{5,3},{6,4},{7,5},{64,70},{65,71},{6... | collective-permute-start | bytes 786440 | tf_op jit(solution)/shard_map/ppermute | solution.py:34
  62.6 2.1 %copy-start.1 = (f32[32,4096]{1,0:T(8,128)S(1)}, f32[32,4096]{1,0:T(8,128)}, u32[]{:S(2)}) copy-start(f32[32,4096]{1,0:T(8,128)} %param.15) | copy-start | bytes 1572868
  62.7 7.7 %collective-permute-start.20 = (bf16[16,4096]{1,0:T(8,128)(2,1)S(1)}, bf16[16,4096]{1,0:T(8,128)(2,1)S(1)}, u32[]{:S(2)}, u32[]{:S(2)}) collective-permute-start(bf16[16,4096]{1,0:T(8,128)(2,1)S(1)} %get-tuple-element.63), channel_id=1, source_target_pairs={{0,2},{1,3},{2,4},{3,5},{4,6},{5,7},{6,0},{7,1},{64,66},{65,67},{6... | collective-permute-start | bytes 393224 | tf_op jit(solution)/shard_map/ppermute | solution.py:34
  62.8 7.6 %collective-permute-start.21 = (bf16[16,4096]{1,0:T(8,128)(2,1)S(1)}, bf16[16,4096]{1,0:T(8,128)(2,1)S(1)}, u32[]{:S(2)}, u32[]{:S(2)}) collective-permute-start(bf16[16,4096]{1,0:T(8,128)(2,1)S(1)} %get-tuple-element.64), channel_id=1, source_target_pairs={{0,4},{1,5},{2,6},{3,7},{4,0},{5,1},{6,2},{7,3},{64,68},{65,69},{6... | collective-permute-start | bytes 393224 | tf_op jit(solution)/shard_map/ppermute | solution.py:34
  65.8 5.4 %collective-permute-start.22 = (bf16[16,4096]{1,0:T(8,128)(2,1)S(1)}, bf16[16,4096]{1,0:T(8,128)(2,1)S(1)}, u32[]{:S(2)}, u32[]{:S(2)}) collective-permute-start(bf16[16,4096]{1,0:T(8,128)(2,1)S(1)} %get-tuple-element.65), channel_id=1, source_target_pairs={{0,6},{1,7},{2,0},{3,1},{4,2},{5,3},{6,4},{7,5},{64,70},{65,71},{6... | collective-permute-start | bytes 393224 | tf_op jit(solution)/shard_map/ppermute | solution.py:34
  67.6 6.3 %collective-permute-start.26 = (bf16[16,4096]{1,0:T(8,128)(2,1)S(1)}, bf16[16,4096]{1,0:T(8,128)(2,1)S(1)}, u32[]{:S(2)}, u32[]{:S(2)}) collective-permute-start(bf16[16,4096]{1,0:T(8,128)(2,1)S(1)} %get-tuple-element.73), channel_id=1, source_target_pairs={{0,72},{1,73},{2,74},{3,75},{4,76},{5,77},{6,78},{7,79},{64,8},{65... | collective-permute-start | bytes 393224 | tf_op jit(solution)/shard_map/ppermute | solution.py:34

commit v5 on v4

--- a/solution.py
+++ b/solution.py
@@ -186,6 +186,15 @@
     sent_ref[...] = half(both[16:])
 
 
+def last_kernel(grad_line_ref, grad_across_ref, out_line_ref, *refs):
+    *arrived_refs, output_ref, grad_ref = refs
+    total = out_line_ref[...]
+    for arrived_ref in arrived_refs:
+        total += full(arrived_ref[...])
+    output_ref[...] = total
+    grad_ref[...] = grad_line_ref[...] + full(grad_across_ref[...])
+
+
 def add_kernel(left_ref, right_ref, sum_ref):
     sum_ref[...] = left_ref[...] + right_ref[...]
 
@@ -208,24 +217,41 @@
     return lax.optimization_barrier(values)
 
 
-def place_kernel(own_hbm, *refs):
-    block_ref, sem = refs[-2:]
-    copy = pltpu.make_async_copy(own_hbm, block_ref.at[pl.ds(0, own_hbm.shape[0])], sem)
-    copy.start()
-    copy.wait()
-
-
-def place_own(own, times_rows, gflop, needs=()):
-    rows, width = own.shape
+def place_kernel(tokens_hbm, cotangent_hbm, both_ref, line_ref, sems):
+    moves = ((tokens_hbm, both_ref), (cotangent_hbm, line_ref))
+    copies = [
+        pltpu.make_async_copy(a, b.at[pl.ds(0, a.shape[0])], sems.at[i])
+        for i, (a, b) in enumerate(moves)
+    ]
+    for copy in copies:
+        copy.start()
+    for copy in copies:
+        copy.wait()
+
+
+def place_own(tokens, cotangent):
+    rows, width = tokens.shape
     return pl.pallas_call(
         place_kernel,
-        out_shape=[pltpu.VMEM((times_rows * rows, width), BF16)],
+        out_shape=[pltpu.VMEM((2 * rows, width), BF16), pltpu.VMEM((4 * rows, width), BF16)],
+        in_specs=[ANY] * 2,
+        out_specs=[ANY] * 2,
+        scratch_shapes=[pltpu.SemaphoreType.DMA((2,))],
+        compiler_params=pltpu.CompilerParams(vmem_limit_bytes=MIB),
+        cost_estimate=cost(1.0),
+    )(*[pltpu.with_memory_space_constraint(own, pltpu.HBM) for own in (tokens, cotangent)])
+
+
+def hold(block, *needs):
+    return pl.pallas_call(
+        lambda *refs: None,
+        out_shape=pltpu.VMEM(block.shape, block.dtype),
         in_specs=[ANY] * (1 + len(needs)),
-        out_specs=[ANY],
-        scratch_shapes=[pltpu.SemaphoreType.DMA],
+        out_specs=ANY,
+        input_output_aliases={0: 0},
         compiler_params=pltpu.CompilerParams(vmem_limit_bytes=MIB),
-        cost_estimate=cost(gflop),
-    )(pltpu.with_memory_space_constraint(own, pltpu.HBM), *needs)[0]
+        cost_estimate=cost(LONG),
+    )(block, *needs)
 
 
 def after(value, *others):
@@ -238,18 +264,19 @@
 
 def on_device(tokens, cotangent, w_gate, w_up, w_down, outer_frag, local_frag, momentum):
     width, units = w_gate.shape
-    both = place_own(tokens, 2, 1.0)
+    both, line = place_own(tokens, cotangent)
     both = put(both, swap_y(tokens), 16)
     line_arrived = [send_z(cotangent, -d) for d in (1, 2, 3)]
     token_arrived = [send_z(both, -d) for d in (1, 2, 3)]
-    line = place_own(cotangent, 4, LONG, needs=(both,))
+    line = hold(line, both)
     line_arrived = tie(*line_arrived, line)[:3]
     for d in (1, 2, 3):
         line = put(line, line_arrived[d - 1], 16 * d)
     across = swap_y(line)
     local = after(local_frag[0], line)
     local_next = swap_y_low(local)
-    gate, up, down = weights_in_vmem(after(w_gate, line), w_up, w_down)
+    gate, up = weights_in_vmem(after(w_gate, line), w_up)
+    down = pltpu.with_memory_space_constraint(w_down, pltpu.VMEM)
     token_arrived = tie(*token_arrived, up, local_next)[:3]
     pseudo = (outer_frag - full(local)) + (outer_frag - full(local_next))
     token_near = [both, *token_arrived]
@@ -313,32 +340,41 @@
         grad_here,
         swap_core(grad_there),
     )
-    grad_arrived = [send_z(grad_sent[d - 1], d) for d in (1, 2, 3)]
+    grad_arrived = {d: send_z(grad_sent[d - 1], d) for d in (2, 1, 3)}
+    grad_arrived = [grad_arrived[d] for d in (1, 2, 3)]
     (pseudo,) = on_core(
         add_kernel, SHORT, [(pseudo.shape, F32)], pseudo, pseudo_next, needs=(grad_sent[0],)
     )
+    mean_delta = pseudo / lax.axis_size("replica")
+    new_momentum = outer_beta * momentum + mean_delta
+    new_outer = outer_frag - outer_rate * (mean_delta + outer_beta * new_momentum)
     out_line, *out_sent = on_core(
         line_kernel,
         LONG,
         [((16, width), F32)] + [((16, width), BF16)] * 3,
         out_keep,
         out_across,
-        needs=(grad_sent[0], pseudo),
+        needs=(grad_sent[0], new_outer),
     )
     grad_line, grad_sent = on_core(
         both_kernel,
         LONG,
         [((16, width), F32), ((16, width), BF16)],
         grad_keep,
-        *grad_arrived,
-    )
-    input_grad = grad_line + full(swap_y(grad_sent))
+        grad_arrived[1],
+        grad_arrived[0],
+        grad_arrived[2],
+    )
     out_arrived = [send_z(out_sent[d - 1], d) for d in (1, 2, 3)]
-    mean_delta = pseudo / lax.axis_size("replica")
-    new_momentum = outer_beta * momentum + mean_delta
-    new_outer = outer_frag - outer_rate * (mean_delta + outer_beta * new_momentum)
-    out_arrived = tie(*out_arrived, grad_line)[:3]
-    layer_output = out_line + full(out_arrived[0]) + full(out_arrived[1]) + full(out_arrived[2])
+    layer_output, input_grad = on_core(
+        last_kernel,
+        SHORT,
+        [((16, width), F32), ((16, width), F32)],
+        grad_line,
+        swap_y(grad_sent),
+        out_line,
+        *out_arrived,
+    )
     return (layer_output, input_grad, new_outer, new_momentum)
 
 

time: 74.7 us -> 74 us (level)
  starting transfers between devices: 29 us -> 31.8 us
  Pallas kernels: 22.5 us -> 20.3 us
  other arithmetic: 2.67 us -> 1.02 us
    ppermute x27, starting transfers between devices: 29 us -> 31.8 us  [send(): return lax.ppermute(rows, AXES, pairs(move))]
    pallas_call x1, Pallas kernels: 7.28 us -> 5.19 us  [weights_in_vmem(): pl.pallas_call(load_weights, out_shape=[pltpu.VMEM(weight.shape, weight.d...]
    add x2 -> x0, other arithmetic: 1.48 us -> none  [the longest x1 0.76 us: on_device(): out_line + full(out_arrived[0]) + full(out_arrived[1])]
    pallas_call x2, Pallas kernels: 1.87 us -> 0.99 us  [the longest x1 0.99 us: place_own(): pl.pallas_call(place_kernel, out_shape=[pltpu.VMEM((2 * rows, width), BF1...]
    pallas_call x10 -> x11, Pallas kernels: 13.3 us -> 14.2 us  [on_core(): pl.pallas_call(body, out_shape=[jax.ShapeDtypeStruct(shape, dtype) for sh...]
  transfers between devices with their start and end apart: 27 -> 27, of which waited for: 10 -> 11; matrix products, arithmetic and copies ran while one was open for 3% -> 1% of each run, Pallas kernels for 25% -> 21%
where the time goes in v5:
time: 74 us; the launch traced here: 73.8 us
  starting transfers between devices  31.8 us (43%)
  Pallas kernels  20.3 us (27%)
  waiting for transfers between devices  19.7 us (27%)
  other arithmetic  1.02 us (1%)
  between operations  0.9 us (1%)
    ppermute x27, starting transfers between devices, send(): return lax.ppermute(rows, AXES, pairs(move))  31.8 us
    ppermute x27, waiting for transfers between devices, send(): return lax.ppermute(rows, AXES, pairs(move))  19.7 us
    pallas_call x11, Pallas kernels, on_core(): pl.pallas_call(body, out_shape=[jax.ShapeDtypeStruct(shape, dtype) for sh...  14.2 us
    pallas_call x1, Pallas kernels, weights_in_vmem(): pl.pallas_call(load_weights, out_shape=[pltpu.VMEM(weight.shape, weight.d...  5.19 us
  transfers between devices with their start and end apart: 27, of which 11 were waited for; matrix products, arithmetic and copies ran while one was open for 1% of the time, Pallas kernels for 21%

profile of v5, /device:TPU:0, one launch (start us, length us, event | category | flops | bytes accessed | tf_op | source)
XLA Modules:
  0.0 73.8 jit_solution(16456707001762741724)
XLA Ops:
  0.6 3.2 %collective-permute-start = (bf16[16,4096]{1,0:T(8,128)(2,1)}, bf16[16,4096]{1,0:T(8,128)(2,1)S(1)}, u32[]{:S(2)}, u32[]{:S(2)}) collective-permute-start(bf16[16,4096]{1,0:T(8,128)(2,1)} %tokens_hbm.1), channel_id=1, source_target_pairs={{0,72},{1,73},{2,74},{3,75},{4,76},{5,77},{6,78},{7,79},{64,8},{65... | collective-permute-start | bytes 393224 | tf_op jit(solution)/shard_map/ppermute | solution.py:34
  3.8 4.0 %collective-permute-start.1 = (bf16[16,4096]{1,0:T(8,128)(2,1)}, bf16[16,4096]{1,0:T(8,128)(2,1)S(1)}, u32[]{:S(2)}, u32[]{:S(2)}) collective-permute-start(bf16[16,4096]{1,0:T(8,128)(2,1)} %cotangent_hbm.1), channel_id=1, source_target_pairs={{0,6},{1,7},{2,0},{3,1},{4,2},{5,3},{6,4},{7,5},{64,70},{65,71},{6... | collective-permute-start | bytes 393224 | tf_op jit(solution)/shard_map/ppermute | solution.py:34
  7.8 1.3 %collective-permute-start.3 = (bf16[16,4096]{1,0:T(8,128)(2,1)}, bf16[16,4096]{1,0:T(8,128)(2,1)S(1)}, u32[]{:S(2)}, u32[]{:S(2)}) collective-permute-start(bf16[16,4096]{1,0:T(8,128)(2,1)} %cotangent_hbm.1), channel_id=1, source_target_pairs={{0,2},{1,3},{2,4},{3,5},{4,6},{5,7},{6,0},{7,1},{64,66},{65,67},{6... | collective-permute-start | bytes 393224 | tf_op jit(solution)/shard_map/ppermute | solution.py:34
  9.1 1.0 %shard_map.111 = (bf16[32,4096]{1,0:T(8,128)(2,1)S(1)}, bf16[64,4096]{1,0:T(8,128)(2,1)S(1)}) custom-call(bf16[16,4096]{1,0:T(8,128)(2,1)} %tokens_hbm.1, bf16[16,4096]{1,0:T(8,128)(2,1)} %cotangent_hbm.1), custom_call_target="tpu_custom_call" | custom-call | flops 1000000000 | tf_op jit(solution)/shard_map/pallas_call | solution.py:234
  10.1 2.0 %collective-permute-start.6 = (bf16[32,4096]{1,0:T(8,128)(2,1)S(1)}, bf16[32,4096]{1,0:T(8,128)(2,1)S(1)}, u32[]{:S(2)}, u32[]{:S(2)}) collective-permute-start(bf16[32,4096]{1,0:T(8,128)(2,1)S(1)} %constant_dynamic-update-slice_fusion.3.refs_1_.refs_0_), channel_id=1, source_target_pairs={{0,6},{1,7},{2,0},{3,1},{4,2},{5,3},{6,4},{7,5},{64,70},{65,71},{6... | collective-permute-start | bytes 786440 | tf_op jit(solution)/shard_map/ppermute | solution.py:34
  12.2 2.3 %collective-permute-start.7 = (bf16[32,4096]{1,0:T(8,128)(2,1)S(1)}, bf16[32,4096]{1,0:T(8,128)(2,1)S(1)}, u32[]{:S(2)}, u32[]{:S(2)}) collective-permute-start(bf16[32,4096]{1,0:T(8,128)(2,1)S(1)} %constant_dynamic-update-slice_fusion.3.refs_1_.refs_0_), channel_id=1, source_target_pairs={{0,4},{1,5},{2,6},{3,7},{4,0},{5,1},{6,2},{7,3},{64,68},{65,69},{6... | collective-permute-start | bytes 786440 | tf_op jit(solution)/shard_map/ppermute | solution.py:34
  14.5 1.5 %collective-permute-done.2 = bf16[16,4096]{1,0:T(8,128)(2,1)S(1)} collective-permute-done((bf16[16,4096]{1,0:T(8,128)(2,1)}, bf16[16,4096]{1,0:T(8,128)(2,1)S(1)}, u32[]{:S(2)}, u32[]{:S(2)}) %collective-permute-start.2) | collective-permute-done | bytes 131104 | tf_op jit(solution)/shard_map/ppermute | solution.py:34
  16.0 2.7 %collective-permute-done.3 = bf16[16,4096]{1,0:T(8,128)(2,1)S(1)} collective-permute-done((bf16[16,4096]{1,0:T(8,128)(2,1)}, bf16[16,4096]{1,0:T(8,128)(2,1)S(1)}, u32[]{:S(2)}, u32[]{:S(2)}) %collective-permute-start.3) | collective-permute-done | bytes 131104 | tf_op jit(solution)/shard_map/ppermute | solution.py:34
  19.1 5.2 %shard_map.113 = (bf16[4096,896]{1,0:T(8,128)(2,1)S(1)}, bf16[4096,896]{1,0:T(8,128)(2,1)S(1)}) custom-call(bf16[4096,896]{1,0:T(8,128)(2,1)} %refs_0_, bf16[4096,896]{1,0:T(8,128)(2,1)} %refs_1_.2), custom_call_target="tpu_custom_call" | custom-call | flops 6000000000 | tf_op jit(solution)/shard_map/pallas_call | solution.py:93
  24.3 1.5 %collective-permute-done.9 = bf16[32,4096]{1,0:T(8,128)(2,1)S(1)} collective-permute-done((bf16[32,4096]{1,0:T(8,128)(2,1)S(1)}, bf16[32,4096]{1,0:T(8,128)(2,1)S(1)}, u32[]{:S(2)}, u32[]{:S(2)}) %collective-permute-start.9) | collective-permute-done | bytes 262176 | tf_op jit(solution)/shard_map/ppermute | solution.py:34
  25.8 2.2 %collective-permute-done.8.refs_3_ = bf16[32,4096]{1,0:T(8,128)(2,1)S(1)} collective-permute-done((bf16[32,4096]{1,0:T(8,128)(2,1)S(1)}, bf16[32,4096]{1,0:T(8,128)(2,1)S(1)}, u32[]{:S(2)}, u32[]{:S(2)}) %collective-permute-start.8) | collective-permute-done | bytes 262176 | tf_op jit(solution)/shard_map/ppermute | solution.py:34
  28.0 0.5 collective-permute-start.12
  28.6 0.6 collective-permute-start.5
  29.5 1.5 %collective-permute-start.15 = (f32[32,4096]{1,0:T(8,128)S(1)}, f32[32,4096]{1,0:T(8,128)S(1)}, u32[]{:S(2)}, u32[]{:S(2)}) collective-permute-start(f32[32,4096]{1,0:T(8,128)S(1)} %subtract_add_fusion.refs_0_), channel_id=1, source_target_pairs={{0,16},{1,49},{2,18},{3,51},{4,20},{5,53},{6,22},{7,55},{64,80},{6... | collective-permute-start | bytes 1572872 | tf_op jit(solution)/shard_map/ppermute | solution.py:34
  31.0 1.5 %collective-permute-done.4.refs_10_.refs_1_ = bf16[64,4096]{1,0:T(8,128)(2,1)S(1)} collective-permute-done((bf16[64,4096]{1,0:T(8,128)(2,1)S(1)}, bf16[64,4096]{1,0:T(8,128)(2,1)S(1)}, u32[]{:S(2)}, u32[]{:S(2)}) %collective-permute-start.4) | collective-permute-done | bytes 524320 | tf_op jit(solution)/shard_map/ppermute | solution.py:34
  32.5 4.0 %shard_map.114 = (bf16[256,896]{1,0:T(8,128)(2,1)S(1)}, f32[256,896]{1,0:T(8,128)S(1)}, f32[256,896]{1,0:T(8,128)S(1)}) custom-call(bf16[32,4096]{1,0:T(8,128)(2,1)S(1)} %constant_dynamic-update-slice_fusion.3.refs_1_.refs_0_, bf16[32,4096]{1,0:T(8,128)(2,1)S(1)} %collective-permute-done.6.refs_1_, bf16[32,4096]{1,0:T(8,128)(2,1)S(1)} %collective-permute-done.7.refs_2_, ...), custom_call_target="tpu_custom_call" | custom-call | flops 4000000 | tf_op jit(solution)/shard_map/pallas_call | solution.py:206
  36.6 2.3 %shard_map.115 = (f32[128,4096]{1,0:T(8,128)S(1)}, bf16[128,4096]{1,0:T(8,128)(2,1)S(1)}) custom-call(bf16[256,896]{1,0:T(8,128)(2,1)S(1)} %get-tuple-element.51.refs_0_, bf16[896,4096]{1,0:T(8,128)(2,1)S(1)} %bitcast.2), custom_call_target="tpu_custom_call" | custom-call | flops 4000000 | tf_op jit(solution)/shard_map/pallas_call | solution.py:206
  39.0 0.7 collective-permute-start.16
  39.8 2.4 %shard_map.117.refs_2_.refs_0_ = bf16[256,1792]{1,0:T(8,128)(2,1)S(1)} custom-call(bf16[64,4096]{1,0:T(8,128)(2,1)S(1)} %constant_dynamic-update-slice_fusion.refs_0_, bf16[64,4096]{1,0:T(8,128)(2,1)S(1)} %collective-permute-done.4.refs_10_.refs_1_, bf16[64,4096]{1,0:T(8,128)(2,1)S(1)} %collective-permute-done.5.refs_2_, ...), custom_call_target="tpu_custom_call" | custom-call | flops 6000000000 | tf_op jit(solution)/shard_map/pallas_call | solution.py:206
  42.4 4.0 %shard_map.119 = (f32[128,4096]{1,0:T(8,128)S(1)}, bf16[128,4096]{1,0:T(8,128)(2,1)S(1)}) custom-call(bf16[256,1792]{1,0:T(8,128)(2,1)S(1)} %shard_map.117.refs_2_.refs_0_, bf16[4096,896]{1,0:T(8,128)(2,1)S(1)} %get-tuple-element.50.refs_8_.refs_1_, bf16[4096,896]{1,0:T(8,128)(2,1)S(1)} %get-tuple-element.45.refs_9_.refs_2_, ...), custom_call_target="tpu_custom_call" | custom-call | flops 6000000000 | tf_op jit(solution)/shard_map/pallas_call | solution.py:206
  46.6 2.8 %collective-permute-start.23 = (f32[32,4096]{1,0:T(8,128)S(1)}, f32[32,4096]{1,0:T(8,128)S(1)}, u32[]{:S(2)}, u32[]{:S(2)}) collective-permute-start(f32[32,4096]{1,0:T(8,128)S(1)} %shard_map.116.refs_8_.refs_0_), channel_id=1, source_target_pairs={{0,48},{1,17},{2,50},{3,19},{4,52},{5,21},{6,54},{7,23},{64,112},{... | collective-permute-start | bytes 1572872 | tf_op jit(solution)/shard_map/ppermute | solution.py:34
  49.8 2.9 %collective-permute-start.18 = (bf16[32,4096]{1,0:T(8,128)(2,1)S(1)}, bf16[32,4096]{1,0:T(8,128)(2,1)S(1)}, u32[]{:S(2)}, u32[]{:S(2)}) collective-permute-start(bf16[32,4096]{1,0:T(8,128)(2,1)S(1)} %get-tuple-element.61), channel_id=1, source_target_pairs={{0,4},{1,5},{2,6},{3,7},{4,0},{5,1},{6,2},{7,3},{64,68},{65,69},{6... | collective-permute-start | bytes 786440 | tf_op jit(solution)/shard_map/ppermute | solution.py:34
  52.8 3.2 %collective-permute-start.20 = (bf16[32,4096]{1,0:T(8,128)(2,1)S(1)}, bf16[32,4096]{1,0:T(8,128)(2,1)S(1)}, u32[]{:S(2)}, u32[]{:S(2)}) collective-permute-start(bf16[32,4096]{1,0:T(8,128)(2,1)S(1)} %get-tuple-element.63), channel_id=1, source_target_pairs={{0,6},{1,7},{2,0},{3,1},{4,2},{5,3},{6,4},{7,5},{64,70},{65,71},{6... | collective-permute-start | bytes 786440 | tf_op jit(solution)/shard_map/ppermute | solution.py:34
  56.0 1.0 %collective-permute-done.23.refs_1_ = f32[32,4096]{1,0:T(8,128)S(1)} collective-permute-done((f32[32,4096]{1,0:T(8,128)S(1)}, f32[32,4096]{1,0:T(8,128)S(1)}, u32[]{:S(2)}, u32[]{:S(2)}) %collective-permute-start.23) | collective-permute-done | bytes 524320 | tf_op jit(solution)/shard_map/ppermute | solution.py:34
  57.1 0.9 %multiply_subtract_fusion = (f32[32,4096]{1,0:T(8,128)S(1)}, f32[32,4096]{1,0:T(8,128)}) fusion(f32[32,4096]{1,0:T(8,128)S(1)} %copy-done.1, f32[32,4096]{1,0:T(8,128)S(1)} %shard_map.122, f32[32,4096]{1,0:T(8,128)S(1)} %copy-done.2), kind=kLoop, calls=%fused_computation | loop fusion | flops 917504 | bytes 2621440 | tf_op jit(solution)/shard_map/sub | solution.py:350
  58.0 5.2 %collective-permute-done.22.refs_1_ = bf16[64,4096]{1,0:T(8,128)(2,1)S(1)} collective-permute-done((bf16[64,4096]{1,0:T(8,128)(2,1)S(1)}, bf16[64,4096]{1,0:T(8,128)(2,1)S(1)}, u32[]{:S(2)}, u32[]{:S(2)}) %collective-permute-start.22) | collective-permute-done | bytes 524320 | tf_op jit(solution)/shard_map/ppermute | solution.py:34
  63.4 1.3 %collective-permute-start.25 = (bf16[16,4096]{1,0:T(8,128)(2,1)S(1)}, bf16[16,4096]{1,0:T(8,128)(2,1)S(1)}, u32[]{:S(2)}, u32[]{:S(2)}) collective-permute-start(bf16[16,4096]{1,0:T(8,128)(2,1)S(1)} %get-tuple-element.70), channel_id=1, source_target_pairs={{0,4},{1,5},{2,6},{3,7},{4,0},{5,1},{6,2},{7,3},{64,68},{65,69},{6... | collective-permute-start | bytes 393224 | tf_op jit(solution)/shard_map/ppermute | solution.py:34
  64.7 1.9 %collective-permute-start.26 = (bf16[16,4096]{1,0:T(8,128)(2,1)S(1)}, bf16[16,4096]{1,0:T(8,128)(2,1)S(1)}, u32[]{:S(2)}, u32[]{:S(2)}) collective-permute-start(bf16[16,4096]{1,0:T(8,128)(2,1)S(1)} %get-tuple-element.71), channel_id=1, source_target_pairs={{0,6},{1,7},{2,0},{3,1},{4,2},{5,3},{6,4},{7,5},{64,70},{65,71},{6... | collective-permute-start | bytes 393224 | tf_op jit(solution)/shard_map/ppermute | solution.py:34
  66.7 2.5 %collective-permute-start.21 = (bf16[16,4096]{1,0:T(8,128)(2,1)S(1)}, bf16[16,4096]{1,0:T(8,128)(2,1)S(1)}, u32[]{:S(2)}, u32[]{:S(2)}) collective-permute-start(bf16[16,4096]{1,0:T(8,128)(2,1)S(1)} %get-tuple-element.65), channel_id=1, source_target_pairs={{0,72},{1,73},{2,74},{3,75},{4,76},{5,77},{6,78},{7,79},{64,8},{65... | collective-permute-start | bytes 393224 | tf_op jit(solution)/shard_map/ppermute | solution.py:34
  69.2 2.2 %collective-permute-done.24.refs_3_ = bf16[16,4096]{1,0:T(8,128)(2,1)S(1)} collective-permute-done((bf16[16,4096]{1,0:T(8,128)(2,1)S(1)}, bf16[16,4096]{1,0:T(8,128)(2,1)S(1)}, u32[]{:S(2)}, u32[]{:S(2)}) %collective-permute-start.24) | collective-permute-done | bytes 131104 | tf_op jit(solution)/shard_map/ppermute | solution.py:34
  71.8 1.1 %collective-permute-done.21.refs_1_ = bf16[16,4096]{1,0:T(8,128)(2,1)S(1)} collective-permute-done((bf16[16,4096]{1,0:T(8,128)(2,1)S(1)}, bf16[16,4096]{1,0:T(8,128)(2,1)S(1)}, u32[]{:S(2)}, u32[]{:S(2)}) %collective-permute-start.21) | collective-permute-done | bytes 131104 | tf_op jit(solution)/shard_map/ppermute | solution.py:34
  73.0 0.8 %shard_map.124 = (f32[16,4096]{1,0:T(8,128)}, f32[16,4096]{1,0:T(8,128)}) custom-call(f32[16,4096]{1,0:T(8,128)S(1)} %get-tuple-element.64.refs_0_, bf16[16,4096]{1,0:T(8,128)(2,1)S(1)} %collective-permute-done.21.refs_1_, f32[16,4096]{1,0:T(8,128)S(1)} %get-tuple-element.68.refs_2_, bf16[16,4096]{1,0:T(8,128)(2,1)S(1)} %collective-permute-done.24.refs_3_, ...), custom_call_target="tpu_custom_call" | custom-call | flops 4000000 | tf_op jit(solution)/shard_map/pallas_call | solution.py:206
  (55 shorter events, 2.6 us)
Async XLA Ops:
  0.6 9.5 %collective-permute-start = (bf16[16,4096]{1,0:T(8,128)(2,1)}, bf16[16,4096]{1,0:T(8,128)(2,1)S(1)}, u32[]{:S(2)}, u32[]{:S(2)}) collective-permute-start(bf16[16,4096]{1,0:T(8,128)(2,1)} %tokens_hbm.1), channel_id=1, source_target_pairs={{0,72},{1,73},{2,74},{3,75},{4,76},{5,77},{6,78},{7,79},{64,8},{65... | collective-permute-start | bytes 393224 | tf_op jit(solution)/shard_map/ppermute | solution.py:34
  3.8 10.7 %collective-permute-start.1 = (bf16[16,4096]{1,0:T(8,128)(2,1)}, bf16[16,4096]{1,0:T(8,128)(2,1)S(1)}, u32[]{:S(2)}, u32[]{:S(2)}) collective-permute-start(bf16[16,4096]{1,0:T(8,128)(2,1)} %cotangent_hbm.1), channel_id=1, source_target_pairs={{0,6},{1,7},{2,0},{3,1},{4,2},{5,3},{6,4},{7,5},{64,70},{65,71},{6... | collective-permute-start | bytes 393224 | tf_op jit(solution)/shard_map/ppermute | solution.py:34
  7.8 8.2 %collective-permute-start.2 = (bf16[16,4096]{1,0:T(8,128)(2,1)}, bf16[16,4096]{1,0:T(8,128)(2,1)S(1)}, u32[]{:S(2)}, u32[]{:S(2)}) collective-permute-start(bf16[16,4096]{1,0:T(8,128)(2,1)} %cotangent_hbm.1), channel_id=1, source_target_pairs={{0,4},{1,5},{2,6},{3,7},{4,0},{5,1},{6,2},{7,3},{64,68},{65,69},{6... | collective-permute-start | bytes 393224 | tf_op jit(solution)/shard_map/ppermute | solution.py:34
  7.8 10.9 %collective-permute-start.3 = (bf16[16,4096]{1,0:T(8,128)(2,1)}, bf16[16,4096]{1,0:T(8,128)(2,1)S(1)}, u32[]{:S(2)}, u32[]{:S(2)}) collective-permute-start(bf16[16,4096]{1,0:T(8,128)(2,1)} %cotangent_hbm.1), channel_id=1, source_target_pairs={{0,2},{1,3},{2,4},{3,5},{4,6},{5,7},{6,0},{7,1},{64,66},{65,67},{6... | collective-permute-start | bytes 393224 | tf_op jit(solution)/shard_map/ppermute | solution.py:34
  10.1 15.7 %collective-permute-start.6 = (bf16[32,4096]{1,0:T(8,128)(2,1)S(1)}, bf16[32,4096]{1,0:T(8,128)(2,1)S(1)}, u32[]{:S(2)}, u32[]{:S(2)}) collective-permute-start(bf16[32,4096]{1,0:T(8,128)(2,1)S(1)} %constant_dynamic-update-slice_fusion.3.refs_1_.refs_0_), channel_id=1, source_target_pairs={{0,6},{1,7},{2,0},{3,1},{4,2},{5,3},{6,4},{7,5},{64,70},{65,71},{6... | collective-permute-start | bytes 786440 | tf_op jit(solution)/shard_map/ppermute | solution.py:34
  12.2 13.6 %collective-permute-start.7 = (bf16[32,4096]{1,0:T(8,128)(2,1)S(1)}, bf16[32,4096]{1,0:T(8,128)(2,1)S(1)}, u32[]{:S(2)}, u32[]{:S(2)}) collective-permute-start(bf16[32,4096]{1,0:T(8,128)(2,1)S(1)} %constant_dynamic-update-slice_fusion.3.refs_1_.refs_0_), channel_id=1, source_target_pairs={{0,4},{1,5},{2,6},{3,7},{4,0},{5,1},{6,2},{7,3},{64,68},{65,69},{6... | collective-permute-start | bytes 786440 | tf_op jit(solution)/shard_map/ppermute | solution.py:34
  14.5 4.4 %copy-start.3 = (bf16[1,32,4096]{2,1,0:T(8,128)(2,1)S(1)}, bf16[1,32,4096]{2,1,0:T(8,128)(2,1)}, u32[]{:S(2)}) copy-start(bf16[1,32,4096]{2,1,0:T(8,128)(2,1)} %param.14) | copy-start | bytes 786436
  14.5 13.5 %collective-permute-start.8 = (bf16[32,4096]{1,0:T(8,128)(2,1)S(1)}, bf16[32,4096]{1,0:T(8,128)(2,1)S(1)}, u32[]{:S(2)}, u32[]{:S(2)}) collective-permute-start(bf16[32,4096]{1,0:T(8,128)(2,1)S(1)} %constant_dynamic-update-slice_fusion.3.refs_1_.refs_0_), channel_id=1, source_target_pairs={{0,2},{1,3},{2,4},{3,5},{4,6},{5,7},{6,0},{7,1},{64,66},{65,67},{6... | collective-permute-start | bytes 786440 | tf_op jit(solution)/shard_map/ppermute | solution.py:34
  18.8 13.7 %collective-permute-start.4 = (bf16[64,4096]{1,0:T(8,128)(2,1)S(1)}, bf16[64,4096]{1,0:T(8,128)(2,1)S(1)}, u32[]{:S(2)}, u32[]{:S(2)}) collective-permute-start(bf16[64,4096]{1,0:T(8,128)(2,1)S(1)} %constant_dynamic-update-slice_fusion.refs_0_), channel_id=1, source_target_pairs={{0,72},{1,73},{2,74},{3,75},{4,76},{5,77},{6,78},{7,79},{64,8},{65... | collective-permute-start | bytes 1572872 | tf_op jit(solution)/shard_map/ppermute | solution.py:34
  18.9 9.6 %copy-start.1 = (f32[32,4096]{1,0:T(8,128)S(1)}, f32[32,4096]{1,0:T(8,128)}, u32[]{:S(2)}) copy-start(f32[32,4096]{1,0:T(8,128)} %param.13) | copy-start | bytes 1572868
  18.9 6.9 %collective-permute-start.9 = (bf16[32,4096]{1,0:T(8,128)(2,1)S(1)}, bf16[32,4096]{1,0:T(8,128)(2,1)S(1)}, u32[]{:S(2)}, u32[]{:S(2)}) collective-permute-start(bf16[32,4096]{1,0:T(8,128)(2,1)S(1)} %bitcast.3), channel_id=1, source_target_pairs={{0,64},{1,65},{2,66},{3,67},{4,68},{5,69},{6,70},{7,71},{64,0},{65... | collective-permute-start | bytes 786440 | tf_op jit(solution)/shard_map/ppermute | solution.py:34
  25.8 2.8 %collective-permute-start.10 = (bf16[32,4096]{1,0:T(8,128)(2,1)S(1)}, bf16[32,4096]{1,0:T(8,128)(2,1)S(1)}, u32[]{:S(2)}, u32[]{:S(2)}) collective-permute-start(bf16[32,4096]{1,0:T(8,128)(2,1)S(1)} %constant_dynamic-update-slice_fusion.3.refs_1_.refs_0_), channel_id=1, source_target_pairs={{0,1},{1,0},{2,3},{3,2},{4,5},{5,4},{6,7},{7,6},{64,65},{65,64},{6... | collective-permute-start | bytes 786440 | tf_op jit(solution)/shard_map/ppermute | solution.py:34
  28.0 1.5 %collective-permute-start.11 = (bf16[32,4096]{1,0:T(8,128)(2,1)S(1)}, bf16[32,4096]{1,0:T(8,128)(2,1)S(1)}, u32[]{:S(2)}, u32[]{:S(2)}) collective-permute-start(bf16[32,4096]{1,0:T(8,128)(2,1)S(1)} %collective-permute-done.6.refs_1_), channel_id=1, source_target_pairs={{0,1},{1,0},{2,3},{3,2},{4,5},{5,4},{6,7},{7,6},{64,65},{65,64},{6... | collective-permute-start | bytes 786440 | tf_op jit(solution)/shard_map/ppermute | solution.py:34
  28.0 3.0 %collective-permute-start.12 = (bf16[32,4096]{1,0:T(8,128)(2,1)S(1)}, bf16[32,4096]{1,0:T(8,128)(2,1)S(1)}, u32[]{:S(2)}, u32[]{:S(2)}) collective-permute-start(bf16[32,4096]{1,0:T(8,128)(2,1)S(1)} %collective-permute-done.7.refs_2_), channel_id=1, source_target_pairs={{0,1},{1,0},{2,3},{3,2},{4,5},{5,4},{6,7},{7,6},{64,65},{65,64},{6... | collective-permute-start | bytes 786440 | tf_op jit(solution)/shard_map/ppermute | solution.py:34
  28.5 2.5 %collective-permute-start.13 = (bf16[32,4096]{1,0:T(8,128)(2,1)S(1)}, bf16[32,4096]{1,0:T(8,128)(2,1)S(1)}, u32[]{:S(2)}, u32[]{:S(2)}) collective-permute-start(bf16[32,4096]{1,0:T(8,128)(2,1)S(1)} %collective-permute-done.8.refs_3_), channel_id=1, source_target_pairs={{0,1},{1,0},{2,3},{3,2},{4,5},{5,4},{6,7},{7,6},{64,65},{65,64},{6... | collective-permute-start | bytes 786440 | tf_op jit(solution)/shard_map/ppermute | solution.py:34
  28.5 8.1 %slice-start = ((s8[7340032]{0:T(1024)(128)(4,1)}), s8[4194304]{0:T(1024)(128)(4,1)S(1)}, s32[]{:S(2)}) async-start(s8[7340032]{0:T(1024)(128)(4,1)} %bitcast.1), calls=%async_computation | async-start | bytes 8388608
  28.6 11.2 %collective-permute-start.5 = (bf16[64,4096]{1,0:T(8,128)(2,1)S(1)}, bf16[64,4096]{1,0:T(8,128)(2,1)S(1)}, u32[]{:S(2)}, u32[]{:S(2)}) collective-permute-start(bf16[64,4096]{1,0:T(8,128)(2,1)S(1)} %constant_dynamic-update-slice_fusion.refs_0_), channel_id=1, source_target_pairs={{0,1},{1,0},{2,3},{3,2},{4,5},{5,4},{6,7},{7,6},{64,65},{65,64},{6... | collective-permute-start | bytes 1572872 | tf_op jit(solution)/shard_map/ppermute | solution.py:34
  29.5 10.2 %collective-permute-start.15 = (f32[32,4096]{1,0:T(8,128)S(1)}, f32[32,4096]{1,0:T(8,128)S(1)}, u32[]{:S(2)}, u32[]{:S(2)}) collective-permute-start(f32[32,4096]{1,0:T(8,128)S(1)} %subtract_add_fusion.refs_0_), channel_id=1, source_target_pairs={{0,16},{1,49},{2,18},{3,51},{4,20},{5,53},{6,22},{7,55},{64,80},{6... | collective-permute-start | bytes 1572872 | tf_op jit(solution)/shard_map/ppermute | solution.py:34
  36.5 3.3 %collective-permute-start.14 = (bf16[64,4096]{1,0:T(8,128)(2,1)S(1)}, bf16[64,4096]{1,0:T(8,128)(2,1)S(1)}, u32[]{:S(2)}, u32[]{:S(2)}) collective-permute-start(bf16[64,4096]{1,0:T(8,128)(2,1)S(1)} %collective-permute-done.4.refs_10_.refs_1_), channel_id=1, source_target_pairs={{0,1},{1,0},{2,3},{3,2},{4,5},{5,4},{6,7},{7,6},{64,65},{65,64},{6... | collective-permute-start | bytes 1572872 | tf_op jit(solution)/shard_map/ppermute | solution.py:34
  39.0 3.2 %collective-permute-start.16 = (bf16[128,4096]{1,0:T(8,128)(2,1)S(1)}, bf16[128,4096]{1,0:T(8,128)(2,1)S(1)}, u32[]{:S(2)}, u32[]{:S(2)}) collective-permute-start(bf16[128,4096]{1,0:T(8,128)(2,1)S(1)} %get-tuple-element.55.refs_2_.refs_7_), channel_id=1, source_target_pairs={{0,1},{1,0},{2,3},{3,2},{4,5},{5,4},{6,7},{7,6},{64,65},{65,64},{6... | collective-permute-start | bytes 3145736 | tf_op jit(solution)/shard_map/ppermute | solution.py:34
  42.3 14.7 %copy-start.2 = (f32[32,4096]{1,0:T(8,128)S(1)}, f32[32,4096]{1,0:T(8,128)}, u32[]{:S(2)}) copy-start(f32[32,4096]{1,0:T(8,128)} %param.15) | copy-start | bytes 1572868
  46.3 3.3 %collective-permute-start.17 = (bf16[128,4096]{1,0:T(8,128)(2,1)S(1)}, bf16[128,4096]{1,0:T(8,128)(2,1)S(1)}, u32[]{:S(2)}, u32[]{:S(2)}) collective-permute-start(bf16[128,4096]{1,0:T(8,128)(2,1)S(1)} %get-tuple-element.59), channel_id=1, source_target_pairs={{0,1},{1,0},{2,3},{3,2},{4,5},{5,4},{6,7},{7,6},{64,65},{65,64},{6... | collective-permute-start | bytes 3145736 | tf_op jit(solution)/shard_map/ppermute | solution.py:34
  46.6 10.4 %collective-permute-start.23 = (f32[32,4096]{1,0:T(8,128)S(1)}, f32[32,4096]{1,0:T(8,128)S(1)}, u32[]{:S(2)}, u32[]{:S(2)}) collective-permute-start(f32[32,4096]{1,0:T(8,128)S(1)} %shard_map.116.refs_8_.refs_0_), channel_id=1, source_target_pairs={{0,48},{1,17},{2,50},{3,19},{4,52},{5,21},{6,54},{7,23},{64,112},{... | collective-permute-start | bytes 1572872 | tf_op jit(solution)/shard_map/ppermute | solution.py:34
  49.4 13.8 %collective-permute-start.22 = (bf16[64,4096]{1,0:T(8,128)(2,1)S(1)}, bf16[64,4096]{1,0:T(8,128)(2,1)S(1)}, u32[]{:S(2)}, u32[]{:S(2)}) collective-permute-start(bf16[64,4096]{1,0:T(8,128)(2,1)S(1)} %get-tuple-element.57.refs_3_), channel_id=1, source_target_pairs={{0,72},{1,73},{2,74},{3,75},{4,76},{5,77},{6,78},{7,79},{64,8},{65... | collective-permute-start | bytes 1572872 | tf_op jit(solution)/shard_map/ppermute | solution.py:34
  49.8 14.9 %collective-permute-start.18 = (bf16[32,4096]{1,0:T(8,128)(2,1)S(1)}, bf16[32,4096]{1,0:T(8,128)(2,1)S(1)}, u32[]{:S(2)}, u32[]{:S(2)}) collective-permute-start(bf16[32,4096]{1,0:T(8,128)(2,1)S(1)} %get-tuple-element.61), channel_id=1, source_target_pairs={{0,4},{1,5},{2,6},{3,7},{4,0},{5,1},{6,2},{7,3},{64,68},{65,69},{6... | collective-permute-start | bytes 786440 | tf_op jit(solution)/shard_map/ppermute | solution.py:34
  52.8 13.8 %collective-permute-start.19 = (bf16[32,4096]{1,0:T(8,128)(2,1)S(1)}, bf16[32,4096]{1,0:T(8,128)(2,1)S(1)}, u32[]{:S(2)}, u32[]{:S(2)}) collective-permute-start(bf16[32,4096]{1,0:T(8,128)(2,1)S(1)} %get-tuple-element.62.refs_2_), channel_id=1, source_target_pairs={{0,2},{1,3},{2,4},{3,5},{4,6},{5,7},{6,0},{7,1},{64,66},{65,67},{6... | collective-permute-start | bytes 786440 | tf_op jit(solution)/shard_map/ppermute | solution.py:34
  52.8 13.8 %collective-permute-start.20 = (bf16[32,4096]{1,0:T(8,128)(2,1)S(1)}, bf16[32,4096]{1,0:T(8,128)(2,1)S(1)}, u32[]{:S(2)}, u32[]{:S(2)}) collective-permute-start(bf16[32,4096]{1,0:T(8,128)(2,1)S(1)} %get-tuple-element.63), channel_id=1, source_target_pairs={{0,6},{1,7},{2,0},{3,1},{4,2},{5,3},{6,4},{7,5},{64,70},{65,71},{6... | collective-permute-start | bytes 786440 | tf_op jit(solution)/shard_map/ppermute | solution.py:34
  58.0 5.3 %copy-start = (f32[32,4096]{1,0:T(8,128)}, f32[32,4096]{1,0:T(8,128)S(1)}, u32[]{:S(2)}) copy-start(f32[32,4096]{1,0:T(8,128)S(1)} %get-tuple-element.74.refs_3_) | copy-start | bytes 1572868
  63.3 8.1 %collective-permute-start.24 = (bf16[16,4096]{1,0:T(8,128)(2,1)S(1)}, bf16[16,4096]{1,0:T(8,128)(2,1)S(1)}, u32[]{:S(2)}, u32[]{:S(2)}) collective-permute-start(bf16[16,4096]{1,0:T(8,128)(2,1)S(1)} %get-tuple-element.69), channel_id=1, source_target_pairs={{0,2},{1,3},{2,4},{3,5},{4,6},{5,7},{6,0},{7,1},{64,66},{65,67},{6... | collective-permute-start | bytes 393224 | tf_op jit(solution)/shard_map/ppermute | solution.py:34
  63.4 8.1 %collective-permute-start.25 = (bf16[16,4096]{1,0:T(8,128)(2,1)S(1)}, bf16[16,4096]{1,0:T(8,128)(2,1)S(1)}, u32[]{:S(2)}, u32[]{:S(2)}) collective-permute-start(bf16[16,4096]{1,0:T(8,128)(2,1)S(1)} %get-tuple-element.70), channel_id=1, source_target_pairs={{0,4},{1,5},{2,6},{3,7},{4,0},{5,1},{6,2},{7,3},{64,68},{65,69},{6... | collective-permute-start | bytes 393224 | tf_op jit(solution)/shard_map/ppermute | solution.py:34
  64.7 7.1 %collective-permute-start.26 = (bf16[16,4096]{1,0:T(8,128)(2,1)S(1)}, bf16[16,4096]{1,0:T(8,128)(2,1)S(1)}, u32[]{:S(2)}, u32[]{:S(2)}) collective-permute-start(bf16[16,4096]{1,0:T(8,128)(2,1)S(1)} %get-tuple-element.71), channel_id=1, source_target_pairs={{0,6},{1,7},{2,0},{3,1},{4,2},{5,3},{6,4},{7,5},{64,70},{65,71},{6... | collective-permute-start | bytes 393224 | tf_op jit(solution)/shard_map/ppermute | solution.py:34
  66.7 6.3 %collective-permute-start.21 = (bf16[16,4096]{1,0:T(8,128)(2,1)S(1)}, bf16[16,4096]{1,0:T(8,128)(2,1)S(1)}, u32[]{:S(2)}, u32[]{:S(2)}) collective-permute-start(bf16[16,4096]{1,0:T(8,128)(2,1)S(1)} %get-tuple-element.65), channel_id=1, source_target_pairs={{0,72},{1,73},{2,74},{3,75},{4,76},{5,77},{6,78},{7,79},{64,8},{65... | collective-permute-start | bytes 393224 | tf_op jit(solution)/shard_map/ppermute | solution.py:34
  (1 other events, 4.1 us)

commit v6 on v5

--- a/solution.py
+++ b/solution.py
@@ -275,9 +275,11 @@
     across = swap_y(line)
     local = after(local_frag[0], line)
     local_next = swap_y_low(local)
-    gate, up = weights_in_vmem(after(w_gate, line), w_up)
-    down = pltpu.with_memory_space_constraint(w_down, pltpu.VMEM)
-    token_arrived = tie(*token_arrived, up, local_next)[:3]
+    (gate,) = weights_in_vmem(after(w_gate, line))
+    up, down = [
+        pltpu.with_memory_space_constraint(weight, pltpu.VMEM) for weight in (w_up, w_down)
+    ]
+    token_arrived = tie(*token_arrived, gate, local_next)[:3]
     pseudo = (outer_frag - full(local)) + (outer_frag - full(local_next))
     token_near = [both, *token_arrived]
     token_far = [swap_core(piece) for piece in token_near]
@@ -325,7 +327,7 @@
     out_across = swap_y(out_sent)
     grad_here, grad_there = on_core(
         grad_kernel,
-        LONG,
+        SHORT,
         [((128, width), F32), ((128, width), BF16)],
         grads,
         gate,
@@ -350,7 +352,7 @@
     new_outer = outer_frag - outer_rate * (mean_delta + outer_beta * new_momentum)
     out_line, *out_sent = on_core(
         line_kernel,
-        LONG,
+        SHORT,
         [((16, width), F32)] + [((16, width), BF16)] * 3,
         out_keep,
         out_across,

time: 74 us -> 74 us (level)
  Pallas kernels: 20.3 us -> 18.4 us
  waiting for transfers between devices: 19.7 us -> 21.4 us
    pallas_call x1, Pallas kernels: 5.19 us -> 3.24 us  [weights_in_vmem(): pl.pallas_call(load_weights, out_shape=[pltpu.VMEM(weight.shape, weight.d...]
    ppermute x27, waiting for transfers between devices: 19.7 us -> 21.4 us  [send(): return lax.ppermute(rows, AXES, pairs(move))]
  transfers between devices with their start and end apart: 27 -> 27, of which waited for: 11 -> 11; matrix products, arithmetic and copies ran while one was open for 1% -> 1% of each run, Pallas kernels for 21% -> 18%
where the time goes in v6:
time: 74 us; the launch traced here: 73.8 us
  starting transfers between devices  32 us (43%)
  waiting for transfers between devices  21.4 us (29%)
  Pallas kernels  18.4 us (25%)
  other arithmetic  1.02 us (1%)
  between operations  0.92 us (1%)
    ppermute x27, starting transfers between devices, send(): return lax.ppermute(rows, AXES, pairs(move))  32 us
    ppermute x27, waiting for transfers between devices, send(): return lax.ppermute(rows, AXES, pairs(move))  21.4 us
    pallas_call x11, Pallas kernels, on_core(): pl.pallas_call(body, out_shape=[jax.ShapeDtypeStruct(shape, dtype) for sh...  14.2 us
    pallas_call x1, Pallas kernels, weights_in_vmem(): pl.pallas_call(load_weights, out_shape=[pltpu.VMEM(weight.shape, weight.d...  3.24 us
  transfers between devices with their start and end apart: 27, of which 11 were waited for; matrix products, arithmetic and copies ran while one was open for 1% of the time, Pallas kernels for 18%

profile of v6, /device:TPU:0, one launch (start us, length us, event | category | flops | bytes accessed | tf_op | source)
XLA Modules:
  0.0 73.8 jit_solution(15023787290378262556)
XLA Ops:
  0.6 3.2 %collective-permute-start = (bf16[16,4096]{1,0:T(8,128)(2,1)}, bf16[16,4096]{1,0:T(8,128)(2,1)S(1)}, u32[]{:S(2)}, u32[]{:S(2)}) collective-permute-start(bf16[16,4096]{1,0:T(8,128)(2,1)} %tokens_hbm.1), channel_id=1, source_target_pairs={{0,72},{1,73},{2,74},{3,75},{4,76},{5,77},{6,78},{7,79},{64,8},{65... | collective-permute-start | bytes 393224 | tf_op jit(solution)/shard_map/ppermute | solution.py:34
  3.8 4.0 %collective-permute-start.1 = (bf16[16,4096]{1,0:T(8,128)(2,1)}, bf16[16,4096]{1,0:T(8,128)(2,1)S(1)}, u32[]{:S(2)}, u32[]{:S(2)}) collective-permute-start(bf16[16,4096]{1,0:T(8,128)(2,1)} %cotangent_hbm.1), channel_id=1, source_target_pairs={{0,6},{1,7},{2,0},{3,1},{4,2},{5,3},{6,4},{7,5},{64,70},{65,71},{6... | collective-permute-start | bytes 393224 | tf_op jit(solution)/shard_map/ppermute | solution.py:34
  7.8 1.3 %collective-permute-start.3 = (bf16[16,4096]{1,0:T(8,128)(2,1)}, bf16[16,4096]{1,0:T(8,128)(2,1)S(1)}, u32[]{:S(2)}, u32[]{:S(2)}) collective-permute-start(bf16[16,4096]{1,0:T(8,128)(2,1)} %cotangent_hbm.1), channel_id=1, source_target_pairs={{0,2},{1,3},{2,4},{3,5},{4,6},{5,7},{6,0},{7,1},{64,66},{65,67},{6... | collective-permute-start | bytes 393224 | tf_op jit(solution)/shard_map/ppermute | solution.py:34
  9.1 1.0 %shard_map.111 = (bf16[32,4096]{1,0:T(8,128)(2,1)S(1)}, bf16[64,4096]{1,0:T(8,128)(2,1)S(1)}) custom-call(bf16[16,4096]{1,0:T(8,128)(2,1)} %tokens_hbm.1, bf16[16,4096]{1,0:T(8,128)(2,1)} %cotangent_hbm.1), custom_call_target="tpu_custom_call" | custom-call | flops 1000000000 | tf_op jit(solution)/shard_map/pallas_call | solution.py:234
  10.1 2.0 %collective-permute-start.6 = (bf16[32,4096]{1,0:T(8,128)(2,1)S(1)}, bf16[32,4096]{1,0:T(8,128)(2,1)S(1)}, u32[]{:S(2)}, u32[]{:S(2)}) collective-permute-start(bf16[32,4096]{1,0:T(8,128)(2,1)S(1)} %constant_dynamic-update-slice_fusion.3.refs_1_.refs_0_), channel_id=1, source_target_pairs={{0,6},{1,7},{2,0},{3,1},{4,2},{5,3},{6,4},{7,5},{64,70},{65,71},{6... | collective-permute-start | bytes 786440 | tf_op jit(solution)/shard_map/ppermute | solution.py:34
  12.2 2.3 %collective-permute-start.7 = (bf16[32,4096]{1,0:T(8,128)(2,1)S(1)}, bf16[32,4096]{1,0:T(8,128)(2,1)S(1)}, u32[]{:S(2)}, u32[]{:S(2)}) collective-permute-start(bf16[32,4096]{1,0:T(8,128)(2,1)S(1)} %constant_dynamic-update-slice_fusion.3.refs_1_.refs_0_), channel_id=1, source_target_pairs={{0,4},{1,5},{2,6},{3,7},{4,0},{5,1},{6,2},{7,3},{64,68},{65,69},{6... | collective-permute-start | bytes 786440 | tf_op jit(solution)/shard_map/ppermute | solution.py:34
  14.5 1.5 %collective-permute-done.2 = bf16[16,4096]{1,0:T(8,128)(2,1)S(1)} collective-permute-done((bf16[16,4096]{1,0:T(8,128)(2,1)}, bf16[16,4096]{1,0:T(8,128)(2,1)S(1)}, u32[]{:S(2)}, u32[]{:S(2)}) %collective-permute-start.2) | collective-permute-done | bytes 131104 | tf_op jit(solution)/shard_map/ppermute | solution.py:34
  16.0 2.7 %collective-permute-done.3 = bf16[16,4096]{1,0:T(8,128)(2,1)S(1)} collective-permute-done((bf16[16,4096]{1,0:T(8,128)(2,1)}, bf16[16,4096]{1,0:T(8,128)(2,1)S(1)}, u32[]{:S(2)}, u32[]{:S(2)}) %collective-permute-start.3) | collective-permute-done | bytes 131104 | tf_op jit(solution)/shard_map/ppermute | solution.py:34
  19.1 3.2 %shard_map.113.refs_8_.refs_1_ = bf16[4096,896]{1,0:T(8,128)(2,1)S(1)} custom-call(bf16[4096,896]{1,0:T(8,128)(2,1)} %refs_0_), custom_call_target="tpu_custom_call" | custom-call | flops 6000000000 | tf_op jit(solution)/shard_map/pallas_call | solution.py:93
  22.4 3.4 %collective-permute-done.9 = bf16[32,4096]{1,0:T(8,128)(2,1)S(1)} collective-permute-done((bf16[32,4096]{1,0:T(8,128)(2,1)S(1)}, bf16[32,4096]{1,0:T(8,128)(2,1)S(1)}, u32[]{:S(2)}, u32[]{:S(2)}) %collective-permute-start.9) | collective-permute-done | bytes 262176 | tf_op jit(solution)/shard_map/ppermute | solution.py:34
  25.8 2.2 %collective-permute-done.8.refs_3_ = bf16[32,4096]{1,0:T(8,128)(2,1)S(1)} collective-permute-done((bf16[32,4096]{1,0:T(8,128)(2,1)S(1)}, bf16[32,4096]{1,0:T(8,128)(2,1)S(1)}, u32[]{:S(2)}, u32[]{:S(2)}) %collective-permute-start.8) | collective-permute-done | bytes 262176 | tf_op jit(solution)/shard_map/ppermute | solution.py:34
  28.0 0.5 collective-permute-start.12
  28.6 0.6 collective-permute-start.5
  29.5 1.5 %collective-permute-start.15 = (f32[32,4096]{1,0:T(8,128)S(1)}, f32[32,4096]{1,0:T(8,128)S(1)}, u32[]{:S(2)}, u32[]{:S(2)}) collective-permute-start(f32[32,4096]{1,0:T(8,128)S(1)} %subtract_add_fusion.refs_0_), channel_id=1, source_target_pairs={{0,16},{1,49},{2,18},{3,51},{4,20},{5,53},{6,22},{7,55},{64,80},{6... | collective-permute-start | bytes 1572872 | tf_op jit(solution)/shard_map/ppermute | solution.py:34
  31.0 1.5 %collective-permute-done.4.refs_10_.refs_1_ = bf16[64,4096]{1,0:T(8,128)(2,1)S(1)} collective-permute-done((bf16[64,4096]{1,0:T(8,128)(2,1)S(1)}, bf16[64,4096]{1,0:T(8,128)(2,1)S(1)}, u32[]{:S(2)}, u32[]{:S(2)}) %collective-permute-start.4) | collective-permute-done | bytes 524320 | tf_op jit(solution)/shard_map/ppermute | solution.py:34
  32.5 4.0 %shard_map.114 = (bf16[256,896]{1,0:T(8,128)(2,1)S(1)}, f32[256,896]{1,0:T(8,128)S(1)}, f32[256,896]{1,0:T(8,128)S(1)}) custom-call(bf16[32,4096]{1,0:T(8,128)(2,1)S(1)} %constant_dynamic-update-slice_fusion.3.refs_1_.refs_0_, bf16[32,4096]{1,0:T(8,128)(2,1)S(1)} %collective-permute-done.6.refs_1_, bf16[32,4096]{1,0:T(8,128)(2,1)S(1)} %collective-permute-done.7.refs_2_, ...), custom_call_target="tpu_custom_call" | custom-call | flops 4000000 | tf_op jit(solution)/shard_map/pallas_call | solution.py:206
  36.6 2.3 %shard_map.115 = (f32[128,4096]{1,0:T(8,128)S(1)}, bf16[128,4096]{1,0:T(8,128)(2,1)S(1)}) custom-call(bf16[256,896]{1,0:T(8,128)(2,1)S(1)} %get-tuple-element.47.refs_0_, bf16[896,4096]{1,0:T(8,128)(2,1)S(1)} %bitcast.4), custom_call_target="tpu_custom_call" | custom-call | flops 4000000 | tf_op jit(solution)/shard_map/pallas_call | solution.py:206
  39.0 0.7 collective-permute-start.16
  39.8 2.4 %shard_map.117.refs_2_.refs_0_ = bf16[256,1792]{1,0:T(8,128)(2,1)S(1)} custom-call(bf16[64,4096]{1,0:T(8,128)(2,1)S(1)} %constant_dynamic-update-slice_fusion.refs_0_, bf16[64,4096]{1,0:T(8,128)(2,1)S(1)} %collective-permute-done.4.refs_10_.refs_1_, bf16[64,4096]{1,0:T(8,128)(2,1)S(1)} %collective-permute-done.5.refs_2_, ...), custom_call_target="tpu_custom_call" | custom-call | flops 6000000000 | tf_op jit(solution)/shard_map/pallas_call | solution.py:206
  42.4 4.0 %shard_map.119 = (f32[128,4096]{1,0:T(8,128)S(1)}, bf16[128,4096]{1,0:T(8,128)(2,1)S(1)}) custom-call(bf16[256,1792]{1,0:T(8,128)(2,1)S(1)} %shard_map.117.refs_2_.refs_0_, bf16[4096,896]{1,0:T(8,128)(2,1)S(1)} %shard_map.113.refs_8_.refs_1_, bf16[4096,896]{1,0:T(8,128)(2,1)S(1)} %bitcast.2, bf16[64,4096]{1,0:T(8,128)(2,1)S(1)} %get-tuple-element.53.refs_3_), custom_call_target="tpu_custom_call" | custom-call | flops 4000000 | tf_op jit(solution)/shard_map/pallas_call | solution.py:206
  46.6 2.8 %collective-permute-start.23 = (f32[32,4096]{1,0:T(8,128)S(1)}, f32[32,4096]{1,0:T(8,128)S(1)}, u32[]{:S(2)}, u32[]{:S(2)}) collective-permute-start(f32[32,4096]{1,0:T(8,128)S(1)} %shard_map.116.refs_8_.refs_0_), channel_id=1, source_target_pairs={{0,48},{1,17},{2,50},{3,19},{4,52},{5,21},{6,54},{7,23},{64,112},{... | collective-permute-start | bytes 1572872 | tf_op jit(solution)/shard_map/ppermute | solution.py:34
  49.8 3.0 %collective-permute-start.18 = (bf16[32,4096]{1,0:T(8,128)(2,1)S(1)}, bf16[32,4096]{1,0:T(8,128)(2,1)S(1)}, u32[]{:S(2)}, u32[]{:S(2)}) collective-permute-start(bf16[32,4096]{1,0:T(8,128)(2,1)S(1)} %get-tuple-element.57), channel_id=1, source_target_pairs={{0,4},{1,5},{2,6},{3,7},{4,0},{5,1},{6,2},{7,3},{64,68},{65,69},{6... | collective-permute-start | bytes 786440 | tf_op jit(solution)/shard_map/ppermute | solution.py:34
  52.9 3.2 %collective-permute-start.20 = (bf16[32,4096]{1,0:T(8,128)(2,1)S(1)}, bf16[32,4096]{1,0:T(8,128)(2,1)S(1)}, u32[]{:S(2)}, u32[]{:S(2)}) collective-permute-start(bf16[32,4096]{1,0:T(8,128)(2,1)S(1)} %get-tuple-element.59), channel_id=1, source_target_pairs={{0,6},{1,7},{2,0},{3,1},{4,2},{5,3},{6,4},{7,5},{64,70},{65,71},{6... | collective-permute-start | bytes 786440 | tf_op jit(solution)/shard_map/ppermute | solution.py:34
  56.1 0.9 %collective-permute-done.23.refs_1_ = f32[32,4096]{1,0:T(8,128)S(1)} collective-permute-done((f32[32,4096]{1,0:T(8,128)S(1)}, f32[32,4096]{1,0:T(8,128)S(1)}, u32[]{:S(2)}, u32[]{:S(2)}) %collective-permute-start.23) | collective-permute-done | bytes 524320 | tf_op jit(solution)/shard_map/ppermute | solution.py:34
  57.1 0.9 %multiply_subtract_fusion = (f32[32,4096]{1,0:T(8,128)S(1)}, f32[32,4096]{1,0:T(8,128)}) fusion(f32[32,4096]{1,0:T(8,128)S(1)} %copy-done.1, f32[32,4096]{1,0:T(8,128)S(1)} %shard_map.122, f32[32,4096]{1,0:T(8,128)S(1)} %copy-done.2), kind=kLoop, calls=%fused_computation | loop fusion | flops 917504 | bytes 2621440 | tf_op jit(solution)/shard_map/sub | solution.py:352
  58.0 5.2 %collective-permute-done.22.refs_1_ = bf16[64,4096]{1,0:T(8,128)(2,1)S(1)} collective-permute-done((bf16[64,4096]{1,0:T(8,128)(2,1)S(1)}, bf16[64,4096]{1,0:T(8,128)(2,1)S(1)}, u32[]{:S(2)}, u32[]{:S(2)}) %collective-permute-start.22) | collective-permute-done | bytes 524320 | tf_op jit(solution)/shard_map/ppermute | solution.py:34
  63.4 1.3 %collective-permute-start.25 = (bf16[16,4096]{1,0:T(8,128)(2,1)S(1)}, bf16[16,4096]{1,0:T(8,128)(2,1)S(1)}, u32[]{:S(2)}, u32[]{:S(2)}) collective-permute-start(bf16[16,4096]{1,0:T(8,128)(2,1)S(1)} %get-tuple-element.66), channel_id=1, source_target_pairs={{0,4},{1,5},{2,6},{3,7},{4,0},{5,1},{6,2},{7,3},{64,68},{65,69},{6... | collective-permute-start | bytes 393224 | tf_op jit(solution)/shard_map/ppermute | solution.py:34
  64.7 1.9 %collective-permute-start.26 = (bf16[16,4096]{1,0:T(8,128)(2,1)S(1)}, bf16[16,4096]{1,0:T(8,128)(2,1)S(1)}, u32[]{:S(2)}, u32[]{:S(2)}) collective-permute-start(bf16[16,4096]{1,0:T(8,128)(2,1)S(1)} %get-tuple-element.67), channel_id=1, source_target_pairs={{0,6},{1,7},{2,0},{3,1},{4,2},{5,3},{6,4},{7,5},{64,70},{65,71},{6... | collective-permute-start | bytes 393224 | tf_op jit(solution)/shard_map/ppermute | solution.py:34
  66.7 2.6 %collective-permute-start.21 = (bf16[16,4096]{1,0:T(8,128)(2,1)S(1)}, bf16[16,4096]{1,0:T(8,128)(2,1)S(1)}, u32[]{:S(2)}, u32[]{:S(2)}) collective-permute-start(bf16[16,4096]{1,0:T(8,128)(2,1)S(1)} %get-tuple-element.61), channel_id=1, source_target_pairs={{0,72},{1,73},{2,74},{3,75},{4,76},{5,77},{6,78},{7,79},{64,8},{65... | collective-permute-start | bytes 393224 | tf_op jit(solution)/shard_map/ppermute | solution.py:34
  69.3 2.1 %collective-permute-done.24.refs_3_ = bf16[16,4096]{1,0:T(8,128)(2,1)S(1)} collective-permute-done((bf16[16,4096]{1,0:T(8,128)(2,1)S(1)}, bf16[16,4096]{1,0:T(8,128)(2,1)S(1)}, u32[]{:S(2)}, u32[]{:S(2)}) %collective-permute-start.24) | collective-permute-done | bytes 131104 | tf_op jit(solution)/shard_map/ppermute | solution.py:34
  71.8 1.1 %collective-permute-done.21.refs_1_ = bf16[16,4096]{1,0:T(8,128)(2,1)S(1)} collective-permute-done((bf16[16,4096]{1,0:T(8,128)(2,1)S(1)}, bf16[16,4096]{1,0:T(8,128)(2,1)S(1)}, u32[]{:S(2)}, u32[]{:S(2)}) %collective-permute-start.21) | collective-permute-done | bytes 131104 | tf_op jit(solution)/shard_map/ppermute | solution.py:34
  73.0 0.8 %shard_map.124 = (f32[16,4096]{1,0:T(8,128)}, f32[16,4096]{1,0:T(8,128)}) custom-call(f32[16,4096]{1,0:T(8,128)S(1)} %get-tuple-element.60.refs_0_, bf16[16,4096]{1,0:T(8,128)(2,1)S(1)} %collective-permute-done.21.refs_1_, f32[16,4096]{1,0:T(8,128)S(1)} %get-tuple-element.64.refs_2_, bf16[16,4096]{1,0:T(8,128)(2,1)S(1)} %collective-permute-done.24.refs_3_, ...), custom_call_target="tpu_custom_call" | custom-call | flops 4000000 | tf_op jit(solution)/shard_map/pallas_call | solution.py:206
  (60 shorter events, 2.6 us)
Async XLA Ops:
  0.6 9.5 %collective-permute-start = (bf16[16,4096]{1,0:T(8,128)(2,1)}, bf16[16,4096]{1,0:T(8,128)(2,1)S(1)}, u32[]{:S(2)}, u32[]{:S(2)}) collective-permute-start(bf16[16,4096]{1,0:T(8,128)(2,1)} %tokens_hbm.1), channel_id=1, source_target_pairs={{0,72},{1,73},{2,74},{3,75},{4,76},{5,77},{6,78},{7,79},{64,8},{65... | collective-permute-start | bytes 393224 | tf_op jit(solution)/shard_map/ppermute | solution.py:34
  3.8 10.7 %collective-permute-start.1 = (bf16[16,4096]{1,0:T(8,128)(2,1)}, bf16[16,4096]{1,0:T(8,128)(2,1)S(1)}, u32[]{:S(2)}, u32[]{:S(2)}) collective-permute-start(bf16[16,4096]{1,0:T(8,128)(2,1)} %cotangent_hbm.1), channel_id=1, source_target_pairs={{0,6},{1,7},{2,0},{3,1},{4,2},{5,3},{6,4},{7,5},{64,70},{65,71},{6... | collective-permute-start | bytes 393224 | tf_op jit(solution)/shard_map/ppermute | solution.py:34
  7.8 8.2 %collective-permute-start.2 = (bf16[16,4096]{1,0:T(8,128)(2,1)}, bf16[16,4096]{1,0:T(8,128)(2,1)S(1)}, u32[]{:S(2)}, u32[]{:S(2)}) collective-permute-start(bf16[16,4096]{1,0:T(8,128)(2,1)} %cotangent_hbm.1), channel_id=1, source_target_pairs={{0,4},{1,5},{2,6},{3,7},{4,0},{5,1},{6,2},{7,3},{64,68},{65,69},{6... | collective-permute-start | bytes 393224 | tf_op jit(solution)/shard_map/ppermute | solution.py:34
  7.8 10.9 %collective-permute-start.3 = (bf16[16,4096]{1,0:T(8,128)(2,1)}, bf16[16,4096]{1,0:T(8,128)(2,1)S(1)}, u32[]{:S(2)}, u32[]{:S(2)}) collective-permute-start(bf16[16,4096]{1,0:T(8,128)(2,1)} %cotangent_hbm.1), channel_id=1, source_target_pairs={{0,2},{1,3},{2,4},{3,5},{4,6},{5,7},{6,0},{7,1},{64,66},{65,67},{6... | collective-permute-start | bytes 393224 | tf_op jit(solution)/shard_map/ppermute | solution.py:34
  10.1 15.7 %collective-permute-start.6 = (bf16[32,4096]{1,0:T(8,128)(2,1)S(1)}, bf16[32,4096]{1,0:T(8,128)(2,1)S(1)}, u32[]{:S(2)}, u32[]{:S(2)}) collective-permute-start(bf16[32,4096]{1,0:T(8,128)(2,1)S(1)} %constant_dynamic-update-slice_fusion.3.refs_1_.refs_0_), channel_id=1, source_target_pairs={{0,6},{1,7},{2,0},{3,1},{4,2},{5,3},{6,4},{7,5},{64,70},{65,71},{6... | collective-permute-start | bytes 786440 | tf_op jit(solution)/shard_map/ppermute | solution.py:34
  12.2 13.6 %collective-permute-start.7 = (bf16[32,4096]{1,0:T(8,128)(2,1)S(1)}, bf16[32,4096]{1,0:T(8,128)(2,1)S(1)}, u32[]{:S(2)}, u32[]{:S(2)}) collective-permute-start(bf16[32,4096]{1,0:T(8,128)(2,1)S(1)} %constant_dynamic-update-slice_fusion.3.refs_1_.refs_0_), channel_id=1, source_target_pairs={{0,4},{1,5},{2,6},{3,7},{4,0},{5,1},{6,2},{7,3},{64,68},{65,69},{6... | collective-permute-start | bytes 786440 | tf_op jit(solution)/shard_map/ppermute | solution.py:34
  14.5 13.5 %collective-permute-start.8 = (bf16[32,4096]{1,0:T(8,128)(2,1)S(1)}, bf16[32,4096]{1,0:T(8,128)(2,1)S(1)}, u32[]{:S(2)}, u32[]{:S(2)}) collective-permute-start(bf16[32,4096]{1,0:T(8,128)(2,1)S(1)} %constant_dynamic-update-slice_fusion.3.refs_1_.refs_0_), channel_id=1, source_target_pairs={{0,2},{1,3},{2,4},{3,5},{4,6},{5,7},{6,0},{7,1},{64,66},{65,67},{6... | collective-permute-start | bytes 786440 | tf_op jit(solution)/shard_map/ppermute | solution.py:34
  18.8 13.7 %collective-permute-start.4 = (bf16[64,4096]{1,0:T(8,128)(2,1)S(1)}, bf16[64,4096]{1,0:T(8,128)(2,1)S(1)}, u32[]{:S(2)}, u32[]{:S(2)}) collective-permute-start(bf16[64,4096]{1,0:T(8,128)(2,1)S(1)} %constant_dynamic-update-slice_fusion.refs_0_), channel_id=1, source_target_pairs={{0,72},{1,73},{2,74},{3,75},{4,76},{5,77},{6,78},{7,79},{64,8},{65... | collective-permute-start | bytes 1572872 | tf_op jit(solution)/shard_map/ppermute | solution.py:34
  18.9 13.7 %slice-start = ((s8[7340032]{0:T(1024)(128)(4,1)}), s8[4194304]{0:T(1024)(128)(4,1)S(1)}, s32[]{:S(2)}) async-start(s8[7340032]{0:T(1024)(128)(4,1)} %bitcast.1), calls=%async_computation | async-start | bytes 8388608
  18.9 9.6 %copy-start.1 = (f32[32,4096]{1,0:T(8,128)S(1)}, f32[32,4096]{1,0:T(8,128)}, u32[]{:S(2)}) copy-start(f32[32,4096]{1,0:T(8,128)} %param.13) | copy-start | bytes 1572868
  18.9 13.6 %slice-start.1 = ((s8[7340032]{0:T(1024)(128)(4,1)}), s8[3145728]{0:T(1024)(128)(4,1)S(1)}, s32[]{:S(2)}) async-start(s8[7340032]{0:T(1024)(128)(4,1)} %bitcast.1), calls=%async_computation.1 | async-start | bytes 6291456
  18.9 6.9 %collective-permute-start.9 = (bf16[32,4096]{1,0:T(8,128)(2,1)S(1)}, bf16[32,4096]{1,0:T(8,128)(2,1)S(1)}, u32[]{:S(2)}, u32[]{:S(2)}) collective-permute-start(bf16[32,4096]{1,0:T(8,128)(2,1)S(1)} %bitcast.5), channel_id=1, source_target_pairs={{0,64},{1,65},{2,66},{3,67},{4,68},{5,69},{6,70},{7,71},{64,0},{65... | collective-permute-start | bytes 786440 | tf_op jit(solution)/shard_map/ppermute | solution.py:34
  25.8 2.8 %collective-permute-start.10 = (bf16[32,4096]{1,0:T(8,128)(2,1)S(1)}, bf16[32,4096]{1,0:T(8,128)(2,1)S(1)}, u32[]{:S(2)}, u32[]{:S(2)}) collective-permute-start(bf16[32,4096]{1,0:T(8,128)(2,1)S(1)} %constant_dynamic-update-slice_fusion.3.refs_1_.refs_0_), channel_id=1, source_target_pairs={{0,1},{1,0},{2,3},{3,2},{4,5},{5,4},{6,7},{7,6},{64,65},{65,64},{6... | collective-permute-start | bytes 786440 | tf_op jit(solution)/shard_map/ppermute | solution.py:34
  28.0 1.5 %collective-permute-start.11 = (bf16[32,4096]{1,0:T(8,128)(2,1)S(1)}, bf16[32,4096]{1,0:T(8,128)(2,1)S(1)}, u32[]{:S(2)}, u32[]{:S(2)}) collective-permute-start(bf16[32,4096]{1,0:T(8,128)(2,1)S(1)} %collective-permute-done.6.refs_1_), channel_id=1, source_target_pairs={{0,1},{1,0},{2,3},{3,2},{4,5},{5,4},{6,7},{7,6},{64,65},{65,64},{6... | collective-permute-start | bytes 786440 | tf_op jit(solution)/shard_map/ppermute | solution.py:34
  28.0 3.0 %collective-permute-start.12 = (bf16[32,4096]{1,0:T(8,128)(2,1)S(1)}, bf16[32,4096]{1,0:T(8,128)(2,1)S(1)}, u32[]{:S(2)}, u32[]{:S(2)}) collective-permute-start(bf16[32,4096]{1,0:T(8,128)(2,1)S(1)} %collective-permute-done.7.refs_2_), channel_id=1, source_target_pairs={{0,1},{1,0},{2,3},{3,2},{4,5},{5,4},{6,7},{7,6},{64,65},{65,64},{6... | collective-permute-start | bytes 786440 | tf_op jit(solution)/shard_map/ppermute | solution.py:34
  28.5 2.5 %collective-permute-start.13 = (bf16[32,4096]{1,0:T(8,128)(2,1)S(1)}, bf16[32,4096]{1,0:T(8,128)(2,1)S(1)}, u32[]{:S(2)}, u32[]{:S(2)}) collective-permute-start(bf16[32,4096]{1,0:T(8,128)(2,1)S(1)} %collective-permute-done.8.refs_3_), channel_id=1, source_target_pairs={{0,1},{1,0},{2,3},{3,2},{4,5},{5,4},{6,7},{7,6},{64,65},{65,64},{6... | collective-permute-start | bytes 786440 | tf_op jit(solution)/shard_map/ppermute | solution.py:34
  28.6 11.1 %collective-permute-start.5 = (bf16[64,4096]{1,0:T(8,128)(2,1)S(1)}, bf16[64,4096]{1,0:T(8,128)(2,1)S(1)}, u32[]{:S(2)}, u32[]{:S(2)}) collective-permute-start(bf16[64,4096]{1,0:T(8,128)(2,1)S(1)} %constant_dynamic-update-slice_fusion.refs_0_), channel_id=1, source_target_pairs={{0,1},{1,0},{2,3},{3,2},{4,5},{5,4},{6,7},{7,6},{64,65},{65,64},{6... | collective-permute-start | bytes 1572872 | tf_op jit(solution)/shard_map/ppermute | solution.py:34
  29.5 10.2 %collective-permute-start.15 = (f32[32,4096]{1,0:T(8,128)S(1)}, f32[32,4096]{1,0:T(8,128)S(1)}, u32[]{:S(2)}, u32[]{:S(2)}) collective-permute-start(f32[32,4096]{1,0:T(8,128)S(1)} %subtract_add_fusion.refs_0_), channel_id=1, source_target_pairs={{0,16},{1,49},{2,18},{3,51},{4,20},{5,53},{6,22},{7,55},{64,80},{6... | collective-permute-start | bytes 1572872 | tf_op jit(solution)/shard_map/ppermute | solution.py:34
  36.5 3.3 %collective-permute-start.14 = (bf16[64,4096]{1,0:T(8,128)(2,1)S(1)}, bf16[64,4096]{1,0:T(8,128)(2,1)S(1)}, u32[]{:S(2)}, u32[]{:S(2)}) collective-permute-start(bf16[64,4096]{1,0:T(8,128)(2,1)S(1)} %collective-permute-done.4.refs_10_.refs_1_), channel_id=1, source_target_pairs={{0,1},{1,0},{2,3},{3,2},{4,5},{5,4},{6,7},{7,6},{64,65},{65,64},{6... | collective-permute-start | bytes 1572872 | tf_op jit(solution)/shard_map/ppermute | solution.py:34
  39.0 3.2 %collective-permute-start.16 = (bf16[128,4096]{1,0:T(8,128)(2,1)S(1)}, bf16[128,4096]{1,0:T(8,128)(2,1)S(1)}, u32[]{:S(2)}, u32[]{:S(2)}) collective-permute-start(bf16[128,4096]{1,0:T(8,128)(2,1)S(1)} %get-tuple-element.51.refs_2_.refs_7_), channel_id=1, source_target_pairs={{0,1},{1,0},{2,3},{3,2},{4,5},{5,4},{6,7},{7,6},{64,65},{65,64},{6... | collective-permute-start | bytes 3145736 | tf_op jit(solution)/shard_map/ppermute | solution.py:34
  42.3 14.7 %copy-start.2 = (f32[32,4096]{1,0:T(8,128)S(1)}, f32[32,4096]{1,0:T(8,128)}, u32[]{:S(2)}) copy-start(f32[32,4096]{1,0:T(8,128)} %param.15) | copy-start | bytes 1572868
  46.3 3.3 %collective-permute-start.17 = (bf16[128,4096]{1,0:T(8,128)(2,1)S(1)}, bf16[128,4096]{1,0:T(8,128)(2,1)S(1)}, u32[]{:S(2)}, u32[]{:S(2)}) collective-permute-start(bf16[128,4096]{1,0:T(8,128)(2,1)S(1)} %get-tuple-element.55), channel_id=1, source_target_pairs={{0,1},{1,0},{2,3},{3,2},{4,5},{5,4},{6,7},{7,6},{64,65},{65,64},{6... | collective-permute-start | bytes 3145736 | tf_op jit(solution)/shard_map/ppermute | solution.py:34
  46.6 10.4 %collective-permute-start.23 = (f32[32,4096]{1,0:T(8,128)S(1)}, f32[32,4096]{1,0:T(8,128)S(1)}, u32[]{:S(2)}, u32[]{:S(2)}) collective-permute-start(f32[32,4096]{1,0:T(8,128)S(1)} %shard_map.116.refs_8_.refs_0_), channel_id=1, source_target_pairs={{0,48},{1,17},{2,50},{3,19},{4,52},{5,21},{6,54},{7,23},{64,112},{... | collective-permute-start | bytes 1572872 | tf_op jit(solution)/shard_map/ppermute | solution.py:34
  49.4 13.8 %collective-permute-start.22 = (bf16[64,4096]{1,0:T(8,128)(2,1)S(1)}, bf16[64,4096]{1,0:T(8,128)(2,1)S(1)}, u32[]{:S(2)}, u32[]{:S(2)}) collective-permute-start(bf16[64,4096]{1,0:T(8,128)(2,1)S(1)} %get-tuple-element.53.refs_3_), channel_id=1, source_target_pairs={{0,72},{1,73},{2,74},{3,75},{4,76},{5,77},{6,78},{7,79},{64,8},{65... | collective-permute-start | bytes 1572872 | tf_op jit(solution)/shard_map/ppermute | solution.py:34
  49.8 14.9 %collective-permute-start.18 = (bf16[32,4096]{1,0:T(8,128)(2,1)S(1)}, bf16[32,4096]{1,0:T(8,128)(2,1)S(1)}, u32[]{:S(2)}, u32[]{:S(2)}) collective-permute-start(bf16[32,4096]{1,0:T(8,128)(2,1)S(1)} %get-tuple-element.57), channel_id=1, source_target_pairs={{0,4},{1,5},{2,6},{3,7},{4,0},{5,1},{6,2},{7,3},{64,68},{65,69},{6... | collective-permute-start | bytes 786440 | tf_op jit(solution)/shard_map/ppermute | solution.py:34
  52.9 13.8 %collective-permute-start.19 = (bf16[32,4096]{1,0:T(8,128)(2,1)S(1)}, bf16[32,4096]{1,0:T(8,128)(2,1)S(1)}, u32[]{:S(2)}, u32[]{:S(2)}) collective-permute-start(bf16[32,4096]{1,0:T(8,128)(2,1)S(1)} %get-tuple-element.58.refs_2_), channel_id=1, source_target_pairs={{0,2},{1,3},{2,4},{3,5},{4,6},{5,7},{6,0},{7,1},{64,66},{65,67},{6... | collective-permute-start | bytes 786440 | tf_op jit(solution)/shard_map/ppermute | solution.py:34
  52.9 13.8 %collective-permute-start.20 = (bf16[32,4096]{1,0:T(8,128)(2,1)S(1)}, bf16[32,4096]{1,0:T(8,128)(2,1)S(1)}, u32[]{:S(2)}, u32[]{:S(2)}) collective-permute-start(bf16[32,4096]{1,0:T(8,128)(2,1)S(1)} %get-tuple-element.59), channel_id=1, source_target_pairs={{0,6},{1,7},{2,0},{3,1},{4,2},{5,3},{6,4},{7,5},{64,70},{65,71},{6... | collective-permute-start | bytes 786440 | tf_op jit(solution)/shard_map/ppermute | solution.py:34
  58.0 8.7 %copy-start = (f32[32,4096]{1,0:T(8,128)}, f32[32,4096]{1,0:T(8,128)S(1)}, u32[]{:S(2)}) copy-start(f32[32,4096]{1,0:T(8,128)S(1)} %get-tuple-element.70.refs_3_) | copy-start | bytes 1572868
  63.3 8.2 %collective-permute-start.24 = (bf16[16,4096]{1,0:T(8,128)(2,1)S(1)}, bf16[16,4096]{1,0:T(8,128)(2,1)S(1)}, u32[]{:S(2)}, u32[]{:S(2)}) collective-permute-start(bf16[16,4096]{1,0:T(8,128)(2,1)S(1)} %get-tuple-element.65), channel_id=1, source_target_pairs={{0,2},{1,3},{2,4},{3,5},{4,6},{5,7},{6,0},{7,1},{64,66},{65,67},{6... | collective-permute-start | bytes 393224 | tf_op jit(solution)/shard_map/ppermute | solution.py:34
  63.4 8.1 %collective-permute-start.25 = (bf16[16,4096]{1,0:T(8,128)(2,1)S(1)}, bf16[16,4096]{1,0:T(8,128)(2,1)S(1)}, u32[]{:S(2)}, u32[]{:S(2)}) collective-permute-start(bf16[16,4096]{1,0:T(8,128)(2,1)S(1)} %get-tuple-element.66), channel_id=1, source_target_pairs={{0,4},{1,5},{2,6},{3,7},{4,0},{5,1},{6,2},{7,3},{64,68},{65,69},{6... | collective-permute-start | bytes 393224 | tf_op jit(solution)/shard_map/ppermute | solution.py:34
  64.7 7.1 %collective-permute-start.26 = (bf16[16,4096]{1,0:T(8,128)(2,1)S(1)}, bf16[16,4096]{1,0:T(8,128)(2,1)S(1)}, u32[]{:S(2)}, u32[]{:S(2)}) collective-permute-start(bf16[16,4096]{1,0:T(8,128)(2,1)S(1)} %get-tuple-element.67), channel_id=1, source_target_pairs={{0,6},{1,7},{2,0},{3,1},{4,2},{5,3},{6,4},{7,5},{64,70},{65,71},{6... | collective-permute-start | bytes 393224 | tf_op jit(solution)/shard_map/ppermute | solution.py:34
  66.7 6.3 %collective-permute-start.21 = (bf16[16,4096]{1,0:T(8,128)(2,1)S(1)}, bf16[16,4096]{1,0:T(8,128)(2,1)S(1)}, u32[]{:S(2)}, u32[]{:S(2)}) collective-permute-start(bf16[16,4096]{1,0:T(8,128)(2,1)S(1)} %get-tuple-element.61), channel_id=1, source_target_pairs={{0,72},{1,73},{2,74},{3,75},{4,76},{5,77},{6,78},{7,79},{64,8},{65... | collective-permute-start | bytes 393224 | tf_op jit(solution)/shard_map/ppermute | solution.py:34
  (3 other events, 20.5 us)
